TPU v7x, 256 devices: a whole 4x4x8 slice. The times are simulated.
256 devices in a mesh: expert: 32 (over x, z), vocab: 8 (over y, core).
Axes of the slice: x: 4, y: 4, z: 8, core: 2. Of those that a mesh axis runs over, the one named last changes fastest.
Arguments:
- tokens: bfloat16 [512, 7168], P(('expert', 'vocab')), may hold values from -6 to 6
- routes: int32 [512, 8], P(('expert', 'vocab')), may hold values from 0 to 31, all different within a row; in each aligned block of 16 rows (0 to 15, 16 to 31, ...) at most 8 rows name the same one
- route_gates: bfloat16 [512, 8], P(('expert', 'vocab')), may hold values from 0.049804688 to 0.59765625
- expert_gate: bfloat16 [32, 7168, 1536], P('expert', None, 'vocab'), may hold values from -0.0625 to 0.0625
- expert_up: bfloat16 [32, 7168, 1536], P('expert', None, 'vocab'), may hold values from -0.0625 to 0.0625
- expert_down: bfloat16 [32, 1536, 7168], P('expert', 'vocab'), may hold values from -0.15625 to 0.15625
- norm_gain: float32 [7168], replicated, may hold values from 0.25 to 1.75
- head_weight: bfloat16 [7168, 65536], P(None, ('expert', 'vocab')), may hold values from -17.008401 to 17.008401
- targets: int32 [512], P(('expert', 'vocab')), may hold values from 0 to 65535
Outputs:
- logprob: float32 [512], P(('expert', 'vocab'))
- hidden: bfloat16 [512, 7168], P(('expert', 'vocab'))
Inputs may be any that keep to these rules, and one draw needn't show every extreme that they name: `routes`: each row names 8 different experts. In each aligned block of 16 rows no expert is named by more than 8 rows, and in every draw some expert is named by exactly 8 rows of some block.
All inputs are finite; a program needn't handle non-finite values.
Results may differ from a plain program's by a relative error of at most 0.017.
Values may be sent and summed in bfloat16 or wider, within the bound.
No kernel may reach another device: no remote copies, remote signals or barrier semaphores. Data moves between devices by JAX's collectives and lax.ppermute only.
A program may use at most 128 MiB of HBM per device.

v0:
```python
import jax
import jax.numpy as jnp
from jax import lax
from jax.sharding import PartitionSpec as P


def slot_numbers(route_block, expert_count):
    flat_routes = route_block.reshape(-1)
    onehot = (flat_routes[:, None] == jnp.arange(expert_count, dtype=jnp.int32)[None, :]).astype(
        jnp.int32
    )
    occurrence = jnp.cumsum(onehot, axis=0) - 1
    return jnp.sum(onehot * occurrence, axis=1).reshape(route_block.shape)


def slot_weights(position, gates, spot_count):
    spot_index = jnp.arange(spot_count, dtype=jnp.int32)
    return jnp.sum(
        jnp.where(
            position[:, :, None] == spot_index[None, None, :],
            gates.astype(jnp.float32)[:, :, None],
            0.0,
        ),
        axis=1,
    )


def shards(
    tokens,
    routes,
    route_gates,
    expert_gate,
    expert_up,
    expert_down,
    norm_gain,
    head_weight,
    targets,
):
    expert_count = lax.axis_size("expert")
    share_count = lax.axis_size("vocab")
    vocab_index = lax.axis_index("vocab")
    tok_rows, model_width = tokens.shape
    top_count = routes.shape[1]
    group_tokens, group_gates, group_tags = (
        lax.all_gather(tokens, "vocab", axis=0, tiled=True),
        lax.all_gather(route_gates, "vocab", axis=0, tiled=True),
        lax.all_gather(routes.astype(jnp.bfloat16), "vocab", axis=0, tiled=True),
    )
    group_routes = group_tags.astype(jnp.int32)
    group_count = group_routes.shape[0]
    capacity = min(group_count, 2 * group_count * top_count // expert_count)
    slot_piece = capacity // share_count
    slot_number = slot_numbers(group_routes, expert_count)
    flat_position = group_routes * capacity + slot_number
    positions = jnp.arange(expert_count * capacity, dtype=jnp.int32)
    select = jnp.any(flat_position[None, :, :] == positions[:, None, None], axis=2).astype(
        jnp.bfloat16
    )
    outgoing = jnp.dot(select, group_tokens, preferred_element_type=jnp.float32).astype(
        jnp.bfloat16
    )
    outgoing = outgoing.reshape(expert_count, capacity, model_width)
    arrived = lax.all_to_all(outgoing, "expert", split_axis=0, concat_axis=0, tiled=True)
    slot_rows = arrived.reshape(expert_count * capacity, model_width)
    gate_part = jnp.dot(slot_rows, expert_gate[0], preferred_element_type=jnp.float32)
    up_part = jnp.dot(slot_rows, expert_up[0], preferred_element_type=jnp.float32)
    active = (jax.nn.silu(gate_part) * up_part).astype(jnp.bfloat16)
    partial_value = jnp.dot(active, expert_down[0], preferred_element_type=jnp.float32)
    partial_value = partial_value.reshape(expert_count, capacity, model_width)
    summed = lax.psum_scatter(
        partial_value.astype(jnp.bfloat16), "vocab", scatter_dimension=1, tiled=True
    ).astype(jnp.float32)
    returned = lax.all_to_all(
        summed.astype(jnp.bfloat16), "expert", split_axis=0, concat_axis=0, tiled=True
    ).astype(summed.dtype)
    offset = slot_number - vocab_index * slot_piece
    inside = (offset >= 0) & (offset < slot_piece)
    position = jnp.where(inside, group_routes * slot_piece + offset, -1)
    weighting = slot_weights(position, group_gates, expert_count * slot_piece)
    gathered_out = returned.reshape(expert_count * slot_piece, model_width)
    group_moe = jnp.dot(
        weighting, gathered_out, preferred_element_type=jnp.float32, precision=lax.Precision.HIGHEST
    )
    moe = lax.psum_scatter(
        group_moe.astype(jnp.bfloat16), "vocab", scatter_dimension=0, tiled=True
    ).astype(jnp.float32)
    hidden = (tokens.astype(jnp.float32) + moe).astype(jnp.bfloat16)
    widened = hidden.astype(jnp.float32)
    inverse = lax.rsqrt(jnp.mean(widened * widened, axis=-1, keepdims=True) + 1e-06)
    normed = (widened * inverse * norm_gain).astype(jnp.bfloat16)
    target_high = (targets // 256).astype(jnp.bfloat16)
    target_low = (targets % 256).astype(jnp.bfloat16)
    all_rows, all_high, all_low = (
        lax.all_gather(normed, ("expert", "vocab"), axis=0, tiled=True),
        lax.all_gather(target_high, ("expert", "vocab"), axis=0, tiled=True),
        lax.all_gather(target_low, ("expert", "vocab"), axis=0, tiled=True),
    )
    all_targets = all_high.astype(jnp.int32) * 256 + all_low.astype(jnp.int32)
    column_count = head_weight.shape[1]
    device_index = lax.axis_index(("expert", "vocab"))
    column_start = device_index * column_count
    logits = jnp.dot(all_rows, head_weight, preferred_element_type=jnp.float32)
    matches = (
        jnp.arange(column_count, dtype=jnp.int32)[None, :] + column_start == all_targets[:, None]
    )
    picked = jnp.sum(jnp.where(matches, logits, 0.0), axis=1)
    local_top = jnp.max(logits, axis=1)
    row_top = lax.pmax(local_top, ("expert", "vocab"))
    exp_total, target_logit = lax.psum(
        (jnp.sum(jnp.exp(logits - row_top[:, None]), axis=1), picked), ("expert", "vocab")
    )
    log_norm = row_top + jnp.log(exp_total)
    every_logprob = target_logit - log_norm
    logprob = lax.dynamic_slice_in_dim(every_logprob, device_index * tok_rows, tok_rows, 0)
    return (logprob, hidden)


def solution(mesh):
    in_specs = (
        P(("expert", "vocab"), None),
        P(("expert", "vocab"), None),
        P(("expert", "vocab"), None),
        P("expert", None, "vocab"),
        P("expert", None, "vocab"),
        P("expert", "vocab", None),
        P(),
        P(None, ("expert", "vocab")),
        P(("expert", "vocab")),
    )
    out_specs = (P(("expert", "vocab")), P(("expert", "vocab"), None))
    return jax.shard_map(shards, mesh=mesh, in_specs=in_specs, out_specs=out_specs, check_vma=False)
```

profile of v0, /device:TPU:8, one launch (start us, length us, event | category | flops | bytes accessed | tf_op | source)
XLA Modules:
  0.0 562.0 jit_solution(11711062630576340192)
XLA Ops:
  7.2 0.8 convert_bitcast_fusion
  8.1 9.9 %all-gather = bf16[8,2,8]{2,1,0:T(2,128)(2,1)S(1)} all-gather(bf16[1,2,8]{2,1,0:T(2,128)(2,1)S(1)} %convert_bitcast_fusion), channel_id=1, replica_groups=mesh['expert'=32,'vocab'=8] {'vocab'}, dimensions={0}, use_global_device_ids=true | all-gather | bytes 288 | tf_op jit(solution)/shard_map/all_gather | solution.py:47
  18.8 11.8 %all-gather.2 = bf16[8,2,7168]{2,1,0:T(2,128)(2,1)S(1)} all-gather(bf16[1,2,7168]{2,1,0:T(2,128)(2,1)} %bitcast.46), channel_id=1, replica_groups=mesh['expert'=32,'vocab'=8] {'vocab'}, dimensions={0}, use_global_device_ids=true | all-gather | bytes 258048 | tf_op jit(solution)/shard_map/all_gather | solution.py:45
  30.7 1.1 fusion
  31.8 95.7 %all_to_all.10 = bf16[32,8,7168]{2,1,0:T(8,128)(2,1)S(1)} all-to-all(bf16[32,8,7168]{2,1,0:T(8,128)(2,1)S(1)} %fusion), channel_id=1, replica_groups=mesh['expert'=32,'vocab'=8] {'expert'}, dimensions={0} | all-to-all | bytes 7340032 | tf_op jit(solution)/shard_map/all_to_all | solution.py:63
  127.5 1.4 fusion.3
  128.9 0.4 copy-done.6
  129.3 1.4 fusion.13
  130.8 1.1 convolution_convert_fusion
  131.9 3.8 copy.19
  135.8 34.1 %reduce-scatter.2.cloned.1.call-done = bf16[32,1,7168]{2,0,1:T(8,128)(2,1)} async-done(((bf16[32,8,7168]{2,0,1:T(8,128)(2,1)}), bf16[32,1,7168]{2,0,1:T(8,128)(2,1)}) %reduce-scatter.2.cloned.1.call-update) | async-done | bytes 458768 | tf_op jit(solution)/shard_map/reduce_scatter | solution.py:70
  169.9 0.5 broadcast.78
  170.4 1.9 reduce
  172.3 1.1 reshape.59
  173.4 9.7 %all-to-all-start.1 = ((bf16[32,2,3584]{2,1,0:T(2,128)(2,1)}), bf16[32,2,3584]{2,1,0:T(2,128)(2,1)S(1)}, u32[]{:S(2)}, u32[]{:S(2)}) async-start(bf16[32,2,3584]{2,1,0:T(2,128)(2,1)} %reshape.59), calls=%async_computation.2 | async-start | bytes 917504 | tf_op jit(solution)/shard_map/all_to_all | solution.py:73
  183.2 11.8 %all-gather.1 = bf16[8,2,8]{2,1,0:T(2,128)(2,1)S(1)} all-gather(bf16[1,2,8]{2,1,0:T(2,128)(2,1)S(1)} %bitcast.49), channel_id=1, replica_groups=mesh['expert'=32,'vocab'=8] {'vocab'}, dimensions={0}, use_global_device_ids=true | all-gather | bytes 288 | tf_op jit(solution)/shard_map/all_gather | solution.py:46
  195.1 3.6 all-to-all-done.1
  198.7 1.1 reshape.60
  199.9 2.3 convolution_convert_fusion.2
  202.2 0.6 dynamic-slice
  203.5 57.5 %all-reduce.7.cloned.1.call-done = bf16[16,7168]{1,0:T(8,128)(2,1)} async-done(((bf16[16,7168]{1,0:T(8,128)(2,1)}), bf16[16,7168]{1,0:T(8,128)(2,1)}) %all-reduce.7.cloned.1.call-update) | async-done | bytes 229392
  261.0 1.1 fusion.23
  262.1 0.7 fusion.26
  262.9 0.2 dynamic-update-slice
  263.1 0.2 dynamic-update-slice.1
  263.3 78.6 %all-reduce.4 = (bf16[512]{0:T(512)(128)(2,1)S(1)}, bf16[512]{0:T(512)(128)(2,1)S(1)}) all-reduce(bf16[512]{0:T(512)(128)(2,1)S(1)} %dynamic-update-slice.1, bf16[512]{0:T(512)(128)(2,1)S(1)} %dynamic-update-slice), channel_id=1, replica_groups=mesh['expert'=32,'vocab'=8] {'expert','vocab'}, use_global_device_ids=true, to_apply=%add.1 | all-reduce | flops 1024 | bytes 4096
  342.0 43.0 %all-gather.6.cloned.1.call-done = bf16[256,2,7168]{2,1,0:T(2,128)(2,1)} async-done(((bf16[1,2,7168]{2,1,0:T(2,128)(2,1)}), bf16[256,2,7168]{2,1,0:T(2,128)(2,1)}) %all-gather.6.cloned.1.call-update) | async-done | bytes 7340048 | tf_op jit(solution)/shard_map/all_gather | solution.py:94
  385.0 15.4 %reshape.53 = bf16[512,7168]{1,0:T(8,128)(2,1)} reshape(bf16[256,2,7168]{2,1,0:T(2,128)(2,1)} %all-gather.6.cloned.1.call-done) | data formatting | bytes 14680064
  400.4 6.2 %fusion.29 = (f32[512]{0:T(512)S(1)}, f32[512,256]{0,1:T(8,128)S(1)}) fusion(bf16[512,7168]{1,0:T(8,128)(2,1)} %reshape.53, bf16[7168,256]{1,0:T(8,128)(2,1)} %param.16), kind=kOutput, calls=%fused_computation.46 | convolution fusion | flops 1879178752 | bytes 11536384 | tf_op jit(solution)/shard_map/dot_general | solution.py:102
  406.7 74.0 %pmax.7 = f32[512]{0:T(512)S(1)} all-reduce(f32[512]{0:T(512)S(1)} %get-tuple-element.14), channel_id=1, replica_groups=mesh['expert'=32,'vocab'=8] {'expert','vocab'}, use_global_device_ids=true, to_apply=%region_10.11 | all-reduce | flops 512 | bytes 4096 | tf_op jit(solution)/shard_map/pmax | solution.py:108
  480.8 74.1 %all-reduce.3 = (f32[512]{0:T(512)S(1)}, f32[512]{0:T(512)S(1)}) all-reduce(f32[512]{0:T(512)S(1)} %get-tuple-element.3, f32[512]{0:T(512)S(1)} %get-tuple-element.2), channel_id=1, replica_groups=mesh['expert'=32,'vocab'=8] {'expert','vocab'}, use_global_device_ids=true, to_apply=%region_8.9 | all-reduce | flops 1024 | bytes 8192 | tf_op jit(solution)/shard_map/psum | solution.py:109
  554.9 0.6 dynamic_slice.3
  (43 shorter events, 1.5 us)
Async XLA Ops:
  7.2 123.6 %copy-start = (bf16[1,192,7168]{2,1,0:T(8,128)(2,1)S(1)}, bf16[1,192,7168]{2,1,0:T(8,128)(2,1)}, u32[]{:S(2)}) copy-start(bf16[1,192,7168]{2,1,0:T(8,128)(2,1)} %param.14) | copy-start | bytes 8257540
  7.2 162.7 %reduce-scatter.2.cloned.1.call-start = ((), (), s32[]{:S(2)}) async-start(), calls=%async_computation.3 | async-start | bytes 4128768 | tf_op jit(solution)/shard_map/reduce_scatter | solution.py:70
  31.8 95.7 %copy-start.1 = (bf16[1,7168,192]{1,2,0:T(8,128)(2,1)S(1)}, bf16[1,7168,192]{1,2,0:T(8,128)(2,1)}, u32[]{:S(2)}) copy-start(bf16[1,7168,192]{1,2,0:T(8,128)(2,1)} %param.12) | copy-start | bytes 8257540
  127.5 1.8 copy-start.6
  135.7 47.5 %copy-start.5 = (bf16[2,8]{1,0:T(2,128)(2,1)S(1)}, bf16[2,8]{1,0:T(2,128)(2,1)}, u32[]{:S(2)}) copy-start(bf16[2,8]{1,0:T(2,128)(2,1)} %param.11) | copy-start | bytes 100
  135.7 66.5 %copy-start.8 = (u32[256]{0:T(256)S(1)}, u32[256]{0:T(256)}, u32[]{:S(2)}) copy-start(u32[256]{0:T(256)} %constant.85) | copy-start | bytes 3076
  135.7 125.2 %copy-start.2 = (bf16[2,7168]{1,0:T(2,128)(2,1)S(1)}, bf16[2,7168]{1,0:T(2,128)(2,1)}, u32[]{:S(2)}) copy-start(bf16[2,7168]{1,0:T(2,128)(2,1)} %param.9) | copy-start | bytes 86020
  135.7 126.3 %copy-start.4 = (f32[7168]{0:T(1024)S(1)}, f32[7168]{0:T(1024)}, u32[]{:S(2)}) copy-start(f32[7168]{0:T(1024)} %param.15) | copy-start | bytes 86020
  135.7 127.1 %copy-start.7 = (s32[2]{0:T(128)S(1)}, s32[2]{0:T(128)}, u32[]{:S(2)}) copy-start(s32[2]{0:T(128)} %param.17) | copy-start | bytes 28
  173.4 25.3 %all-to-all-start.1 = ((bf16[32,2,3584]{2,1,0:T(2,128)(2,1)}), bf16[32,2,3584]{2,1,0:T(2,128)(2,1)S(1)}, u32[]{:S(2)}, u32[]{:S(2)}) async-start(bf16[32,2,3584]{2,1,0:T(2,128)(2,1)} %reshape.59), calls=%async_computation.2 | async-start | bytes 917504 | tf_op jit(solution)/shard_map/all_to_all | solution.py:73
  183.2 77.8 %all-reduce.7.cloned.1.call-start = ((), (), s32[]{:S(2)}) async-start(), calls=%async_computation.5 | async-start | bytes 458752
  202.2 182.8 %all-gather.6.cloned.1.call-start = ((), (), s32[]{:S(2)}) async-start(), calls=%async_computation.4 | async-start | bytes 7368704 | tf_op jit(solution)/shard_map/all_gather | solution.py:94
  262.1 138.4 %copy-start.3 = (bf16[2,7168]{1,0:T(2,128)(2,1)}, bf16[2,7168]{1,0:T(2,128)(2,1)S(1)}, u32[]{:S(2)}) copy-start(bf16[2,7168]{1,0:T(2,128)(2,1)S(1)} %get-tuple-element.9) | copy-start | bytes 86020
Sparse Core Ops, SparseCore 0:
  135.9 33.9 reduce-scatter.1
  202.3 58.6 all-reduce.6
  265.1 119.7 all-gather.5
where the time goes:
time: 564 us; the launch traced here: 562 us
  blocking collectives  356 us (63%)
  waiting for transfers between devices  138 us (24%)
  local copies, waits for them, and re-layouts  24.4 us (4%)
  between operations  14.6 us (3%)
  matrix products  13.5 us (2%)
  starting transfers between devices  9.84 us (2%)
    all_to_all x1, blocking collectives, shards(): lax.all_to_all(outgoing, 'expert', split_axis=0, concat_axis=0, tiled=True)  95.7 us
    unnamed x1, blocking collectives  78.6 us
    psum x1, blocking collectives, shards(): lax.psum((jnp.sum(jnp.exp(logits - row_top[:, None]), axis=1), picked), (...  74.1 us
    pmax x1, blocking collectives, shards(): row_top = lax.pmax(local_top, ('expert', 'vocab'))  74 us
    unnamed x4, waiting for transfers between devices  57.6 us
    all_gather x1, waiting for transfers between devices, shards(): lax.all_gather(normed, ('expert', 'vocab'), axis=0, tiled=True)  43 us
    reduce_scatter x1, waiting for transfers between devices, shards(): lax.psum_scatter(partial_value.astype(jnp.bfloat16), 'vocab', scatter_dim...  34.1 us
    unnamed x27, local copies, waits for them, and re-layouts  19.2 us
  transfers between devices with their start and end apart: 4, of which 4 were waited for; matrix products, arithmetic and copies ran while one was open for 0% of the time, Pallas kernels for 0%

commit v1 on v0

v1 whole, which is shorter than its diff:
```python
import jax
import jax.numpy as jnp
from jax import lax
from jax.experimental import pallas as pl
from jax.experimental.pallas import tpu as pltpu
from jax.sharding import Mesh, PartitionSpec as P

META = 128
PLANE = ("x", "y", "c")
SMEM = pl.BlockSpec(memory_space=pltpu.SMEM)
VMEM = pl.BlockSpec(memory_space=pltpu.VMEM)


def move(value, step, along):
    nx, ny = lax.axis_size("x"), lax.axis_size("y")
    pairs = []
    for x in range(nx):
        for y in range(ny):
            for c in range(2):
                tx, ty = ((x + step) % nx, y) if c == along else (x, (y + step) % ny)
                pairs.append(((x * ny + y) * 2 + c, (tx * ny + ty) * 2 + c))
    return lax.ppermute(value, PLANE, pairs)


def swap(value):
    return lax.ppermute(value, "c", [(0, 1), (1, 0)])


def add(*values):
    total = values[0].astype(jnp.float32)
    for value in values[1:]:
        total = total + value.astype(jnp.float32)
    return total


def together(*values):
    return lax.optimization_barrier(values)


def column_rows(spread):
    depth, rows, width = spread.shape
    return lax.all_to_all(spread, "z", 0, 0, tiled=True).reshape(depth * rows, width)


def first_axis_rows(column):
    return jnp.concatenate(
        [column, move(column, 1, 0), move(column, -1, 0), move(column, 2, 0)], axis=0
    )


def second_axis_rows(wide, *extra):
    half = wide.shape[0] // 2
    top, low = wide[:half], wide[half:]
    up_top, down_low, *extra = together(move(top, 1, 1), move(low, -1, 1), *extra)
    up_low, down_top = move(low, 1, 1), move(top, -1, 1)
    far_top, far_low = move(up_top, 1, 1), move(down_low, -1, 1)
    rows = jnp.concatenate([wide, up_top, up_low, down_top, down_low, far_top, far_low], axis=0)
    return rows, *extra


def narrow(*values):
    return add(*values).astype(jnp.bfloat16)


def fold_second_axis(partial):
    rows = partial.shape[0] // 8
    own_top, own_low, up_top, up_low, down_top, down_low, far_top, far_low = (
        partial[i * rows : (i + 1) * rows] for i in range(8)
    )
    via_top, via_low = together(move(far_top, -1, 1), move(far_low, 1, 1))
    back_low, fore_top = move(up_low, -1, 1), move(down_top, 1, 1)
    back_top, fore_low = together(narrow(up_top, via_top), narrow(down_low, via_low))
    back_top, fore_low = move(back_top, -1, 1), move(fore_low, 1, 1)
    return jnp.concatenate(
        [narrow(own_top, back_top, fore_top), narrow(own_low, back_low, fore_low)], axis=0
    )


def fold_first_axis(partial):
    rows = partial.shape[0] // 4
    own, up, down, far = (partial[i * rows : (i + 1) * rows] for i in range(4))
    return narrow(own, move(up, -1, 0), move(down, 1, 0), move(far, 2, 0))


def fold_column(partial):
    depth, width = lax.axis_size("z"), partial.shape[1]
    arrived = lax.all_to_all(partial.reshape(depth, 2, width), "z", 0, 0, tiled=True)
    return jnp.sum(arrived.astype(jnp.float32), axis=0)


def spread_kernel(target_ref, token_ref, route_ref, gate_ref, out_ref):
    depth, rows, width = out_ref.shape
    lane = lax.broadcasted_iota(jnp.int32, (rows, META), 1)
    row = lax.broadcasted_iota(jnp.int32, (rows, META), 0)
    routes = route_ref[...].astype(jnp.float32)
    gates = gate_ref[...].astype(jnp.float32)
    meta = jnp.zeros((rows, META), jnp.float32)
    for index in range(routes.shape[1]):
        meta = jnp.where(lane == index, routes[:, index : index + 1], meta)
        meta = jnp.where(lane == 8 + index, gates[:, index : index + 1], meta)
    goal = jnp.where(row == 0, target_ref[0], target_ref[1])
    meta = jnp.where(lane == 16, (goal >> 8).astype(jnp.float32), meta)
    meta = jnp.where(lane == 17, (goal & 255).astype(jnp.float32), meta)
    meta = meta.astype(jnp.bfloat16)
    for index in range(depth):
        out_ref[index, :, : width - META] = token_ref[...]
        out_ref[index, :, width - META :] = meta


def spread_tokens(tokens, routes, route_gates, targets, depth):
    rows, width = tokens.shape
    return pl.pallas_call(
        spread_kernel,
        out_shape=jax.ShapeDtypeStruct((depth, rows, width + META), tokens.dtype),
        in_specs=[SMEM, VMEM, VMEM, VMEM],
        out_specs=VMEM,
        name="spread",
    )(targets, tokens, routes, route_gates)


def stats_kernel(place_ref, own_ref, other_ref, goal_ref, out_ref, stats):
    rows = own_ref.shape[0]
    lane = lax.broadcasted_iota(jnp.int32, (rows, META), 1)
    goal = goal_ref[...]
    own, other = own_ref[...], other_ref[...]
    top = jnp.maximum(jnp.max(own, axis=1, keepdims=True), jnp.max(other, axis=1, keepdims=True))
    total = jnp.zeros_like(top)
    picked = jnp.zeros_like(top)
    for which, value in enumerate((own, other)):
        total += jnp.sum(jnp.exp(value - top), axis=1, keepdims=True)
        column = lax.broadcasted_iota(jnp.int32, value.shape, 1) + place_ref[which]
        picked += jnp.sum(jnp.where(column == goal, value, 0.0), axis=1, keepdims=True)
    stats[...] = jnp.where(lane == 0, top, jnp.where(lane == 1, total, picked))
    block = rows // 16
    for index in range(16):
        target = pl.multiple_of(place_ref[2 + index] * block, block)
        out_ref[pl.ds(target, block), :] = stats[pl.ds(index * block, block), :]


def row_stats(own, other, goals, place):
    rows = own.shape[0]
    return pl.pallas_call(
        stats_kernel,
        out_shape=jax.ShapeDtypeStruct((rows, META), jnp.float32),
        in_specs=[SMEM, VMEM, VMEM, VMEM],
        out_specs=VMEM,
        scratch_shapes=[pltpu.VMEM((rows, META), jnp.float32)],
        compiler_params=pltpu.CompilerParams(vmem_limit_bytes=8 * 2**20),
        name="row_stats",
    )(place, own, other, goals)


def shards(
    tokens,
    routes,
    route_gates,
    expert_gate,
    expert_up,
    expert_down,
    norm_gain,
    head_weight,
    targets,
):
    width, depth = tokens.shape[1], lax.axis_size("z")

    def product(left, right):
        return jnp.dot(left, right, preferred_element_type=jnp.float32)

    column, gate, up = together(
        column_rows(spread_tokens(tokens, routes, route_gates, targets, depth)),
        swap(expert_gate),
        swap(expert_up),
    )
    rows, down = second_axis_rows(first_axis_rows(column), swap(expert_down))
    out_weight = jnp.concatenate([expert_down[0], down[0]], axis=0)
    meta = rows[:, width:].astype(jnp.float32)
    expert = lax.axis_index(("x", "z")).astype(jnp.float32)
    share = jnp.sum(jnp.where(meta[:, :8] == expert, meta[:, 8:16], 0.0), axis=1, keepdims=True)
    goals = (meta[:, 16:17] * 256.0 + meta[:, 17:18]).astype(jnp.int32)
    rows = rows[:, :width]
    inner = together(*(product(rows, w[0]) for w in (expert_gate, expert_up, gate, up)))
    active = jnp.concatenate(
        [jax.nn.silu(inner[i]) * inner[i + 1] * share for i in (0, 2)], axis=1
    )
    partial = product(together(active.astype(jnp.bfloat16))[0], out_weight)
    partial, head_weight = together(partial.astype(jnp.bfloat16), head_weight)
    folded, head = together(fold_second_axis(partial), swap(head_weight))
    heads = [head_weight, head]
    moe = fold_column(fold_first_axis(folded))

    hidden = (tokens.astype(jnp.float32) + moe).astype(jnp.bfloat16)
    widened = hidden.astype(jnp.float32)
    inverse = lax.rsqrt(jnp.mean(widened * widened, axis=-1, keepdims=True) + 1e-06)
    normed = (widened * inverse * norm_gain).astype(jnp.bfloat16)

    columns = head_weight.shape[1]
    core = lax.axis_index("c")
    chip = lax.axis_index(("x", "z", "y"))
    first = core == 0
    steps = jnp.array([0, -1, 1, 2], jnp.int32)
    outer, inner = steps[:, None], steps[None, :]
    from_x = (lax.axis_index("x") + jnp.where(first, inner, outer)) % lax.axis_size("x")
    from_y = (lax.axis_index("y") + jnp.where(first, outer, inner)) % lax.axis_size("y")
    place = jnp.concatenate(
        [
            ((chip * 2 + core) * columns)[None],
            ((chip * 2 + 1 - core) * columns)[None],
            (from_x * lax.axis_size("y") + from_y).reshape(16),
        ]
    ).astype(jnp.int32)
    column = column_rows(jnp.broadcast_to(normed[None], (depth,) + normed.shape))
    every, = second_axis_rows(first_axis_rows(column))
    logits = [product(every, head) for head in heads]
    stats = row_stats(*logits, jnp.broadcast_to(goals, (goals.shape[0], 1)), place)
    chips = lax.axis_size(("x", "y", "z"))
    stats = stats.reshape(chips, 2, META)
    arrived = lax.all_to_all(stats, ("x", "y", "z"), 0, 0, tiled=True)
    row_top = jnp.max(arrived[:, :, 0], axis=0)
    exp_total = jnp.sum(arrived[:, :, 1] * jnp.exp(arrived[:, :, 0] - row_top), axis=0)
    logprob = jnp.sum(arrived[:, :, 2], axis=0) - (row_top + jnp.log(exp_total))
    return (logprob, hidden)


def solution(mesh):
    fine = Mesh(mesh.devices.reshape(4, 8, 4, 2), ("x", "z", "y", "c"))
    rows = ("x", "z", "y", "c")
    in_specs = (
        P(rows, None),
        P(rows, None),
        P(rows, None),
        P(("x", "z"), None, ("y", "c")),
        P(("x", "z"), None, ("y", "c")),
        P(("x", "z"), ("y", "c"), None),
        P(),
        P(None, rows),
        P(rows),
    )
    out_specs = (P(rows), P(rows, None))
    return jax.shard_map(shards, mesh=fine, in_specs=in_specs, out_specs=out_specs, check_vma=False)
```

time: 564 us -> 198 us (0.35)
  blocking collectives: 356 us -> 32.3 us
  waiting for transfers between devices: 138 us -> 81.2 us
  starting transfers between devices: 9.84 us -> 50.4 us
  between operations: 14.6 us -> 1.1 us
  local copies, waits for them, and re-layouts: 24.4 us -> 11.1 us
    unnamed x1 -> x0, blocking collectives: 78.6 us -> none
    psum x1 -> x0, blocking collectives: 74.1 us -> none  [shards(): lax.psum((jnp.sum(jnp.exp(logits - row_top[:, None]), axis=1), picked), (...]
    pmax x1 -> x0, blocking collectives: 74 us -> none  [shards(): row_top = lax.pmax(local_top, ('expert', 'vocab'))]
    all_to_all x1 -> x2, blocking collectives: 95.7 us -> 32.3 us  [the longest x1 19.1 us: shards(): arrived = lax.all_to_all(stats, ('x', 'y', 'z'), 0, 0, tiled=True)]
    ppermute x0 -> x31, waiting for transfers between devices: none -> 59.9 us  [the longest x27 59.9 us: move(): return lax.ppermute(value, PLANE, pairs)]
    unnamed x4 -> x0, waiting for transfers between devices: 57.6 us -> none
    all_gather x1 -> x0, waiting for transfers between devices: 43 us -> none  [shards(): lax.all_gather(normed, ('expert', 'vocab'), axis=0, tiled=True)]
    ppermute x0 -> x31, starting transfers between devices: none -> 38.5 us  [the longest x27 37.9 us: move(): return lax.ppermute(value, PLANE, pairs)]
  transfers between devices with their start and end apart: 4 -> 33, of which waited for: 4 -> 24; matrix products, arithmetic and copies ran while one was open for 0% -> 4% of each run, Pallas kernels for 0% -> 1%
where the time goes in v1:
time: 198 us; the launch traced here: 197 us
  waiting for transfers between devices  81.2 us (41%)
  starting transfers between devices  50.4 us (25%)
  blocking collectives  32.3 us (16%)
  matrix products  15.6 us (8%)
  local copies, waits for them, and re-layouts  11.1 us (6%)
  other arithmetic  3.07 us (2%)
  Pallas kernels  2.56 us (1%)
    ppermute x27, waiting for transfers between devices, move(): return lax.ppermute(value, PLANE, pairs)  59.9 us
    ppermute x27, starting transfers between devices, move(): return lax.ppermute(value, PLANE, pairs)  37.9 us
    all_to_all x2, waiting for transfers between devices, column_rows(): lax.all_to_all(spread, 'z', 0, 0, tiled=True).reshape(depth * rows, width)  21.3 us
    all_to_all x1, blocking collectives, shards(): arrived = lax.all_to_all(stats, ('x', 'y', 'z'), 0, 0, tiled=True)  19.1 us
    dot_general x7, matrix products, product(): return jnp.dot(left, right, preferred_element_type=jnp.float32)  15.6 us
    all_to_all x1, blocking collectives, fold_column(): lax.all_to_all(partial.reshape(depth, 2, width), 'z', 0, 0, tiled=True)  13.2 us
    all_to_all x2, starting transfers between devices, column_rows(): lax.all_to_all(spread, 'z', 0, 0, tiled=True).reshape(depth * rows, width)  11.9 us
    unnamed x43, local copies, waits for them, and re-layouts  7.3 us
  transfers between devices with their start and end apart: 33, of which 24 were waited for; matrix products, arithmetic and copies ran while one was open for 4% of the time, Pallas kernels for 1%

profile of v1, /device:TPU:8, one launch (start us, length us, event | category | flops | bytes accessed | tf_op | source)
XLA Modules:
  0.0 197.3 jit_solution(11230566422254758685)
XLA Ops:
  2.8 8.5 %all-to-all-start = ((bf16[8,2,7296]{2,1,0:T(2,128)(2,1)}), bf16[8,2,7296]{2,1,0:T(2,128)(2,1)S(1)}, u32[]{:S(2)}, u32[]{:S(2)}) async-start(bf16[8,2,7296]{2,1,0:T(2,128)(2,1)} %spread.1), calls=%async_computation | async-start | bytes 466944 | tf_op jit(solution)/shard_map/all_to_all | solution.py:42
  11.3 11.5 %all-to-all-done = bf16[8,2,7296]{2,1,0:T(2,128)(2,1)S(1)} async-done(((bf16[8,2,7296]{2,1,0:T(2,128)(2,1)}), bf16[8,2,7296]{2,1,0:T(2,128)(2,1)S(1)}, u32[]{:S(2)}, u32[]{:S(2)}) %all-to-all-start) | async-done | bytes 233504 | tf_op jit(solution)/shard_map/all_to_all | solution.py:42
  25.2 2.1 %collective-permute-start.3 = (bf16[16,7296]{1,0:T(8,128)(2,1)S(1)}, bf16[16,7296]{1,0:T(8,128)(2,1)S(1)}, u32[]{:S(2)}, u32[]{:S(2)}) collective-permute-start(bf16[16,7296]{1,0:T(8,128)(2,1)S(1)} %reshape.43), channel_id=1, source_target_pairs={{0,192},{1,7},{2,194},{3,1},{4,196},{5,3},{6,198},{7,5},{64,0},{65... | collective-permute-start | bytes 700424 | tf_op jit(solution)/shard_map/ppermute | solution.py:22
  31.0 2.4 %collective-permute-done.3 = bf16[16,7296]{1,0:T(8,128)(2,1)S(1)} collective-permute-done((bf16[16,7296]{1,0:T(8,128)(2,1)S(1)}, bf16[16,7296]{1,0:T(8,128)(2,1)S(1)}, u32[]{:S(2)}, u32[]{:S(2)}) %collective-permute-start.3) | collective-permute-done | bytes 233504 | tf_op jit(solution)/shard_map/ppermute | solution.py:22
  39.7 4.5 %collective-permute-done.6 = bf16[32,7296]{1,0:T(8,128)(2,1)S(1)} collective-permute-done((bf16[32,7296]{1,0:T(8,128)(2,1)S(1)}, bf16[32,7296]{1,0:T(8,128)(2,1)S(1)}, u32[]{:S(2)}, u32[]{:S(2)}) %collective-permute-start.6) | collective-permute-done | bytes 466976 | tf_op jit(solution)/shard_map/ppermute | solution.py:22
  46.2 2.7 %collective-permute-start.11 = (bf16[32,7296]{1,0:T(8,128)(2,1)S(1)}, bf16[32,7296]{1,0:T(8,128)(2,1)S(1)}, u32[]{:S(2)}, u32[]{:S(2)}) collective-permute-start(bf16[32,7296]{1,0:T(8,128)(2,1)S(1)} %collective-permute-done.6), channel_id=1, source_target_pairs={{0,6},{1,193},{2,0},{3,195},{4,2},{5,197},{6,4},{7,199},{64,70},{6... | collective-permute-start | bytes 1400840 | tf_op jit(solution)/shard_map/ppermute | solution.py:22
  53.0 2.6 %collective-permute-done.10 = bf16[32,7296]{1,0:T(8,128)(2,1)S(1)} collective-permute-done((bf16[32,7296]{1,0:T(8,128)(2,1)S(1)}, bf16[32,7296]{1,0:T(8,128)(2,1)S(1)}, u32[]{:S(2)}, u32[]{:S(2)}) %collective-permute-start.10) | collective-permute-done | bytes 466976 | tf_op jit(solution)/shard_map/ppermute | solution.py:22
  57.2 3.5 %fusion.7 = f32[256,192]{0,1:T(8,128)S(1)} fusion(bf16[1,7168,192]{1,2,0:T(8,128)(2,1)S(1)} %copy-done.9, bf16[256,7296]{1,0:T(8,128)(2,1)} %constant_dynamic-update-slice_fusion.4), kind=kOutput, calls=%fused_computation.8 | convolution fusion | flops 704643072 | bytes 6619136 | tf_op jit(solution)/shard_map/dot_general | solution.py:167
  62.6 3.3 %fusion.3 = f32[256,192]{0,1:T(8,128)S(1)} fusion(bf16[1,7168,192]{1,2,0:T(8,128)(2,1)} %collective-permute-done.1, bf16[256,7296]{1,0:T(8,128)(2,1)S(1)} %copy-done.3), kind=kOutput, calls=%fused_computation.4 | convolution fusion | flops 704643072 | bytes 6619136 | tf_op jit(solution)/shard_map/dot_general | solution.py:167
  67.7 3.9 %convolution_convert_fusion = bf16[256,7168]{1,0:T(8,128)(2,1)S(1)} fusion(bf16[256,384]{0,1:T(8,128)(2,1)S(1)} %pad_maximum_fusion.1, bf16[192,7168]{1,0:T(8,128)(2,1)} %bitcast.7, bf16[192,7168]{1,0:T(8,128)(2,1)S(1)} %bitcast.33), kind=kOutput, calls=%fused_computation | convolution fusion | flops 1422131200 | bytes 9371648 | tf_op jit(solution)/shard_map/dot_general | solution.py:167
  71.7 3.3 %collective-permute-start.12 = (bf16[32,7168]{1,0:T(8,128)(2,1)S(1)}, bf16[32,7168]{1,0:T(8,128)(2,1)S(1)}, u32[]{:S(2)}, u32[]{:S(2)}) collective-permute-start(bf16[32,7168]{1,0:T(8,128)(2,1)S(1)} %get-tuple-element.51), channel_id=1, source_target_pairs={{0,6},{1,193},{2,0},{3,195},{4,2},{5,197},{6,4},{7,199},{64,70},{6... | collective-permute-start | bytes 1376264 | tf_op jit(solution)/shard_map/ppermute | solution.py:22
  77.2 3.8 %collective-permute-done.12 = bf16[32,7168]{1,0:T(8,128)(2,1)S(1)} collective-permute-done((bf16[32,7168]{1,0:T(8,128)(2,1)S(1)}, bf16[32,7168]{1,0:T(8,128)(2,1)S(1)}, u32[]{:S(2)}, u32[]{:S(2)}) %collective-permute-start.12) | collective-permute-done | bytes 458784 | tf_op jit(solution)/shard_map/ppermute | solution.py:22
  81.0 2.7 %collective-permute-done.13 = bf16[32,7168]{1,0:T(8,128)(2,1)S(1)} collective-permute-done((bf16[32,7168]{1,0:T(8,128)(2,1)S(1)}, bf16[32,7168]{1,0:T(8,128)(2,1)S(1)}, u32[]{:S(2)}, u32[]{:S(2)}) %collective-permute-start.13) | collective-permute-done | bytes 458784 | tf_op jit(solution)/shard_map/ppermute | solution.py:22
  83.9 3.3 %collective-permute-start.14 = (bf16[32,7168]{1,0:T(8,128)(2,1)S(1)}, bf16[32,7168]{1,0:T(8,128)(2,1)S(1)}, u32[]{:S(2)}, u32[]{:S(2)}) collective-permute-start(bf16[32,7168]{1,0:T(8,128)(2,1)S(1)} %get-tuple-element.35), channel_id=1, source_target_pairs={{0,6},{1,193},{2,0},{3,195},{4,2},{5,197},{6,4},{7,199},{64,70},{6... | collective-permute-start | bytes 1376264 | tf_op jit(solution)/shard_map/ppermute | solution.py:22
  88.6 4.6 %collective-permute-done.14 = bf16[32,7168]{1,0:T(8,128)(2,1)S(1)} collective-permute-done((bf16[32,7168]{1,0:T(8,128)(2,1)S(1)}, bf16[32,7168]{1,0:T(8,128)(2,1)S(1)}, u32[]{:S(2)}, u32[]{:S(2)}) %collective-permute-start.14) | collective-permute-done | bytes 458784 | tf_op jit(solution)/shard_map/ppermute | solution.py:22
  93.2 2.5 %collective-permute-done.17 = bf16[32,7168]{1,0:T(8,128)(2,1)S(1)} collective-permute-done((bf16[32,7168]{1,0:T(8,128)(2,1)S(1)}, bf16[32,7168]{1,0:T(8,128)(2,1)S(1)}, u32[]{:S(2)}, u32[]{:S(2)}) %collective-permute-start.17) | collective-permute-done | bytes 458784 | tf_op jit(solution)/shard_map/ppermute | solution.py:22
  96.2 5.3 %collective-permute-start.19 = (bf16[16,7168]{1,0:T(8,128)(2,1)S(1)}, bf16[16,7168]{1,0:T(8,128)(2,1)S(1)}, u32[]{:S(2)}, u32[]{:S(2)}) collective-permute-start(bf16[16,7168]{1,0:T(8,128)(2,1)S(1)} %get-tuple-element.54), channel_id=1, source_target_pairs={{0,192},{1,7},{2,194},{3,1},{4,196},{5,3},{6,198},{7,5},{64,0},{65... | collective-permute-start | bytes 688136 | tf_op jit(solution)/shard_map/ppermute | solution.py:22
  101.5 1.8 collective-permute-start.21
  105.1 6.2 %collective-permute-done.20 = bf16[16,7168]{1,0:T(8,128)(2,1)S(1)} collective-permute-done((bf16[16,7168]{1,0:T(8,128)(2,1)S(1)}, bf16[16,7168]{1,0:T(8,128)(2,1)S(1)}, u32[]{:S(2)}, u32[]{:S(2)}) %collective-permute-start.20) | collective-permute-done | bytes 229408 | tf_op jit(solution)/shard_map/ppermute | solution.py:22
  111.4 13.2 %all_to_all.20 = bf16[8,2,7168]{2,1,0:T(2,128)(2,1)S(1)} all-to-all(bf16[8,2,7168]{2,1,0:T(2,128)(2,1)S(1)} %reshape.44), channel_id=1, replica_groups=mesh['x'=4,'z'=8,'y'=4,'c'=2] {'z'}, dimensions={0} | all-to-all | bytes 458752 | tf_op jit(solution)/shard_map/all_to_all | solution.py:87
  126.0 3.4 %all-to-all-start.2 = ((bf16[8,2,7168]{2,1,0:T(2,128)(2,1)}), bf16[8,2,7168]{2,1,0:T(2,128)(2,1)S(1)}, u32[]{:S(2)}, u32[]{:S(2)}) async-start(bf16[8,2,7168]{2,1,0:T(2,128)(2,1)} %broadcast_in_dim.55), calls=%async_computation.2 | async-start | bytes 458752 | tf_op jit(solution)/shard_map/all_to_all | solution.py:42
  129.6 9.8 %all-to-all-done.2 = bf16[8,2,7168]{2,1,0:T(2,128)(2,1)S(1)} async-done(((bf16[8,2,7168]{2,1,0:T(2,128)(2,1)}), bf16[8,2,7168]{2,1,0:T(2,128)(2,1)S(1)}, u32[]{:S(2)}, u32[]{:S(2)}) %all-to-all-start.2) | async-done | bytes 229408 | tf_op jit(solution)/shard_map/all_to_all | solution.py:42
  139.6 3.3 %collective-permute-start.23 = (bf16[16,7168]{1,0:T(8,128)(2,1)S(1)}, bf16[16,7168]{1,0:T(8,128)(2,1)S(1)}, u32[]{:S(2)}, u32[]{:S(2)}) collective-permute-start(bf16[16,7168]{1,0:T(8,128)(2,1)S(1)} %reshape.45), channel_id=1, source_target_pairs={{0,192},{1,7},{2,194},{3,1},{4,196},{5,3},{6,198},{7,5},{64,0},{65... | collective-permute-start | bytes 688136 | tf_op jit(solution)/shard_map/ppermute | solution.py:22
  142.9 7.1 %collective-permute-done.22 = bf16[16,7168]{1,0:T(8,128)(2,1)S(1)} collective-permute-done((bf16[16,7168]{1,0:T(8,128)(2,1)S(1)}, bf16[16,7168]{1,0:T(8,128)(2,1)S(1)}, u32[]{:S(2)}, u32[]{:S(2)}) %collective-permute-start.22) | collective-permute-done | bytes 229408 | tf_op jit(solution)/shard_map/ppermute | solution.py:22
  150.3 3.3 %collective-permute-done.24 = bf16[16,7168]{1,0:T(8,128)(2,1)S(1)} collective-permute-done((bf16[16,7168]{1,0:T(8,128)(2,1)S(1)}, bf16[16,7168]{1,0:T(8,128)(2,1)S(1)}, u32[]{:S(2)}, u32[]{:S(2)}) %collective-permute-start.24) | collective-permute-done | bytes 229408 | tf_op jit(solution)/shard_map/ppermute | solution.py:22
  153.7 2.0 %collective-permute-start.25 = (bf16[32,7168]{1,0:T(8,128)(2,1)S(1)}, bf16[32,7168]{1,0:T(8,128)(2,1)S(1)}, u32[]{:S(2)}, u32[]{:S(2)}) collective-permute-start(bf16[32,7168]{1,0:T(8,128)(2,1)S(1)} %get-tuple-element.69), channel_id=1, source_target_pairs={{0,2},{1,65},{2,4},{3,67},{4,6},{5,69},{6,0},{7,71},{64,66},{65,12... | collective-permute-start | bytes 1376264 | tf_op jit(solution)/shard_map/ppermute | solution.py:22
  156.0 2.0 %collective-permute-start.28 = (bf16[32,7168]{1,0:T(8,128)(2,1)S(1)}, bf16[32,7168]{1,0:T(8,128)(2,1)S(1)}, u32[]{:S(2)}, u32[]{:S(2)}) collective-permute-start(bf16[32,7168]{1,0:T(8,128)(2,1)S(1)} %get-tuple-element.69), channel_id=1, source_target_pairs={{0,6},{1,193},{2,0},{3,195},{4,2},{5,197},{6,4},{7,199},{64,70},{6... | collective-permute-start | bytes 1376264 | tf_op jit(solution)/shard_map/ppermute | solution.py:22
  158.0 4.1 %collective-permute-done.26 = bf16[32,7168]{1,0:T(8,128)(2,1)S(1)} collective-permute-done((bf16[32,7168]{1,0:T(8,128)(2,1)S(1)}, bf16[32,7168]{1,0:T(8,128)(2,1)S(1)}, u32[]{:S(2)}, u32[]{:S(2)}) %collective-permute-start.26) | collective-permute-done | bytes 458784 | tf_op jit(solution)/shard_map/ppermute | solution.py:22
  162.2 1.9 collective-permute-start.29
  164.3 2.9 %collective-permute-done.27 = bf16[32,7168]{1,0:T(8,128)(2,1)S(1)} collective-permute-done((bf16[32,7168]{1,0:T(8,128)(2,1)S(1)}, bf16[32,7168]{1,0:T(8,128)(2,1)S(1)}, u32[]{:S(2)}, u32[]{:S(2)}) %collective-permute-start.27) | collective-permute-done | bytes 458784 | tf_op jit(solution)/shard_map/ppermute | solution.py:22
  167.3 4.8 %collective-permute-done.29 = bf16[32,7168]{1,0:T(8,128)(2,1)S(1)} collective-permute-done((bf16[32,7168]{1,0:T(8,128)(2,1)S(1)}, bf16[32,7168]{1,0:T(8,128)(2,1)S(1)}, u32[]{:S(2)}, u32[]{:S(2)}) %collective-permute-start.29) | collective-permute-done | bytes 458784 | tf_op jit(solution)/shard_map/ppermute | solution.py:22
  176.8 19.1 %all_to_all.21 = f32[128,2,128]{2,1,0:T(2,128)S(1)} all-to-all(f32[128,2,128]{2,1,0:T(2,128)S(1)} %bitcast.32), channel_id=1, replica_groups=mesh['x'=4,'z'=8,'y'=4,'c'=2] {'x','y','z'}, dimensions={0} | all-to-all | bytes 262144 | tf_op jit(solution)/shard_map/all_to_all | solution.py:217
  (122 shorter events, 41.1 us)
Async XLA Ops:
  0.6 22.3 %collective-permute-start = (bf16[1,7168,192]{1,2,0:T(8,128)(2,1)}, bf16[1,7168,192]{1,2,0:T(8,128)(2,1)S(1)}, u32[]{:S(2)}, u32[]{:S(2)}) collective-permute-start(bf16[1,7168,192]{1,2,0:T(8,128)(2,1)} %param.13), channel_id=1, source_target_pairs={{0,1},{1,0},{2,3},{3,2},{4,5},{5,4},{6,7},{7,6},{8,9},{9,8},{10,11... | collective-permute-start | bytes 8257544 | tf_op jit(solution)/shard_map/ppermute | solution.py:26
  0.7 22.2 %collective-permute-start.1 = (bf16[1,7168,192]{1,2,0:T(8,128)(2,1)}, bf16[1,7168,192]{1,2,0:T(8,128)(2,1)}, u32[]{:S(2)}, u32[]{:S(2)}) collective-permute-start(bf16[1,7168,192]{1,2,0:T(8,128)(2,1)} %param.14), channel_id=1, source_target_pairs={{0,1},{1,0},{2,3},{3,2},{4,5},{5,4},{6,7},{7,6},{8,9},{9,8},{10,11... | collective-permute-start | bytes 8257544 | tf_op jit(solution)/shard_map/ppermute | solution.py:26
  2.8 20.0 %all-to-all-start = ((bf16[8,2,7296]{2,1,0:T(2,128)(2,1)}), bf16[8,2,7296]{2,1,0:T(2,128)(2,1)S(1)}, u32[]{:S(2)}, u32[]{:S(2)}) async-start(bf16[8,2,7296]{2,1,0:T(2,128)(2,1)} %spread.1), calls=%async_computation | async-start | bytes 466944 | tf_op jit(solution)/shard_map/all_to_all | solution.py:42
  11.3 28.4 %collective-permute-start.7 = (bf16[1,192,7168]{2,1,0:T(8,128)(2,1)}, bf16[1,192,7168]{2,1,0:T(8,128)(2,1)}, u32[]{:S(2)}, u32[]{:S(2)}) collective-permute-start(bf16[1,192,7168]{2,1,0:T(8,128)(2,1)} %param.15), channel_id=1, source_target_pairs={{0,1},{1,0},{2,3},{3,2},{4,5},{5,4},{6,7},{7,6},{8,9},{9,8},{10,11... | collective-permute-start | bytes 8257544 | tf_op jit(solution)/shard_map/ppermute | solution.py:26
  25.2 8.2 %collective-permute-start.3 = (bf16[16,7296]{1,0:T(8,128)(2,1)S(1)}, bf16[16,7296]{1,0:T(8,128)(2,1)S(1)}, u32[]{:S(2)}, u32[]{:S(2)}) collective-permute-start(bf16[16,7296]{1,0:T(8,128)(2,1)S(1)} %reshape.43), channel_id=1, source_target_pairs={{0,192},{1,7},{2,194},{3,1},{4,196},{5,3},{6,198},{7,5},{64,0},{65... | collective-permute-start | bytes 700424 | tf_op jit(solution)/shard_map/ppermute | solution.py:22
  27.3 7.6 %collective-permute-start.4 = (bf16[16,7296]{1,0:T(8,128)(2,1)S(1)}, bf16[16,7296]{1,0:T(8,128)(2,1)S(1)}, u32[]{:S(2)}, u32[]{:S(2)}) collective-permute-start(bf16[16,7296]{1,0:T(8,128)(2,1)S(1)} %reshape.43), channel_id=1, source_target_pairs={{0,128},{1,5},{2,130},{3,7},{4,132},{5,1},{6,134},{7,3},{64,192},{... | collective-permute-start | bytes 700424 | tf_op jit(solution)/shard_map/ppermute | solution.py:22
  35.6 8.6 %collective-permute-start.6 = (bf16[32,7296]{1,0:T(8,128)(2,1)S(1)}, bf16[32,7296]{1,0:T(8,128)(2,1)S(1)}, u32[]{:S(2)}, u32[]{:S(2)}) collective-permute-start(bf16[32,7296]{1,0:T(8,128)(2,1)S(1)} %get-tuple-element.57), channel_id=1, source_target_pairs={{0,6},{1,193},{2,0},{3,195},{4,2},{5,197},{6,4},{7,199},{64,70},{6... | collective-permute-start | bytes 1400840 | tf_op jit(solution)/shard_map/ppermute | solution.py:22
  36.0 9.6 %collective-permute-start.5 = (bf16[32,7296]{1,0:T(8,128)(2,1)S(1)}, bf16[32,7296]{1,0:T(8,128)(2,1)S(1)}, u32[]{:S(2)}, u32[]{:S(2)}) collective-permute-start(bf16[32,7296]{1,0:T(8,128)(2,1)S(1)} %get-tuple-element.61), channel_id=1, source_target_pairs={{0,2},{1,65},{2,4},{3,67},{4,6},{5,69},{6,0},{7,71},{64,66},{65,12... | collective-permute-start | bytes 1400840 | tf_op jit(solution)/shard_map/ppermute | solution.py:22
  37.6 13.0 %collective-permute-start.8 = (bf16[32,7296]{1,0:T(8,128)(2,1)S(1)}, bf16[32,7296]{1,0:T(8,128)(2,1)S(1)}, u32[]{:S(2)}, u32[]{:S(2)}) collective-permute-start(bf16[32,7296]{1,0:T(8,128)(2,1)S(1)} %get-tuple-element.57), channel_id=1, source_target_pairs={{0,2},{1,65},{2,4},{3,67},{4,6},{5,69},{6,0},{7,71},{64,66},{65,12... | collective-permute-start | bytes 1400840 | tf_op jit(solution)/shard_map/ppermute | solution.py:22
  39.2 12.2 %collective-permute-start.9 = (bf16[32,7296]{1,0:T(8,128)(2,1)S(1)}, bf16[32,7296]{1,0:T(8,128)(2,1)S(1)}, u32[]{:S(2)}, u32[]{:S(2)}) collective-permute-start(bf16[32,7296]{1,0:T(8,128)(2,1)S(1)} %get-tuple-element.61), channel_id=1, source_target_pairs={{0,6},{1,193},{2,0},{3,195},{4,2},{5,197},{6,4},{7,199},{64,70},{6... | collective-permute-start | bytes 1400840 | tf_op jit(solution)/shard_map/ppermute | solution.py:22
  45.6 10.0 %collective-permute-start.10 = (bf16[32,7296]{1,0:T(8,128)(2,1)S(1)}, bf16[32,7296]{1,0:T(8,128)(2,1)S(1)}, u32[]{:S(2)}, u32[]{:S(2)}) collective-permute-start(bf16[32,7296]{1,0:T(8,128)(2,1)S(1)} %collective-permute-done.5), channel_id=1, source_target_pairs={{0,2},{1,65},{2,4},{3,67},{4,6},{5,69},{6,0},{7,71},{64,66},{65,12... | collective-permute-start | bytes 1400840 | tf_op jit(solution)/shard_map/ppermute | solution.py:22
  46.2 10.2 %collective-permute-start.11 = (bf16[32,7296]{1,0:T(8,128)(2,1)S(1)}, bf16[32,7296]{1,0:T(8,128)(2,1)S(1)}, u32[]{:S(2)}, u32[]{:S(2)}) collective-permute-start(bf16[32,7296]{1,0:T(8,128)(2,1)S(1)} %collective-permute-done.6), channel_id=1, source_target_pairs={{0,6},{1,193},{2,0},{3,195},{4,2},{5,197},{6,4},{7,199},{64,70},{6... | collective-permute-start | bytes 1400840 | tf_op jit(solution)/shard_map/ppermute | solution.py:22
  71.7 9.3 %collective-permute-start.12 = (bf16[32,7168]{1,0:T(8,128)(2,1)S(1)}, bf16[32,7168]{1,0:T(8,128)(2,1)S(1)}, u32[]{:S(2)}, u32[]{:S(2)}) collective-permute-start(bf16[32,7168]{1,0:T(8,128)(2,1)S(1)} %get-tuple-element.51), channel_id=1, source_target_pairs={{0,6},{1,193},{2,0},{3,195},{4,2},{5,197},{6,4},{7,199},{64,70},{6... | collective-permute-start | bytes 1376264 | tf_op jit(solution)/shard_map/ppermute | solution.py:22
  75.0 8.7 %collective-permute-start.13 = (bf16[32,7168]{1,0:T(8,128)(2,1)S(1)}, bf16[32,7168]{1,0:T(8,128)(2,1)S(1)}, u32[]{:S(2)}, u32[]{:S(2)}) collective-permute-start(bf16[32,7168]{1,0:T(8,128)(2,1)S(1)} %get-tuple-element.50), channel_id=1, source_target_pairs={{0,2},{1,65},{2,4},{3,67},{4,6},{5,69},{6,0},{7,71},{64,66},{65,12... | collective-permute-start | bytes 1376264 | tf_op jit(solution)/shard_map/ppermute | solution.py:22
  75.0 13.6 %collective-permute-start.15 = (bf16[32,7168]{1,0:T(8,128)(2,1)S(1)}, bf16[32,7168]{1,0:T(8,128)(2,1)S(1)}, u32[]{:S(2)}, u32[]{:S(2)}) collective-permute-start(bf16[32,7168]{1,0:T(8,128)(2,1)S(1)} %get-tuple-element.48), channel_id=1, source_target_pairs={{0,2},{1,65},{2,4},{3,67},{4,6},{5,69},{6,0},{7,71},{64,66},{65,12... | collective-permute-start | bytes 1376264 | tf_op jit(solution)/shard_map/ppermute | solution.py:22
  76.7 11.9 %collective-permute-start.16 = (bf16[32,7168]{1,0:T(8,128)(2,1)S(1)}, bf16[32,7168]{1,0:T(8,128)(2,1)S(1)}, u32[]{:S(2)}, u32[]{:S(2)}) collective-permute-start(bf16[32,7168]{1,0:T(8,128)(2,1)S(1)} %get-tuple-element.49), channel_id=1, source_target_pairs={{0,6},{1,193},{2,0},{3,195},{4,2},{5,197},{6,4},{7,199},{64,70},{6... | collective-permute-start | bytes 1376264 | tf_op jit(solution)/shard_map/ppermute | solution.py:22
  77.2 18.9 %collective-permute-start.18 = (bf16[7168,256]{1,0:T(8,128)(2,1)S(1)}, bf16[7168,256]{1,0:T(8,128)(2,1)S(1)}, u32[]{:S(2)}, u32[]{:S(2)}) collective-permute-start(bf16[7168,256]{1,0:T(8,128)(2,1)S(1)} %copy-done.5), channel_id=1, source_target_pairs={{0,1},{1,0},{2,3},{3,2},{4,5},{5,4},{6,7},{7,6},{8,9},{9,8},{10,11... | collective-permute-start | bytes 11010056 | tf_op jit(solution)/shard_map/ppermute | solution.py:26
  83.9 9.3 %collective-permute-start.14 = (bf16[32,7168]{1,0:T(8,128)(2,1)S(1)}, bf16[32,7168]{1,0:T(8,128)(2,1)S(1)}, u32[]{:S(2)}, u32[]{:S(2)}) collective-permute-start(bf16[32,7168]{1,0:T(8,128)(2,1)S(1)} %get-tuple-element.35), channel_id=1, source_target_pairs={{0,6},{1,193},{2,0},{3,195},{4,2},{5,197},{6,4},{7,199},{64,70},{6... | collective-permute-start | bytes 1376264 | tf_op jit(solution)/shard_map/ppermute | solution.py:22
  87.2 8.5 %collective-permute-start.17 = (bf16[32,7168]{1,0:T(8,128)(2,1)S(1)}, bf16[32,7168]{1,0:T(8,128)(2,1)S(1)}, u32[]{:S(2)}, u32[]{:S(2)}) collective-permute-start(bf16[32,7168]{1,0:T(8,128)(2,1)S(1)} %get-tuple-element.36), channel_id=1, source_target_pairs={{0,2},{1,65},{2,4},{3,67},{4,6},{5,69},{6,0},{7,71},{64,66},{65,12... | collective-permute-start | bytes 1376264 | tf_op jit(solution)/shard_map/ppermute | solution.py:22
  96.2 8.9 %collective-permute-start.19 = (bf16[16,7168]{1,0:T(8,128)(2,1)S(1)}, bf16[16,7168]{1,0:T(8,128)(2,1)S(1)}, u32[]{:S(2)}, u32[]{:S(2)}) collective-permute-start(bf16[16,7168]{1,0:T(8,128)(2,1)S(1)} %get-tuple-element.54), channel_id=1, source_target_pairs={{0,192},{1,7},{2,194},{3,1},{4,196},{5,3},{6,198},{7,5},{64,0},{65... | collective-permute-start | bytes 688136 | tf_op jit(solution)/shard_map/ppermute | solution.py:22
  101.5 9.7 %collective-permute-start.20 = (bf16[16,7168]{1,0:T(8,128)(2,1)S(1)}, bf16[16,7168]{1,0:T(8,128)(2,1)S(1)}, u32[]{:S(2)}, u32[]{:S(2)}) collective-permute-start(bf16[16,7168]{1,0:T(8,128)(2,1)S(1)} %get-tuple-element.56), channel_id=1, source_target_pairs={{0,64},{1,3},{2,66},{3,5},{4,68},{5,7},{6,70},{7,1},{64,128},{65,6... | collective-permute-start | bytes 688136 | tf_op jit(solution)/shard_map/ppermute | solution.py:22
  101.5 9.7 %collective-permute-start.21 = (bf16[16,7168]{1,0:T(8,128)(2,1)S(1)}, bf16[16,7168]{1,0:T(8,128)(2,1)S(1)}, u32[]{:S(2)}, u32[]{:S(2)}) collective-permute-start(bf16[16,7168]{1,0:T(8,128)(2,1)S(1)} %get-tuple-element.55), channel_id=1, source_target_pairs={{0,128},{1,5},{2,130},{3,7},{4,132},{5,1},{6,134},{7,3},{64,192},{... | collective-permute-start | bytes 688136 | tf_op jit(solution)/shard_map/ppermute | solution.py:22
  126.0 13.4 %all-to-all-start.2 = ((bf16[8,2,7168]{2,1,0:T(2,128)(2,1)}), bf16[8,2,7168]{2,1,0:T(2,128)(2,1)S(1)}, u32[]{:S(2)}, u32[]{:S(2)}) async-start(bf16[8,2,7168]{2,1,0:T(2,128)(2,1)} %broadcast_in_dim.55), calls=%async_computation.2 | async-start | bytes 458752 | tf_op jit(solution)/shard_map/all_to_all | solution.py:42
  139.5 10.5 %collective-permute-start.22 = (bf16[16,7168]{1,0:T(8,128)(2,1)S(1)}, bf16[16,7168]{1,0:T(8,128)(2,1)S(1)}, u32[]{:S(2)}, u32[]{:S(2)}) collective-permute-start(bf16[16,7168]{1,0:T(8,128)(2,1)S(1)} %reshape.45), channel_id=1, source_target_pairs={{0,64},{1,3},{2,66},{3,5},{4,68},{5,7},{6,70},{7,1},{64,128},{65,6... | collective-permute-start | bytes 688136 | tf_op jit(solution)/shard_map/ppermute | solution.py:22
  139.6 10.6 %collective-permute-start.23 = (bf16[16,7168]{1,0:T(8,128)(2,1)S(1)}, bf16[16,7168]{1,0:T(8,128)(2,1)S(1)}, u32[]{:S(2)}, u32[]{:S(2)}) collective-permute-start(bf16[16,7168]{1,0:T(8,128)(2,1)S(1)} %reshape.45), channel_id=1, source_target_pairs={{0,192},{1,7},{2,194},{3,1},{4,196},{5,3},{6,198},{7,5},{64,0},{65... | collective-permute-start | bytes 688136 | tf_op jit(solution)/shard_map/ppermute | solution.py:22
  142.9 10.6 %collective-permute-start.24 = (bf16[16,7168]{1,0:T(8,128)(2,1)S(1)}, bf16[16,7168]{1,0:T(8,128)(2,1)S(1)}, u32[]{:S(2)}, u32[]{:S(2)}) collective-permute-start(bf16[16,7168]{1,0:T(8,128)(2,1)S(1)} %reshape.45), channel_id=1, source_target_pairs={{0,128},{1,5},{2,130},{3,7},{4,132},{5,1},{6,134},{7,3},{64,192},{... | collective-permute-start | bytes 688136 | tf_op jit(solution)/shard_map/ppermute | solution.py:22
  153.6 8.6 %collective-permute-start.26 = (bf16[32,7168]{1,0:T(8,128)(2,1)S(1)}, bf16[32,7168]{1,0:T(8,128)(2,1)S(1)}, u32[]{:S(2)}, u32[]{:S(2)}) collective-permute-start(bf16[32,7168]{1,0:T(8,128)(2,1)S(1)} %get-tuple-element.65), channel_id=1, source_target_pairs={{0,6},{1,193},{2,0},{3,195},{4,2},{5,197},{6,4},{7,199},{64,70},{6... | collective-permute-start | bytes 1376264 | tf_op jit(solution)/shard_map/ppermute | solution.py:22
  153.7 8.6 %collective-permute-start.25 = (bf16[32,7168]{1,0:T(8,128)(2,1)S(1)}, bf16[32,7168]{1,0:T(8,128)(2,1)S(1)}, u32[]{:S(2)}, u32[]{:S(2)}) collective-permute-start(bf16[32,7168]{1,0:T(8,128)(2,1)S(1)} %get-tuple-element.69), channel_id=1, source_target_pairs={{0,2},{1,65},{2,4},{3,67},{4,6},{5,69},{6,0},{7,71},{64,66},{65,12... | collective-permute-start | bytes 1376264 | tf_op jit(solution)/shard_map/ppermute | solution.py:22
  155.9 11.2 %collective-permute-start.27 = (bf16[32,7168]{1,0:T(8,128)(2,1)S(1)}, bf16[32,7168]{1,0:T(8,128)(2,1)S(1)}, u32[]{:S(2)}, u32[]{:S(2)}) collective-permute-start(bf16[32,7168]{1,0:T(8,128)(2,1)S(1)} %get-tuple-element.65), channel_id=1, source_target_pairs={{0,2},{1,65},{2,4},{3,67},{4,6},{5,69},{6,0},{7,71},{64,66},{65,12... | collective-permute-start | bytes 1376264 | tf_op jit(solution)/shard_map/ppermute | solution.py:22
  156.0 11.2 %collective-permute-start.28 = (bf16[32,7168]{1,0:T(8,128)(2,1)S(1)}, bf16[32,7168]{1,0:T(8,128)(2,1)S(1)}, u32[]{:S(2)}, u32[]{:S(2)}) collective-permute-start(bf16[32,7168]{1,0:T(8,128)(2,1)S(1)} %get-tuple-element.69), channel_id=1, source_target_pairs={{0,6},{1,193},{2,0},{3,195},{4,2},{5,197},{6,4},{7,199},{64,70},{6... | collective-permute-start | bytes 1376264 | tf_op jit(solution)/shard_map/ppermute | solution.py:22
  162.2 9.8 %collective-permute-start.29 = (bf16[32,7168]{1,0:T(8,128)(2,1)S(1)}, bf16[32,7168]{1,0:T(8,128)(2,1)S(1)}, u32[]{:S(2)}, u32[]{:S(2)}) collective-permute-start(bf16[32,7168]{1,0:T(8,128)(2,1)S(1)} %collective-permute-done.25), channel_id=1, source_target_pairs={{0,2},{1,65},{2,4},{3,67},{4,6},{5,69},{6,0},{7,71},{64,66},{65,12... | collective-permute-start | bytes 1376264 | tf_op jit(solution)/shard_map/ppermute | solution.py:22
  164.2 8.5 %collective-permute-start.30 = (bf16[32,7168]{1,0:T(8,128)(2,1)S(1)}, bf16[32,7168]{1,0:T(8,128)(2,1)S(1)}, u32[]{:S(2)}, u32[]{:S(2)}) collective-permute-start(bf16[32,7168]{1,0:T(8,128)(2,1)S(1)} %collective-permute-done.26), channel_id=1, source_target_pairs={{0,6},{1,193},{2,0},{3,195},{4,2},{5,197},{6,4},{7,199},{64,70},{6... | collective-permute-start | bytes 1376264 | tf_op jit(solution)/shard_map/ppermute | solution.py:22
  (15 other events, 220.7 us)

commit v2 on v1

--- a/solution.py
+++ b/solution.py
@@ -7,6 +7,7 @@
 
 META = 128
 PLANE = ("x", "y", "c")
+ANY = pl.BlockSpec(memory_space=pl.ANY)
 SMEM = pl.BlockSpec(memory_space=pltpu.SMEM)
 VMEM = pl.BlockSpec(memory_space=pltpu.VMEM)
 
@@ -42,20 +43,22 @@
     return lax.all_to_all(spread, "z", 0, 0, tiled=True).reshape(depth * rows, width)
 
 
-def first_axis_rows(column):
-    return jnp.concatenate(
-        [column, move(column, 1, 0), move(column, -1, 0), move(column, 2, 0)], axis=0
-    )
-
-
-def second_axis_rows(wide, *extra):
+def first_axis_rows(column, *extra):
+    up, down = move(column, 1, 0), move(column, -1, 0)
+    far, *extra = together(move(column, 2, 0), *extra)
+    return jnp.concatenate([column, up, down, far], axis=0), *extra
+
+
+def second_axis_rows(wide, staged, *extra):
     half = wide.shape[0] // 2
     top, low = wide[:half], wide[half:]
-    up_top, down_low, *extra = together(move(top, 1, 1), move(low, -1, 1), *extra)
+    up_top, down_low = move(top, 1, 1), move(low, -1, 1)
+    top, low, staged = together(top, low, staged)
     up_low, down_top = move(low, 1, 1), move(top, -1, 1)
+    up_top, down_low, *extra = together(up_top, down_low, *extra)
     far_top, far_low = move(up_top, 1, 1), move(down_low, -1, 1)
     rows = jnp.concatenate([wide, up_top, up_low, down_top, down_low, far_top, far_low], axis=0)
-    return rows, *extra
+    return rows, staged, *extra
 
 
 def narrow(*values):
@@ -118,10 +121,96 @@
     )(targets, tokens, routes, route_gates)
 
 
-def stats_kernel(place_ref, own_ref, other_ref, goal_ref, out_ref, stats):
+def stage_kernel(*refs):
+    sources, out, sems = refs[:-2], refs[-2], refs[-1]
+    rows = sources[0].shape[0]
+    copies = [
+        pltpu.make_async_copy(source, out.at[pl.ds(index * rows, rows)], sems.at[index])
+        for index, source in enumerate(sources)
+    ]
+    for copy in copies:
+        copy.start()
+    for copy in copies:
+        copy.wait()
+
+
+def stage(*weights):
+    rows, width = weights[0].shape
+    shape = (len(weights) * rows, width)
+    return pl.pallas_call(
+        stage_kernel,
+        out_shape=pltpu.VMEM(shape, weights[0].dtype),
+        in_specs=[ANY] * len(weights),
+        out_specs=VMEM,
+        scratch_shapes=[pltpu.SemaphoreType.DMA((len(weights),))],
+        cost_estimate=pl.CostEstimate(
+            flops=0, bytes_accessed=4 * shape[0] * shape[1], transcendentals=0
+        ),
+        compiler_params=pltpu.CompilerParams(vmem_limit_bytes=2**20),
+        name="stage",
+    )(*weights)
+
+
+def expert_kernel(expert_ref, row_ref, in_ref, down_ref, out_ref, meta_ref, inner, active):
+    width, units = down_ref.shape[1], down_ref.shape[0]
+    part = 128 * 3
+    for start in range(0, 2 * units, part):
+        inner[:, start : start + part] = lax.dot_general(
+            row_ref[:, :width],
+            in_ref[start : start + part, :],
+            (((1,), (1,)), ((), ())),
+            preferred_element_type=jnp.float32,
+        )
+    meta = row_ref[:, width:].astype(jnp.float32)
+    meta_ref[...] = meta
+    lane = lax.broadcasted_iota(jnp.int32, meta.shape, 1)
+    gates = pltpu.roll(meta, META - 8, 1)
+    chosen = (lane < 8) & (meta == expert_ref[0].astype(jnp.float32))
+    share = jnp.sum(jnp.where(chosen, gates, 0.0), axis=1, keepdims=True)
+    gate = inner[:, :units]
+    value = gate / (1.0 + jnp.exp(-gate)) * inner[:, units:] * share
+    active[...] = value.astype(jnp.bfloat16)
+    step = width // 7
+
+    @pl.loop(0, 7)
+    def _(index):
+        span = pl.ds(pl.multiple_of(index * step, step), step)
+        out_ref[:, span] = jnp.dot(
+            active[...], down_ref[:, span], preferred_element_type=jnp.float32
+        ).astype(jnp.bfloat16)
+
+
+def expert_layer(rows, in_weight, out_weight, expert):
+    count = rows.shape[0]
+    units, width = out_weight.shape
+    return pl.pallas_call(
+        expert_kernel,
+        out_shape=[
+            jax.ShapeDtypeStruct((count, width), jnp.bfloat16),
+            jax.ShapeDtypeStruct((count, META), jnp.float32),
+        ],
+        in_specs=[SMEM, VMEM, VMEM, VMEM],
+        out_specs=[VMEM, VMEM],
+        scratch_shapes=[
+            pltpu.VMEM((count, 2 * units), jnp.float32),
+            pltpu.VMEM((count, units), jnp.bfloat16),
+        ],
+        cost_estimate=pl.CostEstimate(
+            flops=6 * count * units * width,
+            bytes_accessed=2 * (3 * units * width + 2 * count * width),
+            transcendentals=count * units,
+        ),
+        compiler_params=pltpu.CompilerParams(vmem_limit_bytes=16 * 2**20),
+        name="expert",
+    )(expert, rows, in_weight, out_weight)
+
+
+def stats_kernel(place_ref, own_ref, other_ref, meta_ref, out_ref, stats):
     rows = own_ref.shape[0]
     lane = lax.broadcasted_iota(jnp.int32, (rows, META), 1)
-    goal = goal_ref[...]
+    meta = meta_ref[...]
+    goal = jnp.where(lane == 16, meta * 256.0, jnp.where(lane == 17, meta, 0.0))
+    goal = jnp.sum(goal, axis=1, keepdims=True).astype(jnp.int32)
     own, other = own_ref[...], other_ref[...]
     top = jnp.maximum(jnp.max(own, axis=1, keepdims=True), jnp.max(other, axis=1, keepdims=True))
     total = jnp.zeros_like(top)
@@ -130,24 +219,49 @@
         total += jnp.sum(jnp.exp(value - top), axis=1, keepdims=True)
         column = lax.broadcasted_iota(jnp.int32, value.shape, 1) + place_ref[which]
         picked += jnp.sum(jnp.where(column == goal, value, 0.0), axis=1, keepdims=True)
-    stats[...] = jnp.where(lane == 0, top, jnp.where(lane == 1, total, picked))
-    block = rows // 16
+    values = jnp.where(lane == 0, top, jnp.where(lane == 1, total, picked))
+    stats[...] = jnp.where(lane < 3, values, 0.0)
+    block = rows // 32
     for index in range(16):
+        first = stats[pl.ds(index * 2 * block, block, 2), :]
+        second = stats[pl.ds(index * 2 * block + 1, block, 2), :]
         target = pl.multiple_of(place_ref[2 + index] * block, block)
-        out_ref[pl.ds(target, block), :] = stats[pl.ds(index * block, block), :]
-
-
-def row_stats(own, other, goals, place):
+        out_ref[pl.ds(target, block), :] = first + pltpu.roll(second, 4, 1)
+
+
+def combine_kernel(stats_ref, out_ref):
+    stats = stats_ref[...]
+    lane = lax.broadcasted_iota(jnp.int32, (1, META), 1)
+    top = jnp.max(stats, axis=0, keepdims=True)
+    scale = jnp.exp(stats - top)
+    total = jnp.sum(pltpu.roll(scale, 1, 1) * stats, axis=0, keepdims=True)
+    picked = jnp.sum(stats, axis=0, keepdims=True)
+    result = pltpu.roll(picked, META - 2, 1) - top - jnp.log(pltpu.roll(total, META - 1, 1))
+    out_ref[...] = jnp.where((lane == 0) | (lane == 4), result, 0.0)
+
+
+def combine(stats):
+    return pl.pallas_call(
+        combine_kernel,
+        out_shape=jax.ShapeDtypeStruct((1, META), jnp.float32),
+        in_specs=[VMEM],
+        out_specs=VMEM,
+        compiler_params=pltpu.CompilerParams(vmem_limit_bytes=4 * 2**20),
+        name="combine",
+    )(stats)
+
+
+def row_stats(own, other, meta, place):
     rows = own.shape[0]
     return pl.pallas_call(
         stats_kernel,
-        out_shape=jax.ShapeDtypeStruct((rows, META), jnp.float32),
+        out_shape=jax.ShapeDtypeStruct((rows // 2, META), jnp.float32),
         in_specs=[SMEM, VMEM, VMEM, VMEM],
         out_specs=VMEM,
         scratch_shapes=[pltpu.VMEM((rows, META), jnp.float32)],
         compiler_params=pltpu.CompilerParams(vmem_limit_bytes=8 * 2**20),
         name="row_stats",
-    )(place, own, other, goals)
+    )(place, own, other, meta)
 
 
 def shards(
@@ -165,33 +279,6 @@
 
     def product(left, right):
         return jnp.dot(left, right, preferred_element_type=jnp.float32)
-
-    column, gate, up = together(
-        column_rows(spread_tokens(tokens, routes, route_gates, targets, depth)),
-        swap(expert_gate),
-        swap(expert_up),
-    )
-    rows, down = second_axis_rows(first_axis_rows(column), swap(expert_down))
-    out_weight = jnp.concatenate([expert_down[0], down[0]], axis=0)
-    meta = rows[:, width:].astype(jnp.float32)
-    expert = lax.axis_index(("x", "z")).astype(jnp.float32)
-    share = jnp.sum(jnp.where(meta[:, :8] == expert, meta[:, 8:16], 0.0), axis=1, keepdims=True)
-    goals = (meta[:, 16:17] * 256.0 + meta[:, 17:18]).astype(jnp.int32)
-    rows = rows[:, :width]
-    inner = together(*(product(rows, w[0]) for w in (expert_gate, expert_up, gate, up)))
-    active = jnp.concatenate(
-        [jax.nn.silu(inner[i]) * inner[i + 1] * share for i in (0, 2)], axis=1
-    )
-    partial = product(together(active.astype(jnp.bfloat16))[0], out_weight)
-    partial, head_weight = together(partial.astype(jnp.bfloat16), head_weight)
-    folded, head = together(fold_second_axis(partial), swap(head_weight))
-    heads = [head_weight, head]
-    moe = fold_column(fold_first_axis(folded))
-
-    hidden = (tokens.astype(jnp.float32) + moe).astype(jnp.bfloat16)
-    widened = hidden.astype(jnp.float32)
-    inverse = lax.rsqrt(jnp.mean(widened * widened, axis=-1, keepdims=True) + 1e-06)
-    normed = (widened * inverse * norm_gain).astype(jnp.bfloat16)
 
     columns = head_weight.shape[1]
     core = lax.axis_index("c")
@@ -208,16 +295,34 @@
             (from_x * lax.axis_size("y") + from_y).reshape(16),
         ]
     ).astype(jnp.int32)
+    expert = lax.axis_index(("x", "z")).astype(jnp.int32)[None]
+    column, gate, up, place, expert = together(
+        column_rows(spread_tokens(tokens, routes, route_gates, targets, depth)),
+        swap(expert_gate),
+        swap(expert_up),
+        place,
+        expert,
+    )
+    wide, down = first_axis_rows(column, swap(expert_down))
+    rows, out_weight, gate, up, head = second_axis_rows(
+        wide, stage(expert_down[0], down[0]), gate, up, swap(head_weight)
+    )
+    in_weight = stage(expert_gate[0].T, gate[0].T, expert_up[0].T, up[0].T)
+    partial, meta = expert_layer(rows, in_weight, out_weight, expert)
+    folded = fold_second_axis(partial)
+    moe = fold_column(fold_first_axis(folded))
+
+    hidden = (tokens.astype(jnp.float32) + moe).astype(jnp.bfloat16)
+    widened = hidden.astype(jnp.float32)
+    inverse = lax.rsqrt(jnp.mean(widened * widened, axis=-1, keepdims=True) + 1e-06)
+    normed = (widened * inverse * norm_gain).astype(jnp.bfloat16)
+
     column = column_rows(jnp.broadcast_to(normed[None], (depth,) + normed.shape))
-    every, = second_axis_rows(first_axis_rows(column))
-    logits = [product(every, head) for head in heads]
-    stats = row_stats(*logits, jnp.broadcast_to(goals, (goals.shape[0], 1)), place)
-    chips = lax.axis_size(("x", "y", "z"))
-    stats = stats.reshape(chips, 2, META)
+    wide, head = first_axis_rows(column, head)
+    every, head = second_axis_rows(wide, stage(head))
+    stats = row_stats(product(every, head_weight), product(every, head), meta, place)
     arrived = lax.all_to_all(stats, ("x", "y", "z"), 0, 0, tiled=True)
-    row_top = jnp.max(arrived[:, :, 0], axis=0)
-    exp_total = jnp.sum(arrived[:, :, 1] * jnp.exp(arrived[:, :, 0] - row_top), axis=0)
-    logprob = jnp.sum(arrived[:, :, 2], axis=0) - (row_top + jnp.log(exp_total))
+    logprob = combine(arrived)[0, 0:8:4]
     return (logprob, hidden)
 
 

time: 198 us -> 187 us (0.944)
  Pallas kernels: 2.56 us -> 17.3 us
  waiting for transfers between devices: 81.2 us -> 66.7 us
  blocking collectives: 32.3 us -> 45.8 us
  matrix products: 15.6 us -> 2.22 us
  local copies, waits for them, and re-layouts: 11.1 us -> 2.06 us
    pallas_call x1 -> x6, Pallas kernels: 0.98 us -> 15.6 us  [the longest x3 7.43 us: stage(): pl.pallas_call(stage_kernel, out_shape=pltpu.VMEM(shape, weights[0].dtype...]
    dot_general x7 -> x2, matrix products: 15.6 us -> 2.22 us  [product(): return jnp.dot(left, right, preferred_element_type=jnp.float32)]
    all_to_all x0 -> x1, blocking collectives: none -> 12.5 us  [column_rows(): lax.all_to_all(spread, 'z', 0, 0, tiled=True).reshape(depth * rows, width)]
    all_to_all x2 -> x1, waiting for transfers between devices: 21.3 us -> 10.6 us  [column_rows(): lax.all_to_all(spread, 'z', 0, 0, tiled=True).reshape(depth * rows, width)]
    unnamed x43 -> x28, local copies, waits for them, and re-layouts: 7.3 us -> 0.52 us
    ppermute x27, waiting for transfers between devices: 59.9 us -> 56.1 us  [move(): return lax.ppermute(value, PLANE, pairs)]
    all_to_all x2 -> x1, starting transfers between devices: 11.9 us -> 8.47 us  [column_rows(): lax.all_to_all(spread, 'z', 0, 0, tiled=True).reshape(depth * rows, width)]
  transfers between devices with their start and end apart: 33 -> 32, of which waited for: 24 -> 19; matrix products, arithmetic and copies ran while one was open for 4% -> 1% of each run, Pallas kernels for 1% -> 5%
where the time goes in v2:
time: 187 us; the launch traced here: 186 us
  waiting for transfers between devices  66.7 us (36%)
  starting transfers between devices  49.1 us (26%)
  blocking collectives  45.8 us (24%)
  Pallas kernels  17.3 us (9%)
  matrix products  2.22 us (1%)
  local copies, waits for them, and re-layouts  2.06 us (1%)
  other arithmetic  2.03 us (1%)
    ppermute x27, waiting for transfers between devices, move(): return lax.ppermute(value, PLANE, pairs)  56.1 us
    ppermute x27, starting transfers between devices, move(): return lax.ppermute(value, PLANE, pairs)  39.9 us
    all_to_all x1, blocking collectives, shards(): arrived = lax.all_to_all(stats, ('x', 'y', 'z'), 0, 0, tiled=True)  19.1 us
    all_to_all x1, blocking collectives, fold_column(): lax.all_to_all(partial.reshape(depth, 2, width), 'z', 0, 0, tiled=True)  14.2 us
    all_to_all x1, blocking collectives, column_rows(): lax.all_to_all(spread, 'z', 0, 0, tiled=True).reshape(depth * rows, width)  12.5 us
    all_to_all x1, waiting for transfers between devices, column_rows(): lax.all_to_all(spread, 'z', 0, 0, tiled=True).reshape(depth * rows, width)  10.6 us
    all_to_all x1, starting transfers between devices, column_rows(): lax.all_to_all(spread, 'z', 0, 0, tiled=True).reshape(depth * rows, width)  8.47 us
    pallas_call x3, Pallas kernels, stage(): pl.pallas_call(stage_kernel, out_shape=pltpu.VMEM(shape, weights[0].dtype...  7.43 us
  transfers between devices with their start and end apart: 32, of which 19 were waited for; matrix products, arithmetic and copies ran while one was open for 1% of the time, Pallas kernels for 5%

profile of v2, /device:TPU:8, one launch (start us, length us, event | category | flops | bytes accessed | tf_op | source)
XLA Modules:
  0.0 186.3 jit_solution(4988528593849269173)
XLA Ops:
  1.3 1.7 spread.1
  3.0 8.5 %all-to-all-start = ((bf16[8,2,7296]{2,1,0:T(2,128)(2,1)}), bf16[8,2,7296]{2,1,0:T(2,128)(2,1)S(1)}, u32[]{:S(2)}, u32[]{:S(2)}) async-start(bf16[8,2,7296]{2,1,0:T(2,128)(2,1)} %spread.1), calls=%async_computation | async-start | bytes 466944 | tf_op jit(solution)/shard_map/all_to_all | solution.py:43
  12.6 10.6 %all-to-all-done = bf16[8,2,7296]{2,1,0:T(2,128)(2,1)S(1)} async-done(((bf16[8,2,7296]{2,1,0:T(2,128)(2,1)}), bf16[8,2,7296]{2,1,0:T(2,128)(2,1)S(1)}, u32[]{:S(2)}, u32[]{:S(2)}) %all-to-all-start) | async-done | bytes 233504 | tf_op jit(solution)/shard_map/all_to_all | solution.py:43
  23.3 3.1 %collective-permute-start.4 = (bf16[16,7296]{1,0:T(8,128)(2,1)S(1)}, bf16[16,7296]{1,0:T(8,128)(2,1)S(1)}, u32[]{:S(2)}, u32[]{:S(2)}) collective-permute-start(bf16[16,7296]{1,0:T(8,128)(2,1)S(1)} %reshape.40), channel_id=1, source_target_pairs={{0,128},{1,5},{2,130},{3,7},{4,132},{5,1},{6,134},{7,3},{64,192},{... | collective-permute-start | bytes 700424 | tf_op jit(solution)/shard_map/ppermute | solution.py:23
  28.5 6.4 %collective-permute-done.2 = bf16[16,7296]{1,0:T(8,128)(2,1)S(1)} collective-permute-done((bf16[16,7296]{1,0:T(8,128)(2,1)S(1)}, bf16[16,7296]{1,0:T(8,128)(2,1)S(1)}, u32[]{:S(2)}, u32[]{:S(2)}) %collective-permute-start.2) | collective-permute-done | bytes 233504 | tf_op jit(solution)/shard_map/ppermute | solution.py:23
  37.1 2.3 %stage.3.down_ref = bf16[384,7168]{1,0:T(8,128)(2,1)S(1)} custom-call(bf16[192,7168]{1,0:T(8,128)(2,1)S(1)} %bitcast.26, bf16[192,7168]{1,0:T(8,128)(2,1)} %bitcast.4.refs_1_), custom_call_target="tpu_custom_call" | custom-call | bytes 11010048 | tf_op jit(solution)/shard_map/stage/pallas_call | solution.py:140
  41.5 2.1 %collective-permute-done.7 = bf16[32,7296]{1,0:T(8,128)(2,1)S(1)} collective-permute-done((bf16[32,7296]{1,0:T(8,128)(2,1)S(1)}, bf16[32,7296]{1,0:T(8,128)(2,1)S(1)}, u32[]{:S(2)}, u32[]{:S(2)}) %collective-permute-start.7) | collective-permute-done | bytes 466976 | tf_op jit(solution)/shard_map/ppermute | solution.py:23
  45.7 2.7 %collective-permute-start.12 = (bf16[32,7296]{1,0:T(8,128)(2,1)S(1)}, bf16[32,7296]{1,0:T(8,128)(2,1)S(1)}, u32[]{:S(2)}, u32[]{:S(2)}) collective-permute-start(bf16[32,7296]{1,0:T(8,128)(2,1)S(1)} %collective-permute-done.7), channel_id=1, source_target_pairs={{0,6},{1,193},{2,0},{3,195},{4,2},{5,197},{6,4},{7,199},{64,70},{6... | collective-permute-start | bytes 1400840 | tf_op jit(solution)/shard_map/ppermute | solution.py:23
  48.4 3.1 %stage.4.in_ref = bf16[768,7168]{1,0:T(8,128)(2,1)S(1)} custom-call(bf16[192,7168]{1,0:T(8,128)(2,1)S(1)} %bitcast.27, bf16[192,7168]{1,0:T(8,128)(2,1)} %bitcast.8.refs_1_, bf16[192,7168]{1,0:T(8,128)(2,1)S(1)} %bitcast.28, bf16[192,7168]{1,0:T(8,128)(2,1)} %bitcast.12.refs_3_), custom_call_target="tpu_custom_call" | custom-call | bytes 22020096 | tf_op jit(solution)/shard_map/stage/pallas_call | solution.py:140
  51.6 3.5 %collective-permute-done.11 = bf16[32,7296]{1,0:T(8,128)(2,1)S(1)} collective-permute-done((bf16[32,7296]{1,0:T(8,128)(2,1)S(1)}, bf16[32,7296]{1,0:T(8,128)(2,1)S(1)}, u32[]{:S(2)}, u32[]{:S(2)}) %collective-permute-start.11) | collective-permute-done | bytes 466976 | tf_op jit(solution)/shard_map/ppermute | solution.py:23
  55.2 7.0 %expert.1 = (bf16[256,7168]{1,0:T(8,128)(2,1)S(1)}, f32[256,128]{1,0:T(8,128)S(1)}) custom-call(s32[1]{0:T(128)} %bitcast.2.expert_ref, bf16[256,7296]{1,0:T(8,128)(2,1)S(1)} %constant_dynamic-update-slice_fusion.4.row_ref, bf16[768,7168]{1,0:T(8,128)(2,1)S(1)} %stage.4.in_ref, bf16[384,7168]{1,0:T(8,128)(2,1)S(1)} %stage.3.down_ref), custom_call_target="tpu_custom_call" | custom-call | flops 4227858432 | bytes 23855104 | tf_op jit(solution)/shard_map/expert/pallas_call | solution.py:186
  62.4 2.4 %collective-permute-start.14 = (bf16[32,7168]{1,0:T(8,128)(2,1)S(1)}, bf16[32,7168]{1,0:T(8,128)(2,1)S(1)}, u32[]{:S(2)}, u32[]{:S(2)}) collective-permute-start(bf16[32,7168]{1,0:T(8,128)(2,1)S(1)} %get-tuple-element.64), channel_id=1, source_target_pairs={{0,2},{1,65},{2,4},{3,67},{4,6},{5,69},{6,0},{7,71},{64,66},{65,12... | collective-permute-start | bytes 1376264 | tf_op jit(solution)/shard_map/ppermute | solution.py:23
  65.8 2.3 %collective-permute-start.16 = (bf16[32,7168]{1,0:T(8,128)(2,1)S(1)}, bf16[32,7168]{1,0:T(8,128)(2,1)S(1)}, u32[]{:S(2)}, u32[]{:S(2)}) collective-permute-start(bf16[32,7168]{1,0:T(8,128)(2,1)S(1)} %get-tuple-element.62), channel_id=1, source_target_pairs={{0,2},{1,65},{2,4},{3,67},{4,6},{5,69},{6,0},{7,71},{64,66},{65,12... | collective-permute-start | bytes 1376264 | tf_op jit(solution)/shard_map/ppermute | solution.py:23
  68.9 3.2 %collective-permute-done.14 = bf16[32,7168]{1,0:T(8,128)(2,1)S(1)} collective-permute-done((bf16[32,7168]{1,0:T(8,128)(2,1)S(1)}, bf16[32,7168]{1,0:T(8,128)(2,1)S(1)}, u32[]{:S(2)}, u32[]{:S(2)}) %collective-permute-start.14) | collective-permute-done | bytes 458784 | tf_op jit(solution)/shard_map/ppermute | solution.py:23
  72.1 2.3 %collective-permute-done.13 = bf16[32,7168]{1,0:T(8,128)(2,1)S(1)} collective-permute-done((bf16[32,7168]{1,0:T(8,128)(2,1)S(1)}, bf16[32,7168]{1,0:T(8,128)(2,1)S(1)}, u32[]{:S(2)}, u32[]{:S(2)}) %collective-permute-start.13) | collective-permute-done | bytes 458784 | tf_op jit(solution)/shard_map/ppermute | solution.py:23
  77.1 2.3 %collective-permute-done.18 = bf16[32,7168]{1,0:T(8,128)(2,1)S(1)} collective-permute-done((bf16[32,7168]{1,0:T(8,128)(2,1)S(1)}, bf16[32,7168]{1,0:T(8,128)(2,1)S(1)}, u32[]{:S(2)}, u32[]{:S(2)}) %collective-permute-start.18) | collective-permute-done | bytes 458784 | tf_op jit(solution)/shard_map/ppermute | solution.py:23
  79.4 5.0 %collective-permute-done.15 = bf16[32,7168]{1,0:T(8,128)(2,1)S(1)} collective-permute-done((bf16[32,7168]{1,0:T(8,128)(2,1)S(1)}, bf16[32,7168]{1,0:T(8,128)(2,1)S(1)}, u32[]{:S(2)}, u32[]{:S(2)}) %collective-permute-start.15) | collective-permute-done | bytes 458784 | tf_op jit(solution)/shard_map/ppermute | solution.py:23
  87.9 2.6 %collective-permute-start.21 = (bf16[16,7168]{1,0:T(8,128)(2,1)S(1)}, bf16[16,7168]{1,0:T(8,128)(2,1)S(1)}, u32[]{:S(2)}, u32[]{:S(2)}) collective-permute-start(bf16[16,7168]{1,0:T(8,128)(2,1)S(1)} %get-tuple-element.69), channel_id=1, source_target_pairs={{0,128},{1,5},{2,130},{3,7},{4,132},{5,1},{6,134},{7,3},{64,192},{... | collective-permute-start | bytes 688136 | tf_op jit(solution)/shard_map/ppermute | solution.py:23
  91.9 2.5 %collective-permute-done.20 = bf16[16,7168]{1,0:T(8,128)(2,1)S(1)} collective-permute-done((bf16[16,7168]{1,0:T(8,128)(2,1)S(1)}, bf16[16,7168]{1,0:T(8,128)(2,1)S(1)}, u32[]{:S(2)}, u32[]{:S(2)}) %collective-permute-start.20) | collective-permute-done | bytes 229408 | tf_op jit(solution)/shard_map/ppermute | solution.py:23
  94.4 2.5 %collective-permute-done.21 = bf16[16,7168]{1,0:T(8,128)(2,1)S(1)} collective-permute-done((bf16[16,7168]{1,0:T(8,128)(2,1)S(1)}, bf16[16,7168]{1,0:T(8,128)(2,1)S(1)}, u32[]{:S(2)}, u32[]{:S(2)}) %collective-permute-start.21) | collective-permute-done | bytes 229408 | tf_op jit(solution)/shard_map/ppermute | solution.py:23
  97.2 14.2 %all_to_all.26 = bf16[8,2,7168]{2,1,0:T(2,128)(2,1)S(1)} all-to-all(bf16[8,2,7168]{2,1,0:T(2,128)(2,1)S(1)} %reshape.41), channel_id=1, replica_groups=mesh['x'=4,'z'=8,'y'=4,'c'=2] {'z'}, dimensions={0} | all-to-all | bytes 458752 | tf_op jit(solution)/shard_map/all_to_all | solution.py:90
  112.0 12.5 %all_to_all.27 = bf16[8,2,7168]{2,1,0:T(2,128)(2,1)S(1)} all-to-all(bf16[8,2,7168]{2,1,0:T(2,128)(2,1)S(1)} %broadcast_in_dim.52), channel_id=1, replica_groups=mesh['x'=4,'z'=8,'y'=4,'c'=2] {'z'}, dimensions={0} | all-to-all | bytes 458752 | tf_op jit(solution)/shard_map/all_to_all | solution.py:43
  128.1 10.3 %collective-permute-done.22 = bf16[16,7168]{1,0:T(8,128)(2,1)S(1)} collective-permute-done((bf16[16,7168]{1,0:T(8,128)(2,1)S(1)}, bf16[16,7168]{1,0:T(8,128)(2,1)S(1)}, u32[]{:S(2)}, u32[]{:S(2)}) %collective-permute-start.22) | collective-permute-done | bytes 229408 | tf_op jit(solution)/shard_map/ppermute | solution.py:23
  138.5 6.2 %collective-permute-start.26 = (bf16[32,7168]{1,0:T(8,128)(2,1)S(1)}, bf16[32,7168]{1,0:T(8,128)(2,1)S(1)}, u32[]{:S(2)}, u32[]{:S(2)}) collective-permute-start(bf16[32,7168]{1,0:T(8,128)(2,1)S(1)} %get-tuple-element.53), channel_id=1, source_target_pairs={{0,6},{1,193},{2,0},{3,195},{4,2},{5,197},{6,4},{7,199},{64,70},{6... | collective-permute-start | bytes 1376264 | tf_op jit(solution)/shard_map/ppermute | solution.py:23
  144.8 2.0 %stage.5 = bf16[7168,256]{1,0:T(8,128)(2,1)S(1)} custom-call(bf16[7168,256]{1,0:T(8,128)(2,1)} %collective-permute-done.8.refs_0_), custom_call_target="tpu_custom_call" | custom-call | bytes 7340032 | tf_op jit(solution)/shard_map/stage/pallas_call | solution.py:140
  146.9 2.1 %collective-permute-start.28 = (bf16[32,7168]{1,0:T(8,128)(2,1)S(1)}, bf16[32,7168]{1,0:T(8,128)(2,1)S(1)}, u32[]{:S(2)}, u32[]{:S(2)}) collective-permute-start(bf16[32,7168]{1,0:T(8,128)(2,1)S(1)} %get-tuple-element.54), channel_id=1, source_target_pairs={{0,6},{1,193},{2,0},{3,195},{4,2},{5,197},{6,4},{7,199},{64,70},{6... | collective-permute-start | bytes 1376264 | tf_op jit(solution)/shard_map/ppermute | solution.py:23
  149.0 1.7 collective-permute-done.26
  150.8 2.5 %collective-permute-done.25 = bf16[32,7168]{1,0:T(8,128)(2,1)S(1)} collective-permute-done((bf16[32,7168]{1,0:T(8,128)(2,1)S(1)}, bf16[32,7168]{1,0:T(8,128)(2,1)S(1)}, u32[]{:S(2)}, u32[]{:S(2)}) %collective-permute-start.25) | collective-permute-done | bytes 458784 | tf_op jit(solution)/shard_map/ppermute | solution.py:23
  153.3 2.0 %collective-permute-start.30 = (bf16[32,7168]{1,0:T(8,128)(2,1)S(1)}, bf16[32,7168]{1,0:T(8,128)(2,1)S(1)}, u32[]{:S(2)}, u32[]{:S(2)}) collective-permute-start(bf16[32,7168]{1,0:T(8,128)(2,1)S(1)} %collective-permute-done.26), channel_id=1, source_target_pairs={{0,6},{1,193},{2,0},{3,195},{4,2},{5,197},{6,4},{7,199},{64,70},{6... | collective-permute-start | bytes 1376264 | tf_op jit(solution)/shard_map/ppermute | solution.py:23
  155.3 2.9 %collective-permute-done.27 = bf16[32,7168]{1,0:T(8,128)(2,1)S(1)} collective-permute-done((bf16[32,7168]{1,0:T(8,128)(2,1)S(1)}, bf16[32,7168]{1,0:T(8,128)(2,1)S(1)}, u32[]{:S(2)}, u32[]{:S(2)}) %collective-permute-start.27) | collective-permute-done | bytes 458784 | tf_op jit(solution)/shard_map/ppermute | solution.py:23
  158.3 4.8 %collective-permute-done.29 = bf16[32,7168]{1,0:T(8,128)(2,1)S(1)} collective-permute-done((bf16[32,7168]{1,0:T(8,128)(2,1)S(1)}, bf16[32,7168]{1,0:T(8,128)(2,1)S(1)}, u32[]{:S(2)}, u32[]{:S(2)}) %collective-permute-start.29) | collective-permute-done | bytes 458784 | tf_op jit(solution)/shard_map/ppermute | solution.py:23
  166.5 19.1 %all_to_all.28 = f32[128,1,128]{2,1,0:T(1,128)S(1)} all-to-all(f32[128,1,128]{2,1,0:T(1,128)S(1)} %bitcast.29), channel_id=1, replica_groups=mesh['x'=4,'z'=8,'y'=4,'c'=2] {'x','y','z'}, dimensions={0} | all-to-all | bytes 131072 | tf_op jit(solution)/shard_map/all_to_all | solution.py:324
  (98 shorter events, 28.6 us)
Async XLA Ops:
  0.6 22.7 %collective-permute-start = (bf16[1,7168,192]{1,2,0:T(8,128)(2,1)}, bf16[1,7168,192]{1,2,0:T(8,128)(2,1)}, u32[]{:S(2)}, u32[]{:S(2)}) collective-permute-start(bf16[1,7168,192]{1,2,0:T(8,128)(2,1)} %param.13), channel_id=1, source_target_pairs={{0,1},{1,0},{2,3},{3,2},{4,5},{5,4},{6,7},{7,6},{8,9},{9,8},{10,11... | collective-permute-start | bytes 8257544 | tf_op jit(solution)/shard_map/ppermute | solution.py:27
  0.7 22.6 %collective-permute-start.1 = (bf16[1,7168,192]{1,2,0:T(8,128)(2,1)}, bf16[1,7168,192]{1,2,0:T(8,128)(2,1)}, u32[]{:S(2)}, u32[]{:S(2)}) collective-permute-start(bf16[1,7168,192]{1,2,0:T(8,128)(2,1)} %param.14), channel_id=1, source_target_pairs={{0,1},{1,0},{2,3},{3,2},{4,5},{5,4},{6,7},{7,6},{8,9},{9,8},{10,11... | collective-permute-start | bytes 8257544 | tf_op jit(solution)/shard_map/ppermute | solution.py:27
  1.2 33.7 %collective-permute-start.5 = (bf16[1,192,7168]{2,1,0:T(8,128)(2,1)}, bf16[1,192,7168]{2,1,0:T(8,128)(2,1)}, u32[]{:S(2)}, u32[]{:S(2)}) collective-permute-start(bf16[1,192,7168]{2,1,0:T(8,128)(2,1)} %param.15), channel_id=1, source_target_pairs={{0,1},{1,0},{2,3},{3,2},{4,5},{5,4},{6,7},{7,6},{8,9},{9,8},{10,11... | collective-permute-start | bytes 8257544 | tf_op jit(solution)/shard_map/ppermute | solution.py:27
  3.0 20.2 %all-to-all-start = ((bf16[8,2,7296]{2,1,0:T(2,128)(2,1)}), bf16[8,2,7296]{2,1,0:T(2,128)(2,1)S(1)}, u32[]{:S(2)}, u32[]{:S(2)}) async-start(bf16[8,2,7296]{2,1,0:T(2,128)(2,1)} %spread.1), calls=%async_computation | async-start | bytes 466944 | tf_op jit(solution)/shard_map/all_to_all | solution.py:43
  11.5 33.6 %collective-permute-start.8 = (bf16[7168,256]{1,0:T(8,128)(2,1)}, bf16[7168,256]{1,0:T(8,128)(2,1)}, u32[]{:S(2)}, u32[]{:S(2)}) collective-permute-start(bf16[7168,256]{1,0:T(8,128)(2,1)} %param.17), channel_id=1, source_target_pairs={{0,1},{1,0},{2,3},{3,2},{4,5},{5,4},{6,7},{7,6},{8,9},{9,8},{10,11... | collective-permute-start | bytes 11010056 | tf_op jit(solution)/shard_map/ppermute | solution.py:27
  23.3 11.6 %collective-permute-start.4 = (bf16[16,7296]{1,0:T(8,128)(2,1)S(1)}, bf16[16,7296]{1,0:T(8,128)(2,1)S(1)}, u32[]{:S(2)}, u32[]{:S(2)}) collective-permute-start(bf16[16,7296]{1,0:T(8,128)(2,1)S(1)} %reshape.40), channel_id=1, source_target_pairs={{0,128},{1,5},{2,130},{3,7},{4,132},{5,1},{6,134},{7,3},{64,192},{... | collective-permute-start | bytes 700424 | tf_op jit(solution)/shard_map/ppermute | solution.py:23
  26.4 8.5 %collective-permute-start.3 = (bf16[16,7296]{1,0:T(8,128)(2,1)S(1)}, bf16[16,7296]{1,0:T(8,128)(2,1)S(1)}, u32[]{:S(2)}, u32[]{:S(2)}) collective-permute-start(bf16[16,7296]{1,0:T(8,128)(2,1)S(1)} %reshape.40), channel_id=1, source_target_pairs={{0,192},{1,7},{2,194},{3,1},{4,196},{5,3},{6,198},{7,5},{64,0},{65... | collective-permute-start | bytes 700424 | tf_op jit(solution)/shard_map/ppermute | solution.py:23
  27.6 7.3 %collective-permute-start.2 = (bf16[16,7296]{1,0:T(8,128)(2,1)S(1)}, bf16[16,7296]{1,0:T(8,128)(2,1)S(1)}, u32[]{:S(2)}, u32[]{:S(2)}) collective-permute-start(bf16[16,7296]{1,0:T(8,128)(2,1)S(1)} %reshape.40), channel_id=1, source_target_pairs={{0,64},{1,3},{2,66},{3,5},{4,68},{5,7},{6,70},{7,1},{64,128},{65,6... | collective-permute-start | bytes 700424 | tf_op jit(solution)/shard_map/ppermute | solution.py:23
  35.0 8.6 %collective-permute-start.7 = (bf16[32,7296]{1,0:T(8,128)(2,1)S(1)}, bf16[32,7296]{1,0:T(8,128)(2,1)S(1)}, u32[]{:S(2)}, u32[]{:S(2)}) collective-permute-start(bf16[32,7296]{1,0:T(8,128)(2,1)S(1)} %get-tuple-element.38), channel_id=1, source_target_pairs={{0,6},{1,193},{2,0},{3,195},{4,2},{5,197},{6,4},{7,199},{64,70},{6... | collective-permute-start | bytes 1400840 | tf_op jit(solution)/shard_map/ppermute | solution.py:23
  35.5 9.6 %collective-permute-start.6 = (bf16[32,7296]{1,0:T(8,128)(2,1)S(1)}, bf16[32,7296]{1,0:T(8,128)(2,1)S(1)}, u32[]{:S(2)}, u32[]{:S(2)}) collective-permute-start(bf16[32,7296]{1,0:T(8,128)(2,1)S(1)} %get-tuple-element.39), channel_id=1, source_target_pairs={{0,2},{1,65},{2,4},{3,67},{4,6},{5,69},{6,0},{7,71},{64,66},{65,12... | collective-permute-start | bytes 1400840 | tf_op jit(solution)/shard_map/ppermute | solution.py:23
  39.4 12.0 %collective-permute-start.9 = (bf16[32,7296]{1,0:T(8,128)(2,1)S(1)}, bf16[32,7296]{1,0:T(8,128)(2,1)S(1)}, u32[]{:S(2)}, u32[]{:S(2)}) collective-permute-start(bf16[32,7296]{1,0:T(8,128)(2,1)S(1)} %get-tuple-element.38), channel_id=1, source_target_pairs={{0,2},{1,65},{2,4},{3,67},{4,6},{5,69},{6,0},{7,71},{64,66},{65,12... | collective-permute-start | bytes 1400840 | tf_op jit(solution)/shard_map/ppermute | solution.py:23
  41.1 10.4 %collective-permute-start.10 = (bf16[32,7296]{1,0:T(8,128)(2,1)S(1)}, bf16[32,7296]{1,0:T(8,128)(2,1)S(1)}, u32[]{:S(2)}, u32[]{:S(2)}) collective-permute-start(bf16[32,7296]{1,0:T(8,128)(2,1)S(1)} %get-tuple-element.39), channel_id=1, source_target_pairs={{0,6},{1,193},{2,0},{3,195},{4,2},{5,197},{6,4},{7,199},{64,70},{6... | collective-permute-start | bytes 1400840 | tf_op jit(solution)/shard_map/ppermute | solution.py:23
  45.1 10.0 %collective-permute-start.11 = (bf16[32,7296]{1,0:T(8,128)(2,1)S(1)}, bf16[32,7296]{1,0:T(8,128)(2,1)S(1)}, u32[]{:S(2)}, u32[]{:S(2)}) collective-permute-start(bf16[32,7296]{1,0:T(8,128)(2,1)S(1)} %collective-permute-done.6), channel_id=1, source_target_pairs={{0,2},{1,65},{2,4},{3,67},{4,6},{5,69},{6,0},{7,71},{64,66},{65,12... | collective-permute-start | bytes 1400840 | tf_op jit(solution)/shard_map/ppermute | solution.py:23
  45.7 9.5 %collective-permute-start.12 = (bf16[32,7296]{1,0:T(8,128)(2,1)S(1)}, bf16[32,7296]{1,0:T(8,128)(2,1)S(1)}, u32[]{:S(2)}, u32[]{:S(2)}) collective-permute-start(bf16[32,7296]{1,0:T(8,128)(2,1)S(1)} %collective-permute-done.7), channel_id=1, source_target_pairs={{0,6},{1,193},{2,0},{3,195},{4,2},{5,197},{6,4},{7,199},{64,70},{6... | collective-permute-start | bytes 1400840 | tf_op jit(solution)/shard_map/ppermute | solution.py:23
  62.4 9.8 %collective-permute-start.14 = (bf16[32,7168]{1,0:T(8,128)(2,1)S(1)}, bf16[32,7168]{1,0:T(8,128)(2,1)S(1)}, u32[]{:S(2)}, u32[]{:S(2)}) collective-permute-start(bf16[32,7168]{1,0:T(8,128)(2,1)S(1)} %get-tuple-element.64), channel_id=1, source_target_pairs={{0,2},{1,65},{2,4},{3,67},{4,6},{5,69},{6,0},{7,71},{64,66},{65,12... | collective-permute-start | bytes 1376264 | tf_op jit(solution)/shard_map/ppermute | solution.py:23
  64.8 9.7 %collective-permute-start.13 = (bf16[32,7168]{1,0:T(8,128)(2,1)S(1)}, bf16[32,7168]{1,0:T(8,128)(2,1)S(1)}, u32[]{:S(2)}, u32[]{:S(2)}) collective-permute-start(bf16[32,7168]{1,0:T(8,128)(2,1)S(1)} %get-tuple-element.65), channel_id=1, source_target_pairs={{0,6},{1,193},{2,0},{3,195},{4,2},{5,197},{6,4},{7,199},{64,70},{6... | collective-permute-start | bytes 1376264 | tf_op jit(solution)/shard_map/ppermute | solution.py:23
  65.8 11.3 %collective-permute-start.16 = (bf16[32,7168]{1,0:T(8,128)(2,1)S(1)}, bf16[32,7168]{1,0:T(8,128)(2,1)S(1)}, u32[]{:S(2)}, u32[]{:S(2)}) collective-permute-start(bf16[32,7168]{1,0:T(8,128)(2,1)S(1)} %get-tuple-element.62), channel_id=1, source_target_pairs={{0,2},{1,65},{2,4},{3,67},{4,6},{5,69},{6,0},{7,71},{64,66},{65,12... | collective-permute-start | bytes 1376264 | tf_op jit(solution)/shard_map/ppermute | solution.py:23
  68.0 11.4 %collective-permute-start.18 = (bf16[32,7168]{1,0:T(8,128)(2,1)S(1)}, bf16[32,7168]{1,0:T(8,128)(2,1)S(1)}, u32[]{:S(2)}, u32[]{:S(2)}) collective-permute-start(bf16[32,7168]{1,0:T(8,128)(2,1)S(1)} %get-tuple-element.63), channel_id=1, source_target_pairs={{0,6},{1,193},{2,0},{3,195},{4,2},{5,197},{6,4},{7,199},{64,70},{6... | collective-permute-start | bytes 1376264 | tf_op jit(solution)/shard_map/ppermute | solution.py:23
  74.7 9.7 %collective-permute-start.15 = (bf16[32,7168]{1,0:T(8,128)(2,1)S(1)}, bf16[32,7168]{1,0:T(8,128)(2,1)S(1)}, u32[]{:S(2)}, u32[]{:S(2)}) collective-permute-start(bf16[32,7168]{1,0:T(8,128)(2,1)S(1)} %get-tuple-element.47), channel_id=1, source_target_pairs={{0,6},{1,193},{2,0},{3,195},{4,2},{5,197},{6,4},{7,199},{64,70},{6... | collective-permute-start | bytes 1376264 | tf_op jit(solution)/shard_map/ppermute | solution.py:23
  75.7 9.7 %collective-permute-start.19 = (bf16[32,7168]{1,0:T(8,128)(2,1)S(1)}, bf16[32,7168]{1,0:T(8,128)(2,1)S(1)}, u32[]{:S(2)}, u32[]{:S(2)}) collective-permute-start(bf16[32,7168]{1,0:T(8,128)(2,1)S(1)} %get-tuple-element.48), channel_id=1, source_target_pairs={{0,2},{1,65},{2,4},{3,67},{4,6},{5,69},{6,0},{7,71},{64,66},{65,12... | collective-permute-start | bytes 1376264 | tf_op jit(solution)/shard_map/ppermute | solution.py:23
  85.8 6.1 %collective-permute-start.17 = (bf16[16,7168]{1,0:T(8,128)(2,1)S(1)}, bf16[16,7168]{1,0:T(8,128)(2,1)S(1)}, u32[]{:S(2)}, u32[]{:S(2)}) collective-permute-start(bf16[16,7168]{1,0:T(8,128)(2,1)S(1)} %slice.61), channel_id=1, source_target_pairs={{0,192},{1,7},{2,194},{3,1},{4,196},{5,3},{6,198},{7,5},{64,0},{65... | collective-permute-start | bytes 688136 | tf_op jit(solution)/shard_map/ppermute | solution.py:23
  87.2 7.2 %collective-permute-start.20 = (bf16[16,7168]{1,0:T(8,128)(2,1)S(1)}, bf16[16,7168]{1,0:T(8,128)(2,1)S(1)}, u32[]{:S(2)}, u32[]{:S(2)}) collective-permute-start(bf16[16,7168]{1,0:T(8,128)(2,1)S(1)} %get-tuple-element.68), channel_id=1, source_target_pairs={{0,64},{1,3},{2,66},{3,5},{4,68},{5,7},{6,70},{7,1},{64,128},{65,6... | collective-permute-start | bytes 688136 | tf_op jit(solution)/shard_map/ppermute | solution.py:23
  87.9 9.0 %collective-permute-start.21 = (bf16[16,7168]{1,0:T(8,128)(2,1)S(1)}, bf16[16,7168]{1,0:T(8,128)(2,1)S(1)}, u32[]{:S(2)}, u32[]{:S(2)}) collective-permute-start(bf16[16,7168]{1,0:T(8,128)(2,1)S(1)} %get-tuple-element.69), channel_id=1, source_target_pairs={{0,128},{1,5},{2,130},{3,7},{4,132},{5,1},{6,134},{7,3},{64,192},{... | collective-permute-start | bytes 688136 | tf_op jit(solution)/shard_map/ppermute | solution.py:23
  124.7 13.8 %collective-permute-start.24 = (bf16[16,7168]{1,0:T(8,128)(2,1)S(1)}, bf16[16,7168]{1,0:T(8,128)(2,1)S(1)}, u32[]{:S(2)}, u32[]{:S(2)}) collective-permute-start(bf16[16,7168]{1,0:T(8,128)(2,1)S(1)} %reshape.42), channel_id=1, source_target_pairs={{0,128},{1,5},{2,130},{3,7},{4,132},{5,1},{6,134},{7,3},{64,192},{... | collective-permute-start | bytes 688136 | tf_op jit(solution)/shard_map/ppermute | solution.py:23
  126.0 12.4 %collective-permute-start.23 = (bf16[16,7168]{1,0:T(8,128)(2,1)S(1)}, bf16[16,7168]{1,0:T(8,128)(2,1)S(1)}, u32[]{:S(2)}, u32[]{:S(2)}) collective-permute-start(bf16[16,7168]{1,0:T(8,128)(2,1)S(1)} %reshape.42), channel_id=1, source_target_pairs={{0,192},{1,7},{2,194},{3,1},{4,196},{5,3},{6,198},{7,5},{64,0},{65... | collective-permute-start | bytes 688136 | tf_op jit(solution)/shard_map/ppermute | solution.py:23
  127.0 11.4 %collective-permute-start.22 = (bf16[16,7168]{1,0:T(8,128)(2,1)S(1)}, bf16[16,7168]{1,0:T(8,128)(2,1)S(1)}, u32[]{:S(2)}, u32[]{:S(2)}) collective-permute-start(bf16[16,7168]{1,0:T(8,128)(2,1)S(1)} %reshape.42), channel_id=1, source_target_pairs={{0,64},{1,3},{2,66},{3,5},{4,68},{5,7},{6,70},{7,1},{64,128},{65,6... | collective-permute-start | bytes 688136 | tf_op jit(solution)/shard_map/ppermute | solution.py:23
  138.5 12.2 %collective-permute-start.26 = (bf16[32,7168]{1,0:T(8,128)(2,1)S(1)}, bf16[32,7168]{1,0:T(8,128)(2,1)S(1)}, u32[]{:S(2)}, u32[]{:S(2)}) collective-permute-start(bf16[32,7168]{1,0:T(8,128)(2,1)S(1)} %get-tuple-element.53), channel_id=1, source_target_pairs={{0,6},{1,193},{2,0},{3,195},{4,2},{5,197},{6,4},{7,199},{64,70},{6... | collective-permute-start | bytes 1376264 | tf_op jit(solution)/shard_map/ppermute | solution.py:23
  144.8 8.5 %collective-permute-start.25 = (bf16[32,7168]{1,0:T(8,128)(2,1)S(1)}, bf16[32,7168]{1,0:T(8,128)(2,1)S(1)}, u32[]{:S(2)}, u32[]{:S(2)}) collective-permute-start(bf16[32,7168]{1,0:T(8,128)(2,1)S(1)} %get-tuple-element.54), channel_id=1, source_target_pairs={{0,2},{1,65},{2,4},{3,67},{4,6},{5,69},{6,0},{7,71},{64,66},{65,12... | collective-permute-start | bytes 1376264 | tf_op jit(solution)/shard_map/ppermute | solution.py:23
  146.9 11.3 %collective-permute-start.27 = (bf16[32,7168]{1,0:T(8,128)(2,1)S(1)}, bf16[32,7168]{1,0:T(8,128)(2,1)S(1)}, u32[]{:S(2)}, u32[]{:S(2)}) collective-permute-start(bf16[32,7168]{1,0:T(8,128)(2,1)S(1)} %get-tuple-element.53), channel_id=1, source_target_pairs={{0,2},{1,65},{2,4},{3,67},{4,6},{5,69},{6,0},{7,71},{64,66},{65,12... | collective-permute-start | bytes 1376264 | tf_op jit(solution)/shard_map/ppermute | solution.py:23
  146.9 11.3 %collective-permute-start.28 = (bf16[32,7168]{1,0:T(8,128)(2,1)S(1)}, bf16[32,7168]{1,0:T(8,128)(2,1)S(1)}, u32[]{:S(2)}, u32[]{:S(2)}) collective-permute-start(bf16[32,7168]{1,0:T(8,128)(2,1)S(1)} %get-tuple-element.54), channel_id=1, source_target_pairs={{0,6},{1,193},{2,0},{3,195},{4,2},{5,197},{6,4},{7,199},{64,70},{6... | collective-permute-start | bytes 1376264 | tf_op jit(solution)/shard_map/ppermute | solution.py:23
  153.3 9.9 %collective-permute-start.29 = (bf16[32,7168]{1,0:T(8,128)(2,1)S(1)}, bf16[32,7168]{1,0:T(8,128)(2,1)S(1)}, u32[]{:S(2)}, u32[]{:S(2)}) collective-permute-start(bf16[32,7168]{1,0:T(8,128)(2,1)S(1)} %collective-permute-done.25), channel_id=1, source_target_pairs={{0,2},{1,65},{2,4},{3,67},{4,6},{5,69},{6,0},{7,71},{64,66},{65,12... | collective-permute-start | bytes 1376264 | tf_op jit(solution)/shard_map/ppermute | solution.py:23
  153.3 9.9 %collective-permute-start.30 = (bf16[32,7168]{1,0:T(8,128)(2,1)S(1)}, bf16[32,7168]{1,0:T(8,128)(2,1)S(1)}, u32[]{:S(2)}, u32[]{:S(2)}) collective-permute-start(bf16[32,7168]{1,0:T(8,128)(2,1)S(1)} %collective-permute-done.26), channel_id=1, source_target_pairs={{0,6},{1,193},{2,0},{3,195},{4,2},{5,197},{6,4},{7,199},{64,70},{6... | collective-permute-start | bytes 1376264 | tf_op jit(solution)/shard_map/ppermute | solution.py:23
  (7 other events, 184.3 us)

commit v3 on v2

--- a/solution.py
+++ b/solution.py
@@ -82,7 +82,8 @@
 def fold_first_axis(partial):
     rows = partial.shape[0] // 4
     own, up, down, far = (partial[i * rows : (i + 1) * rows] for i in range(4))
-    return narrow(own, move(up, -1, 0), move(down, 1, 0), move(far, 2, 0))
+    far = together(move(far, 2, 0))[0]
+    return narrow(own, move(up, -1, 0), move(down, 1, 0), far)
 
 
 def fold_column(partial):
@@ -153,7 +154,7 @@
 
 def expert_kernel(expert_ref, row_ref, in_ref, down_ref, out_ref, meta_ref, inner, active):
     width, units = down_ref.shape[1], down_ref.shape[0]
-    part = 128 * 3
+    part = 256
     for start in range(0, 2 * units, part):
         inner[:, start : start + part] = lax.dot_general(
             row_ref[:, :width],
@@ -205,7 +206,8 @@
     )(expert, rows, in_weight, out_weight)
 
 
-def stats_kernel(place_ref, own_ref, other_ref, meta_ref, out_ref, stats):
+def stats_kernel(place_ref, own_ref, other_ref, meta_ref, *refs):
+    out_ref, stats = refs[-2:]
     rows = own_ref.shape[0]
     lane = lax.broadcasted_iota(jnp.int32, (rows, META), 1)
     meta = meta_ref[...]
@@ -237,31 +239,32 @@
     total = jnp.sum(pltpu.roll(scale, 1, 1) * stats, axis=0, keepdims=True)
     picked = jnp.sum(stats, axis=0, keepdims=True)
     result = pltpu.roll(picked, META - 2, 1) - top - jnp.log(pltpu.roll(total, META - 1, 1))
-    out_ref[...] = jnp.where((lane == 0) | (lane == 4), result, 0.0)
+    for index in range(2):
+        out_ref[index] = jnp.sum(jnp.where(lane == 4 * index, result, 0.0))
 
 
 def combine(stats):
     return pl.pallas_call(
         combine_kernel,
-        out_shape=jax.ShapeDtypeStruct((1, META), jnp.float32),
+        out_shape=jax.ShapeDtypeStruct((2,), jnp.float32),
         in_specs=[VMEM],
-        out_specs=VMEM,
+        out_specs=SMEM,
         compiler_params=pltpu.CompilerParams(vmem_limit_bytes=4 * 2**20),
         name="combine",
     )(stats)
 
 
-def row_stats(own, other, meta, place):
+def row_stats(own, other, meta, place, *signs):
     rows = own.shape[0]
     return pl.pallas_call(
         stats_kernel,
         out_shape=jax.ShapeDtypeStruct((rows // 2, META), jnp.float32),
-        in_specs=[SMEM, VMEM, VMEM, VMEM],
+        in_specs=[SMEM, VMEM, VMEM, VMEM] + [ANY] * len(signs),
         out_specs=VMEM,
         scratch_shapes=[pltpu.VMEM((rows, META), jnp.float32)],
         compiler_params=pltpu.CompilerParams(vmem_limit_bytes=8 * 2**20),
         name="row_stats",
-    )(place, own, other, meta)
+    )(place, own, other, meta, *signs)
 
 
 def shards(
@@ -309,6 +312,7 @@
     )
     in_weight = stage(expert_gate[0].T, gate[0].T, expert_up[0].T, up[0].T)
     partial, meta = expert_layer(rows, in_weight, out_weight, expert)
+    partial, first_sign = together(partial, swap(meta))
     folded = fold_second_axis(partial)
     moe = fold_column(fold_first_axis(folded))
 
@@ -318,11 +322,12 @@
     normed = (widened * inverse * norm_gain).astype(jnp.bfloat16)
 
     column = column_rows(jnp.broadcast_to(normed[None], (depth,) + normed.shape))
+    column, second_sign = together(column, swap(column))
     wide, head = first_axis_rows(column, head)
     every, head = second_axis_rows(wide, stage(head))
-    stats = row_stats(product(every, head_weight), product(every, head), meta, place)
+    stats = row_stats(product(every, head_weight), product(every, head), meta, place, first_sign, second_sign)
     arrived = lax.all_to_all(stats, ("x", "y", "z"), 0, 0, tiled=True)
-    logprob = combine(arrived)[0, 0:8:4]
+    logprob = combine(arrived)
     return (logprob, hidden)
 
 

time: 187 us -> 180 us (0.963)
  starting transfers between devices: 49.1 us -> 45.9 us
    ppermute x27, waiting for transfers between devices: 56.1 us -> 51.9 us  [move(): return lax.ppermute(value, PLANE, pairs)]
    ppermute x27, starting transfers between devices: 39.9 us -> 36.3 us  [move(): return lax.ppermute(value, PLANE, pairs)]
    ppermute x4 -> x6, waiting for transfers between devices: 0.01 us -> 2.82 us  [swap(): return lax.ppermute(value, 'c', [(0, 1), (1, 0)])]
  transfers between devices with their start and end apart: 32 -> 34, of which waited for: 19 -> 21; matrix products, arithmetic and copies ran while one was open for 1% -> 1% of each run, Pallas kernels for 5% -> 5%
where the time goes in v3:
time: 180 us; the launch traced here: 179 us
  waiting for transfers between devices  65.4 us (36%)
  starting transfers between devices  45.9 us (26%)
  blocking collectives  44 us (24%)
  Pallas kernels  17 us (9%)
  matrix products  2.22 us (1%)
  other arithmetic  2.04 us (1%)
    ppermute x27, waiting for transfers between devices, move(): return lax.ppermute(value, PLANE, pairs)  51.9 us
    ppermute x27, starting transfers between devices, move(): return lax.ppermute(value, PLANE, pairs)  36.3 us
    all_to_all x1, blocking collectives, shards(): arrived = lax.all_to_all(stats, ('x', 'y', 'z'), 0, 0, tiled=True)  19 us
    all_to_all x1, blocking collectives, column_rows(): lax.all_to_all(spread, 'z', 0, 0, tiled=True).reshape(depth * rows, width)  12.5 us
    all_to_all x1, blocking collectives, fold_column(): lax.all_to_all(partial.reshape(depth, 2, width), 'z', 0, 0, tiled=True)  12.5 us
    all_to_all x1, waiting for transfers between devices, column_rows(): lax.all_to_all(spread, 'z', 0, 0, tiled=True).reshape(depth * rows, width)  10.6 us
    all_to_all x1, starting transfers between devices, column_rows(): lax.all_to_all(spread, 'z', 0, 0, tiled=True).reshape(depth * rows, width)  8.47 us
    pallas_call x3, Pallas kernels, stage(): pl.pallas_call(stage_kernel, out_shape=pltpu.VMEM(shape, weights[0].dtype...  7.43 us
  transfers between devices with their start and end apart: 34, of which 21 were waited for; matrix products, arithmetic and copies ran while one was open for 1% of the time, Pallas kernels for 5%

profile of v3, /device:TPU:8, one launch (start us, length us, event | category | flops | bytes accessed | tf_op | source)
XLA Modules:
  0.0 179.3 jit_solution(17463138707354752567)
XLA Ops:
  1.3 1.7 spread.1
  3.0 8.5 %all-to-all-start = ((bf16[8,2,7296]{2,1,0:T(2,128)(2,1)}), bf16[8,2,7296]{2,1,0:T(2,128)(2,1)S(1)}, u32[]{:S(2)}, u32[]{:S(2)}) async-start(bf16[8,2,7296]{2,1,0:T(2,128)(2,1)} %spread.1), calls=%async_computation | async-start | bytes 466944 | tf_op jit(solution)/shard_map/all_to_all | solution.py:43
  12.6 10.6 %all-to-all-done = bf16[8,2,7296]{2,1,0:T(2,128)(2,1)S(1)} async-done(((bf16[8,2,7296]{2,1,0:T(2,128)(2,1)}), bf16[8,2,7296]{2,1,0:T(2,128)(2,1)S(1)}, u32[]{:S(2)}, u32[]{:S(2)}) %all-to-all-start) | async-done | bytes 233504 | tf_op jit(solution)/shard_map/all_to_all | solution.py:43
  23.3 3.1 %collective-permute-start.4 = (bf16[16,7296]{1,0:T(8,128)(2,1)S(1)}, bf16[16,7296]{1,0:T(8,128)(2,1)S(1)}, u32[]{:S(2)}, u32[]{:S(2)}) collective-permute-start(bf16[16,7296]{1,0:T(8,128)(2,1)S(1)} %reshape.40), channel_id=1, source_target_pairs={{0,128},{1,5},{2,130},{3,7},{4,132},{5,1},{6,134},{7,3},{64,192},{... | collective-permute-start | bytes 700424 | tf_op jit(solution)/shard_map/ppermute | solution.py:23
  28.5 6.4 %collective-permute-done.2 = bf16[16,7296]{1,0:T(8,128)(2,1)S(1)} collective-permute-done((bf16[16,7296]{1,0:T(8,128)(2,1)S(1)}, bf16[16,7296]{1,0:T(8,128)(2,1)S(1)}, u32[]{:S(2)}, u32[]{:S(2)}) %collective-permute-start.2) | collective-permute-done | bytes 233504 | tf_op jit(solution)/shard_map/ppermute | solution.py:23
  37.1 2.3 %stage.3.down_ref = bf16[384,7168]{1,0:T(8,128)(2,1)S(1)} custom-call(bf16[192,7168]{1,0:T(8,128)(2,1)S(1)} %bitcast.25, bf16[192,7168]{1,0:T(8,128)(2,1)} %bitcast.4.refs_1_), custom_call_target="tpu_custom_call" | custom-call | bytes 11010048 | tf_op jit(solution)/shard_map/stage/pallas_call | solution.py:141
  39.4 1.7 collective-permute-start.9
  41.5 2.1 %collective-permute-done.7 = bf16[32,7296]{1,0:T(8,128)(2,1)S(1)} collective-permute-done((bf16[32,7296]{1,0:T(8,128)(2,1)S(1)}, bf16[32,7296]{1,0:T(8,128)(2,1)S(1)}, u32[]{:S(2)}, u32[]{:S(2)}) %collective-permute-start.7) | collective-permute-done | bytes 466976 | tf_op jit(solution)/shard_map/ppermute | solution.py:23
  45.7 2.7 %collective-permute-start.12 = (bf16[32,7296]{1,0:T(8,128)(2,1)S(1)}, bf16[32,7296]{1,0:T(8,128)(2,1)S(1)}, u32[]{:S(2)}, u32[]{:S(2)}) collective-permute-start(bf16[32,7296]{1,0:T(8,128)(2,1)S(1)} %collective-permute-done.7), channel_id=1, source_target_pairs={{0,6},{1,193},{2,0},{3,195},{4,2},{5,197},{6,4},{7,199},{64,70},{6... | collective-permute-start | bytes 1400840 | tf_op jit(solution)/shard_map/ppermute | solution.py:23
  48.4 3.1 %stage.4.in_ref = bf16[768,7168]{1,0:T(8,128)(2,1)S(1)} custom-call(bf16[192,7168]{1,0:T(8,128)(2,1)S(1)} %bitcast.26, bf16[192,7168]{1,0:T(8,128)(2,1)} %bitcast.8.refs_1_, bf16[192,7168]{1,0:T(8,128)(2,1)S(1)} %bitcast.27, bf16[192,7168]{1,0:T(8,128)(2,1)} %bitcast.12.refs_3_), custom_call_target="tpu_custom_call" | custom-call | bytes 22020096 | tf_op jit(solution)/shard_map/stage/pallas_call | solution.py:141
  51.6 3.5 %collective-permute-done.11 = bf16[32,7296]{1,0:T(8,128)(2,1)S(1)} collective-permute-done((bf16[32,7296]{1,0:T(8,128)(2,1)S(1)}, bf16[32,7296]{1,0:T(8,128)(2,1)S(1)}, u32[]{:S(2)}, u32[]{:S(2)}) %collective-permute-start.11) | collective-permute-done | bytes 466976 | tf_op jit(solution)/shard_map/ppermute | solution.py:23
  55.2 6.1 %expert.1 = (bf16[256,7168]{1,0:T(8,128)(2,1)S(1)}, f32[256,128]{1,0:T(8,128)S(1)}) custom-call(s32[1]{0:T(128)} %bitcast.2.expert_ref, bf16[256,7296]{1,0:T(8,128)(2,1)S(1)} %constant_dynamic-update-slice_fusion.4.row_ref, bf16[768,7168]{1,0:T(8,128)(2,1)S(1)} %stage.4.in_ref, bf16[384,7168]{1,0:T(8,128)(2,1)S(1)} %stage.3.down_ref), custom_call_target="tpu_custom_call" | custom-call | flops 4227858432 | bytes 23855104 | tf_op jit(solution)/shard_map/expert/pallas_call | solution.py:187
  62.9 2.4 %collective-permute-start.15 = (bf16[32,7168]{1,0:T(8,128)(2,1)S(1)}, bf16[32,7168]{1,0:T(8,128)(2,1)S(1)}, u32[]{:S(2)}, u32[]{:S(2)}) collective-permute-start(bf16[32,7168]{1,0:T(8,128)(2,1)S(1)} %get-tuple-element.72), channel_id=1, source_target_pairs={{0,2},{1,65},{2,4},{3,67},{4,6},{5,69},{6,0},{7,71},{64,66},{65,12... | collective-permute-start | bytes 1376264 | tf_op jit(solution)/shard_map/ppermute | solution.py:23
  66.3 2.3 %collective-permute-start.17 = (bf16[32,7168]{1,0:T(8,128)(2,1)S(1)}, bf16[32,7168]{1,0:T(8,128)(2,1)S(1)}, u32[]{:S(2)}, u32[]{:S(2)}) collective-permute-start(bf16[32,7168]{1,0:T(8,128)(2,1)S(1)} %get-tuple-element.70), channel_id=1, source_target_pairs={{0,2},{1,65},{2,4},{3,67},{4,6},{5,69},{6,0},{7,71},{64,66},{65,12... | collective-permute-start | bytes 1376264 | tf_op jit(solution)/shard_map/ppermute | solution.py:23
  69.5 3.2 %collective-permute-done.15 = bf16[32,7168]{1,0:T(8,128)(2,1)S(1)} collective-permute-done((bf16[32,7168]{1,0:T(8,128)(2,1)S(1)}, bf16[32,7168]{1,0:T(8,128)(2,1)S(1)}, u32[]{:S(2)}, u32[]{:S(2)}) %collective-permute-start.15) | collective-permute-done | bytes 458784 | tf_op jit(solution)/shard_map/ppermute | solution.py:23
  72.7 2.3 %collective-permute-done.14 = bf16[32,7168]{1,0:T(8,128)(2,1)S(1)} collective-permute-done((bf16[32,7168]{1,0:T(8,128)(2,1)S(1)}, bf16[32,7168]{1,0:T(8,128)(2,1)S(1)}, u32[]{:S(2)}, u32[]{:S(2)}) %collective-permute-start.14) | collective-permute-done | bytes 458784 | tf_op jit(solution)/shard_map/ppermute | solution.py:23
  77.6 2.3 %collective-permute-done.19 = bf16[32,7168]{1,0:T(8,128)(2,1)S(1)} collective-permute-done((bf16[32,7168]{1,0:T(8,128)(2,1)S(1)}, bf16[32,7168]{1,0:T(8,128)(2,1)S(1)}, u32[]{:S(2)}, u32[]{:S(2)}) %collective-permute-start.19) | collective-permute-done | bytes 458784 | tf_op jit(solution)/shard_map/ppermute | solution.py:23
  80.0 4.9 %collective-permute-done.16 = bf16[32,7168]{1,0:T(8,128)(2,1)S(1)} collective-permute-done((bf16[32,7168]{1,0:T(8,128)(2,1)S(1)}, bf16[32,7168]{1,0:T(8,128)(2,1)S(1)}, u32[]{:S(2)}, u32[]{:S(2)}) %collective-permute-start.16) | collective-permute-done | bytes 458784 | tf_op jit(solution)/shard_map/ppermute | solution.py:23
  86.3 1.7 collective-permute-start.22
  90.1 3.8 %collective-permute-done.22 = bf16[16,7168]{1,0:T(8,128)(2,1)S(1)} collective-permute-done((bf16[16,7168]{1,0:T(8,128)(2,1)S(1)}, bf16[16,7168]{1,0:T(8,128)(2,1)S(1)}, u32[]{:S(2)}, u32[]{:S(2)}) %collective-permute-start.22) | collective-permute-done | bytes 229408 | tf_op jit(solution)/shard_map/ppermute | solution.py:23
  96.7 12.5 %all_to_all.26 = bf16[8,2,7168]{2,1,0:T(2,128)(2,1)S(1)} all-to-all(bf16[8,2,7168]{2,1,0:T(2,128)(2,1)S(1)} %reshape.41), channel_id=1, replica_groups=mesh['x'=4,'z'=8,'y'=4,'c'=2] {'z'}, dimensions={0} | all-to-all | bytes 458752 | tf_op jit(solution)/shard_map/all_to_all | solution.py:91
  109.9 12.5 %all_to_all.27 = bf16[8,2,7168]{2,1,0:T(2,128)(2,1)S(1)} all-to-all(bf16[8,2,7168]{2,1,0:T(2,128)(2,1)S(1)} %broadcast_in_dim.52), channel_id=1, replica_groups=mesh['x'=4,'z'=8,'y'=4,'c'=2] {'z'}, dimensions={0} | all-to-all | bytes 458752 | tf_op jit(solution)/shard_map/all_to_all | solution.py:43
  127.9 6.3 %collective-permute-done.24 = bf16[16,7168]{1,0:T(8,128)(2,1)S(1)} collective-permute-done((bf16[16,7168]{1,0:T(8,128)(2,1)S(1)}, bf16[16,7168]{1,0:T(8,128)(2,1)S(1)}, u32[]{:S(2)}, u32[]{:S(2)}) %collective-permute-start.24) | collective-permute-done | bytes 229408 | tf_op jit(solution)/shard_map/ppermute | solution.py:23
  134.4 3.3 %collective-permute-start.28 = (bf16[32,7168]{1,0:T(8,128)(2,1)S(1)}, bf16[32,7168]{1,0:T(8,128)(2,1)S(1)}, u32[]{:S(2)}, u32[]{:S(2)}) collective-permute-start(bf16[32,7168]{1,0:T(8,128)(2,1)S(1)} %get-tuple-element.60), channel_id=1, source_target_pairs={{0,6},{1,193},{2,0},{3,195},{4,2},{5,197},{6,4},{7,199},{64,70},{6... | collective-permute-start | bytes 1376264 | tf_op jit(solution)/shard_map/ppermute | solution.py:23
  137.7 2.0 %stage.5 = bf16[7168,256]{1,0:T(8,128)(2,1)S(1)} custom-call(bf16[7168,256]{1,0:T(8,128)(2,1)} %collective-permute-done.8.refs_0_), custom_call_target="tpu_custom_call" | custom-call | bytes 7340032 | tf_op jit(solution)/shard_map/stage/pallas_call | solution.py:141
  140.3 1.7 collective-permute-start.30
  142.0 1.7 collective-permute-done.28
  143.7 2.5 %collective-permute-done.27 = bf16[32,7168]{1,0:T(8,128)(2,1)S(1)} collective-permute-done((bf16[32,7168]{1,0:T(8,128)(2,1)S(1)}, bf16[32,7168]{1,0:T(8,128)(2,1)S(1)}, u32[]{:S(2)}, u32[]{:S(2)}) %collective-permute-start.27) | collective-permute-done | bytes 458784 | tf_op jit(solution)/shard_map/ppermute | solution.py:23
  146.2 2.1 %collective-permute-start.32 = (bf16[32,7168]{1,0:T(8,128)(2,1)S(1)}, bf16[32,7168]{1,0:T(8,128)(2,1)S(1)}, u32[]{:S(2)}, u32[]{:S(2)}) collective-permute-start(bf16[32,7168]{1,0:T(8,128)(2,1)S(1)} %collective-permute-done.28), channel_id=1, source_target_pairs={{0,6},{1,193},{2,0},{3,195},{4,2},{5,197},{6,4},{7,199},{64,70},{6... | collective-permute-start | bytes 1376264 | tf_op jit(solution)/shard_map/ppermute | solution.py:23
  148.4 2.8 %collective-permute-done.29 = bf16[32,7168]{1,0:T(8,128)(2,1)S(1)} collective-permute-done((bf16[32,7168]{1,0:T(8,128)(2,1)S(1)}, bf16[32,7168]{1,0:T(8,128)(2,1)S(1)}, u32[]{:S(2)}, u32[]{:S(2)}) %collective-permute-start.29) | collective-permute-done | bytes 458784 | tf_op jit(solution)/shard_map/ppermute | solution.py:23
  151.2 4.8 %collective-permute-done.31 = bf16[32,7168]{1,0:T(8,128)(2,1)S(1)} collective-permute-done((bf16[32,7168]{1,0:T(8,128)(2,1)S(1)}, bf16[32,7168]{1,0:T(8,128)(2,1)S(1)}, u32[]{:S(2)}, u32[]{:S(2)}) %collective-permute-start.31) | collective-permute-done | bytes 458784 | tf_op jit(solution)/shard_map/ppermute | solution.py:23
  159.4 19.0 %all_to_all.28 = f32[128,1,128]{2,1,0:T(1,128)S(1)} all-to-all(f32[128,1,128]{2,1,0:T(1,128)S(1)} %bitcast.29), channel_id=1, replica_groups=mesh['x'=4,'z'=8,'y'=4,'c'=2] {'x','y','z'}, dimensions={0} | all-to-all | bytes 131072 | tf_op jit(solution)/shard_map/all_to_all | solution.py:329
  (101 shorter events, 32.0 us)
Async XLA Ops:
  0.6 22.7 %collective-permute-start = (bf16[1,7168,192]{1,2,0:T(8,128)(2,1)}, bf16[1,7168,192]{1,2,0:T(8,128)(2,1)}, u32[]{:S(2)}, u32[]{:S(2)}) collective-permute-start(bf16[1,7168,192]{1,2,0:T(8,128)(2,1)} %param.13), channel_id=1, source_target_pairs={{0,1},{1,0},{2,3},{3,2},{4,5},{5,4},{6,7},{7,6},{8,9},{9,8},{10,11... | collective-permute-start | bytes 8257544 | tf_op jit(solution)/shard_map/ppermute | solution.py:27
  0.7 22.6 %collective-permute-start.1 = (bf16[1,7168,192]{1,2,0:T(8,128)(2,1)}, bf16[1,7168,192]{1,2,0:T(8,128)(2,1)}, u32[]{:S(2)}, u32[]{:S(2)}) collective-permute-start(bf16[1,7168,192]{1,2,0:T(8,128)(2,1)} %param.14), channel_id=1, source_target_pairs={{0,1},{1,0},{2,3},{3,2},{4,5},{5,4},{6,7},{7,6},{8,9},{9,8},{10,11... | collective-permute-start | bytes 8257544 | tf_op jit(solution)/shard_map/ppermute | solution.py:27
  1.2 33.7 %collective-permute-start.5 = (bf16[1,192,7168]{2,1,0:T(8,128)(2,1)}, bf16[1,192,7168]{2,1,0:T(8,128)(2,1)}, u32[]{:S(2)}, u32[]{:S(2)}) collective-permute-start(bf16[1,192,7168]{2,1,0:T(8,128)(2,1)} %param.15), channel_id=1, source_target_pairs={{0,1},{1,0},{2,3},{3,2},{4,5},{5,4},{6,7},{7,6},{8,9},{9,8},{10,11... | collective-permute-start | bytes 8257544 | tf_op jit(solution)/shard_map/ppermute | solution.py:27
  3.0 20.2 %all-to-all-start = ((bf16[8,2,7296]{2,1,0:T(2,128)(2,1)}), bf16[8,2,7296]{2,1,0:T(2,128)(2,1)S(1)}, u32[]{:S(2)}, u32[]{:S(2)}) async-start(bf16[8,2,7296]{2,1,0:T(2,128)(2,1)} %spread.1), calls=%async_computation | async-start | bytes 466944 | tf_op jit(solution)/shard_map/all_to_all | solution.py:43
  11.5 33.6 %collective-permute-start.8 = (bf16[7168,256]{1,0:T(8,128)(2,1)}, bf16[7168,256]{1,0:T(8,128)(2,1)}, u32[]{:S(2)}, u32[]{:S(2)}) collective-permute-start(bf16[7168,256]{1,0:T(8,128)(2,1)} %param.17), channel_id=1, source_target_pairs={{0,1},{1,0},{2,3},{3,2},{4,5},{5,4},{6,7},{7,6},{8,9},{9,8},{10,11... | collective-permute-start | bytes 11010056 | tf_op jit(solution)/shard_map/ppermute | solution.py:27
  23.3 11.6 %collective-permute-start.4 = (bf16[16,7296]{1,0:T(8,128)(2,1)S(1)}, bf16[16,7296]{1,0:T(8,128)(2,1)S(1)}, u32[]{:S(2)}, u32[]{:S(2)}) collective-permute-start(bf16[16,7296]{1,0:T(8,128)(2,1)S(1)} %reshape.40), channel_id=1, source_target_pairs={{0,128},{1,5},{2,130},{3,7},{4,132},{5,1},{6,134},{7,3},{64,192},{... | collective-permute-start | bytes 700424 | tf_op jit(solution)/shard_map/ppermute | solution.py:23
  26.4 8.5 %collective-permute-start.3 = (bf16[16,7296]{1,0:T(8,128)(2,1)S(1)}, bf16[16,7296]{1,0:T(8,128)(2,1)S(1)}, u32[]{:S(2)}, u32[]{:S(2)}) collective-permute-start(bf16[16,7296]{1,0:T(8,128)(2,1)S(1)} %reshape.40), channel_id=1, source_target_pairs={{0,192},{1,7},{2,194},{3,1},{4,196},{5,3},{6,198},{7,5},{64,0},{65... | collective-permute-start | bytes 700424 | tf_op jit(solution)/shard_map/ppermute | solution.py:23
  27.6 7.3 %collective-permute-start.2 = (bf16[16,7296]{1,0:T(8,128)(2,1)S(1)}, bf16[16,7296]{1,0:T(8,128)(2,1)S(1)}, u32[]{:S(2)}, u32[]{:S(2)}) collective-permute-start(bf16[16,7296]{1,0:T(8,128)(2,1)S(1)} %reshape.40), channel_id=1, source_target_pairs={{0,64},{1,3},{2,66},{3,5},{4,68},{5,7},{6,70},{7,1},{64,128},{65,6... | collective-permute-start | bytes 700424 | tf_op jit(solution)/shard_map/ppermute | solution.py:23
  35.0 8.6 %collective-permute-start.7 = (bf16[32,7296]{1,0:T(8,128)(2,1)S(1)}, bf16[32,7296]{1,0:T(8,128)(2,1)S(1)}, u32[]{:S(2)}, u32[]{:S(2)}) collective-permute-start(bf16[32,7296]{1,0:T(8,128)(2,1)S(1)} %get-tuple-element.42), channel_id=1, source_target_pairs={{0,6},{1,193},{2,0},{3,195},{4,2},{5,197},{6,4},{7,199},{64,70},{6... | collective-permute-start | bytes 1400840 | tf_op jit(solution)/shard_map/ppermute | solution.py:23
  35.5 9.6 %collective-permute-start.6 = (bf16[32,7296]{1,0:T(8,128)(2,1)S(1)}, bf16[32,7296]{1,0:T(8,128)(2,1)S(1)}, u32[]{:S(2)}, u32[]{:S(2)}) collective-permute-start(bf16[32,7296]{1,0:T(8,128)(2,1)S(1)} %get-tuple-element.43), channel_id=1, source_target_pairs={{0,2},{1,65},{2,4},{3,67},{4,6},{5,69},{6,0},{7,71},{64,66},{65,12... | collective-permute-start | bytes 1400840 | tf_op jit(solution)/shard_map/ppermute | solution.py:23
  39.4 12.0 %collective-permute-start.9 = (bf16[32,7296]{1,0:T(8,128)(2,1)S(1)}, bf16[32,7296]{1,0:T(8,128)(2,1)S(1)}, u32[]{:S(2)}, u32[]{:S(2)}) collective-permute-start(bf16[32,7296]{1,0:T(8,128)(2,1)S(1)} %get-tuple-element.42), channel_id=1, source_target_pairs={{0,2},{1,65},{2,4},{3,67},{4,6},{5,69},{6,0},{7,71},{64,66},{65,12... | collective-permute-start | bytes 1400840 | tf_op jit(solution)/shard_map/ppermute | solution.py:23
  41.1 10.4 %collective-permute-start.10 = (bf16[32,7296]{1,0:T(8,128)(2,1)S(1)}, bf16[32,7296]{1,0:T(8,128)(2,1)S(1)}, u32[]{:S(2)}, u32[]{:S(2)}) collective-permute-start(bf16[32,7296]{1,0:T(8,128)(2,1)S(1)} %get-tuple-element.43), channel_id=1, source_target_pairs={{0,6},{1,193},{2,0},{3,195},{4,2},{5,197},{6,4},{7,199},{64,70},{6... | collective-permute-start | bytes 1400840 | tf_op jit(solution)/shard_map/ppermute | solution.py:23
  45.1 10.0 %collective-permute-start.11 = (bf16[32,7296]{1,0:T(8,128)(2,1)S(1)}, bf16[32,7296]{1,0:T(8,128)(2,1)S(1)}, u32[]{:S(2)}, u32[]{:S(2)}) collective-permute-start(bf16[32,7296]{1,0:T(8,128)(2,1)S(1)} %collective-permute-done.6), channel_id=1, source_target_pairs={{0,2},{1,65},{2,4},{3,67},{4,6},{5,69},{6,0},{7,71},{64,66},{65,12... | collective-permute-start | bytes 1400840 | tf_op jit(solution)/shard_map/ppermute | solution.py:23
  45.7 9.5 %collective-permute-start.12 = (bf16[32,7296]{1,0:T(8,128)(2,1)S(1)}, bf16[32,7296]{1,0:T(8,128)(2,1)S(1)}, u32[]{:S(2)}, u32[]{:S(2)}) collective-permute-start(bf16[32,7296]{1,0:T(8,128)(2,1)S(1)} %collective-permute-done.7), channel_id=1, source_target_pairs={{0,6},{1,193},{2,0},{3,195},{4,2},{5,197},{6,4},{7,199},{64,70},{6... | collective-permute-start | bytes 1400840 | tf_op jit(solution)/shard_map/ppermute | solution.py:23
  62.9 9.8 %collective-permute-start.15 = (bf16[32,7168]{1,0:T(8,128)(2,1)S(1)}, bf16[32,7168]{1,0:T(8,128)(2,1)S(1)}, u32[]{:S(2)}, u32[]{:S(2)}) collective-permute-start(bf16[32,7168]{1,0:T(8,128)(2,1)S(1)} %get-tuple-element.72), channel_id=1, source_target_pairs={{0,2},{1,65},{2,4},{3,67},{4,6},{5,69},{6,0},{7,71},{64,66},{65,12... | collective-permute-start | bytes 1376264 | tf_op jit(solution)/shard_map/ppermute | solution.py:23
  65.3 9.7 %collective-permute-start.14 = (bf16[32,7168]{1,0:T(8,128)(2,1)S(1)}, bf16[32,7168]{1,0:T(8,128)(2,1)S(1)}, u32[]{:S(2)}, u32[]{:S(2)}) collective-permute-start(bf16[32,7168]{1,0:T(8,128)(2,1)S(1)} %get-tuple-element.73), channel_id=1, source_target_pairs={{0,6},{1,193},{2,0},{3,195},{4,2},{5,197},{6,4},{7,199},{64,70},{6... | collective-permute-start | bytes 1376264 | tf_op jit(solution)/shard_map/ppermute | solution.py:23
  66.3 11.3 %collective-permute-start.17 = (bf16[32,7168]{1,0:T(8,128)(2,1)S(1)}, bf16[32,7168]{1,0:T(8,128)(2,1)S(1)}, u32[]{:S(2)}, u32[]{:S(2)}) collective-permute-start(bf16[32,7168]{1,0:T(8,128)(2,1)S(1)} %get-tuple-element.70), channel_id=1, source_target_pairs={{0,2},{1,65},{2,4},{3,67},{4,6},{5,69},{6,0},{7,71},{64,66},{65,12... | collective-permute-start | bytes 1376264 | tf_op jit(solution)/shard_map/ppermute | solution.py:23
  68.6 11.4 %collective-permute-start.19 = (bf16[32,7168]{1,0:T(8,128)(2,1)S(1)}, bf16[32,7168]{1,0:T(8,128)(2,1)S(1)}, u32[]{:S(2)}, u32[]{:S(2)}) collective-permute-start(bf16[32,7168]{1,0:T(8,128)(2,1)S(1)} %get-tuple-element.71), channel_id=1, source_target_pairs={{0,6},{1,193},{2,0},{3,195},{4,2},{5,197},{6,4},{7,199},{64,70},{6... | collective-permute-start | bytes 1376264 | tf_op jit(solution)/shard_map/ppermute | solution.py:23
  75.3 9.6 %collective-permute-start.16 = (bf16[32,7168]{1,0:T(8,128)(2,1)S(1)}, bf16[32,7168]{1,0:T(8,128)(2,1)S(1)}, u32[]{:S(2)}, u32[]{:S(2)}) collective-permute-start(bf16[32,7168]{1,0:T(8,128)(2,1)S(1)} %get-tuple-element.53), channel_id=1, source_target_pairs={{0,6},{1,193},{2,0},{3,195},{4,2},{5,197},{6,4},{7,199},{64,70},{6... | collective-permute-start | bytes 1376264 | tf_op jit(solution)/shard_map/ppermute | solution.py:23
  76.2 9.7 %collective-permute-start.20 = (bf16[32,7168]{1,0:T(8,128)(2,1)S(1)}, bf16[32,7168]{1,0:T(8,128)(2,1)S(1)}, u32[]{:S(2)}, u32[]{:S(2)}) collective-permute-start(bf16[32,7168]{1,0:T(8,128)(2,1)S(1)} %get-tuple-element.54), channel_id=1, source_target_pairs={{0,2},{1,65},{2,4},{3,67},{4,6},{5,69},{6,0},{7,71},{64,66},{65,12... | collective-permute-start | bytes 1376264 | tf_op jit(solution)/shard_map/ppermute | solution.py:23
  86.3 7.6 %collective-permute-start.22 = (bf16[16,7168]{1,0:T(8,128)(2,1)S(1)}, bf16[16,7168]{1,0:T(8,128)(2,1)S(1)}, u32[]{:S(2)}, u32[]{:S(2)}) collective-permute-start(bf16[16,7168]{1,0:T(8,128)(2,1)S(1)} %get-tuple-element.77), channel_id=1, source_target_pairs={{0,128},{1,5},{2,130},{3,7},{4,132},{5,1},{6,134},{7,3},{64,192},{... | collective-permute-start | bytes 688136 | tf_op jit(solution)/shard_map/ppermute | solution.py:23
  88.1 7.0 %collective-permute-start.18 = (bf16[16,7168]{1,0:T(8,128)(2,1)S(1)}, bf16[16,7168]{1,0:T(8,128)(2,1)S(1)}, u32[]{:S(2)}, u32[]{:S(2)}) collective-permute-start(bf16[16,7168]{1,0:T(8,128)(2,1)S(1)} %slice.57), channel_id=1, source_target_pairs={{0,192},{1,7},{2,194},{3,1},{4,196},{5,3},{6,198},{7,5},{64,0},{65... | collective-permute-start | bytes 688136 | tf_op jit(solution)/shard_map/ppermute | solution.py:23
  89.3 7.2 %collective-permute-start.21 = (bf16[16,7168]{1,0:T(8,128)(2,1)S(1)}, bf16[16,7168]{1,0:T(8,128)(2,1)S(1)}, u32[]{:S(2)}, u32[]{:S(2)}) collective-permute-start(bf16[16,7168]{1,0:T(8,128)(2,1)S(1)} %get-tuple-element.76), channel_id=1, source_target_pairs={{0,64},{1,3},{2,66},{3,5},{4,68},{5,7},{6,70},{7,1},{64,128},{65,6... | collective-permute-start | bytes 688136 | tf_op jit(solution)/shard_map/ppermute | solution.py:23
  124.3 10.0 %collective-permute-start.26 = (bf16[16,7168]{1,0:T(8,128)(2,1)S(1)}, bf16[16,7168]{1,0:T(8,128)(2,1)S(1)}, u32[]{:S(2)}, u32[]{:S(2)}) collective-permute-start(bf16[16,7168]{1,0:T(8,128)(2,1)S(1)} %reshape.42), channel_id=1, source_target_pairs={{0,128},{1,5},{2,130},{3,7},{4,132},{5,1},{6,134},{7,3},{64,192},{... | collective-permute-start | bytes 688136 | tf_op jit(solution)/shard_map/ppermute | solution.py:23
  125.9 8.5 %collective-permute-start.25 = (bf16[16,7168]{1,0:T(8,128)(2,1)S(1)}, bf16[16,7168]{1,0:T(8,128)(2,1)S(1)}, u32[]{:S(2)}, u32[]{:S(2)}) collective-permute-start(bf16[16,7168]{1,0:T(8,128)(2,1)S(1)} %reshape.42), channel_id=1, source_target_pairs={{0,192},{1,7},{2,194},{3,1},{4,196},{5,3},{6,198},{7,5},{64,0},{65... | collective-permute-start | bytes 688136 | tf_op jit(solution)/shard_map/ppermute | solution.py:23
  127.0 7.2 %collective-permute-start.24 = (bf16[16,7168]{1,0:T(8,128)(2,1)S(1)}, bf16[16,7168]{1,0:T(8,128)(2,1)S(1)}, u32[]{:S(2)}, u32[]{:S(2)}) collective-permute-start(bf16[16,7168]{1,0:T(8,128)(2,1)S(1)} %reshape.42), channel_id=1, source_target_pairs={{0,64},{1,3},{2,66},{3,5},{4,68},{5,7},{6,70},{7,1},{64,128},{65,6... | collective-permute-start | bytes 688136 | tf_op jit(solution)/shard_map/ppermute | solution.py:23
  134.4 9.3 %collective-permute-start.28 = (bf16[32,7168]{1,0:T(8,128)(2,1)S(1)}, bf16[32,7168]{1,0:T(8,128)(2,1)S(1)}, u32[]{:S(2)}, u32[]{:S(2)}) collective-permute-start(bf16[32,7168]{1,0:T(8,128)(2,1)S(1)} %get-tuple-element.60), channel_id=1, source_target_pairs={{0,6},{1,193},{2,0},{3,195},{4,2},{5,197},{6,4},{7,199},{64,70},{6... | collective-permute-start | bytes 1376264 | tf_op jit(solution)/shard_map/ppermute | solution.py:23
  137.7 8.5 %collective-permute-start.27 = (bf16[32,7168]{1,0:T(8,128)(2,1)S(1)}, bf16[32,7168]{1,0:T(8,128)(2,1)S(1)}, u32[]{:S(2)}, u32[]{:S(2)}) collective-permute-start(bf16[32,7168]{1,0:T(8,128)(2,1)S(1)} %get-tuple-element.61), channel_id=1, source_target_pairs={{0,2},{1,65},{2,4},{3,67},{4,6},{5,69},{6,0},{7,71},{64,66},{65,12... | collective-permute-start | bytes 1376264 | tf_op jit(solution)/shard_map/ppermute | solution.py:23
  139.8 11.3 %collective-permute-start.29 = (bf16[32,7168]{1,0:T(8,128)(2,1)S(1)}, bf16[32,7168]{1,0:T(8,128)(2,1)S(1)}, u32[]{:S(2)}, u32[]{:S(2)}) collective-permute-start(bf16[32,7168]{1,0:T(8,128)(2,1)S(1)} %get-tuple-element.60), channel_id=1, source_target_pairs={{0,2},{1,65},{2,4},{3,67},{4,6},{5,69},{6,0},{7,71},{64,66},{65,12... | collective-permute-start | bytes 1376264 | tf_op jit(solution)/shard_map/ppermute | solution.py:23
  140.3 10.9 %collective-permute-start.30 = (bf16[32,7168]{1,0:T(8,128)(2,1)S(1)}, bf16[32,7168]{1,0:T(8,128)(2,1)S(1)}, u32[]{:S(2)}, u32[]{:S(2)}) collective-permute-start(bf16[32,7168]{1,0:T(8,128)(2,1)S(1)} %get-tuple-element.61), channel_id=1, source_target_pairs={{0,6},{1,193},{2,0},{3,195},{4,2},{5,197},{6,4},{7,199},{64,70},{6... | collective-permute-start | bytes 1376264 | tf_op jit(solution)/shard_map/ppermute | solution.py:23
  146.2 9.8 %collective-permute-start.31 = (bf16[32,7168]{1,0:T(8,128)(2,1)S(1)}, bf16[32,7168]{1,0:T(8,128)(2,1)S(1)}, u32[]{:S(2)}, u32[]{:S(2)}) collective-permute-start(bf16[32,7168]{1,0:T(8,128)(2,1)S(1)} %collective-permute-done.27), channel_id=1, source_target_pairs={{0,2},{1,65},{2,4},{3,67},{4,6},{5,69},{6,0},{7,71},{64,66},{65,12... | collective-permute-start | bytes 1376264 | tf_op jit(solution)/shard_map/ppermute | solution.py:23
  146.2 9.9 %collective-permute-start.32 = (bf16[32,7168]{1,0:T(8,128)(2,1)S(1)}, bf16[32,7168]{1,0:T(8,128)(2,1)S(1)}, u32[]{:S(2)}, u32[]{:S(2)}) collective-permute-start(bf16[32,7168]{1,0:T(8,128)(2,1)S(1)} %collective-permute-done.28), channel_id=1, source_target_pairs={{0,6},{1,193},{2,0},{3,195},{4,2},{5,197},{6,4},{7,199},{64,70},{6... | collective-permute-start | bytes 1376264 | tf_op jit(solution)/shard_map/ppermute | solution.py:23
  (9 other events, 177.2 us)

commit v4 on v3

--- a/solution.py
+++ b/solution.py
@@ -152,13 +152,12 @@
     )(*weights)
 
 
-def expert_kernel(expert_ref, row_ref, in_ref, down_ref, out_ref, meta_ref, inner, active):
-    width, units = down_ref.shape[1], down_ref.shape[0]
-    part = 256
-    for start in range(0, 2 * units, part):
-        inner[:, start : start + part] = lax.dot_general(
+def expert_kernel(expert_ref, row_ref, in_ref, active_ref, meta_ref, inner):
+    units, width = active_ref.shape[1], in_ref.shape[1]
+    for start in range(0, 2 * units, 256):
+        inner[:, start : start + 256] = lax.dot_general(
             row_ref[:, :width],
-            in_ref[start : start + part, :],
+            in_ref[start : start + 256, :],
             (((1,), (1,)), ((), ())),
             preferred_element_type=jnp.float32,
         )
@@ -170,40 +169,29 @@
     share = jnp.sum(jnp.where(chosen, gates, 0.0), axis=1, keepdims=True)
     gate = inner[:, :units]
     value = gate / (1.0 + jnp.exp(-gate)) * inner[:, units:] * share
-    active[...] = value.astype(jnp.bfloat16)
-    step = width // 7
-
-    @pl.loop(0, 7)
-    def _(index):
-        span = pl.ds(pl.multiple_of(index * step, step), step)
-        out_ref[:, span] = jnp.dot(
-            active[...], down_ref[:, span], preferred_element_type=jnp.float32
-        ).astype(jnp.bfloat16)
-
-
-def expert_layer(rows, in_weight, out_weight, expert):
+    active_ref[...] = value.astype(jnp.bfloat16)
+
+
+def expert_units(rows, in_weight, expert):
     count = rows.shape[0]
-    units, width = out_weight.shape
+    units, width = in_weight.shape[0] // 2, in_weight.shape[1]
     return pl.pallas_call(
         expert_kernel,
         out_shape=[
-            jax.ShapeDtypeStruct((count, width), jnp.bfloat16),
+            jax.ShapeDtypeStruct((count, units), jnp.bfloat16),
             jax.ShapeDtypeStruct((count, META), jnp.float32),
         ],
-        in_specs=[SMEM, VMEM, VMEM, VMEM],
+        in_specs=[SMEM, VMEM, VMEM],
         out_specs=[VMEM, VMEM],
-        scratch_shapes=[
-            pltpu.VMEM((count, 2 * units), jnp.float32),
-            pltpu.VMEM((count, units), jnp.bfloat16),
-        ],
+        scratch_shapes=[pltpu.VMEM((count, 2 * units), jnp.float32)],
         cost_estimate=pl.CostEstimate(
-            flops=6 * count * units * width,
-            bytes_accessed=2 * (3 * units * width + 2 * count * width),
+            flops=4 * count * units * width,
+            bytes_accessed=4 * units * width + 2 * count * width,
             transcendentals=count * units,
         ),
         compiler_params=pltpu.CompilerParams(vmem_limit_bytes=16 * 2**20),
         name="expert",
-    )(expert, rows, in_weight, out_weight)
+    )(expert, rows, in_weight)
 
 
 def stats_kernel(place_ref, own_ref, other_ref, meta_ref, *refs):
@@ -311,8 +299,8 @@
         wide, stage(expert_down[0], down[0]), gate, up, swap(head_weight)
     )
     in_weight = stage(expert_gate[0].T, gate[0].T, expert_up[0].T, up[0].T)
-    partial, meta = expert_layer(rows, in_weight, out_weight, expert)
-    partial, first_sign = together(partial, swap(meta))
+    active, meta = expert_units(rows, in_weight, expert)
+    partial, first_sign = together(product(active, out_weight).astype(jnp.bfloat16), swap(meta))
     folded = fold_second_axis(partial)
     moe = fold_column(fold_first_axis(folded))
 

time: 180 us -> 178 us (0.989)
  Pallas kernels: 17 us -> 14 us
  matrix products: 2.22 us -> 4.29 us
    pallas_call x1, Pallas kernels: 6.12 us -> 3.05 us  [expert_units(): pl.pallas_call(expert_kernel, out_shape=[jax.ShapeDtypeStruct((count, uni...]
    dot_general x2 -> x3, matrix products: 2.22 us -> 4.29 us  [product(): return jnp.dot(left, right, preferred_element_type=jnp.float32)]
  transfers between devices with their start and end apart: 34 -> 34, of which waited for: 21 -> 20; matrix products, arithmetic and copies ran while one was open for 1% -> 2% of each run, Pallas kernels for 5% -> 5%
where the time goes in v4:
time: 178 us; the launch traced here: 177 us
  waiting for transfers between devices  64 us (36%)
  starting transfers between devices  45.6 us (26%)
  blocking collectives  44.7 us (25%)
  Pallas kernels  14 us (8%)
  matrix products  4.29 us (2%)
  other arithmetic  2.03 us (1%)
    ppermute x27, waiting for transfers between devices, move(): return lax.ppermute(value, PLANE, pairs)  51.9 us
    ppermute x27, starting transfers between devices, move(): return lax.ppermute(value, PLANE, pairs)  36.1 us
    all_to_all x1, blocking collectives, shards(): arrived = lax.all_to_all(stats, ('x', 'y', 'z'), 0, 0, tiled=True)  19.3 us
    all_to_all x1, blocking collectives, fold_column(): lax.all_to_all(partial.reshape(depth, 2, width), 'z', 0, 0, tiled=True)  12.8 us
    all_to_all x1, blocking collectives, column_rows(): lax.all_to_all(spread, 'z', 0, 0, tiled=True).reshape(depth * rows, width)  12.5 us
    all_to_all x1, waiting for transfers between devices, column_rows(): lax.all_to_all(spread, 'z', 0, 0, tiled=True).reshape(depth * rows, width)  10.6 us
    all_to_all x1, starting transfers between devices, column_rows(): lax.all_to_all(spread, 'z', 0, 0, tiled=True).reshape(depth * rows, width)  8.47 us
    pallas_call x3, Pallas kernels, stage(): pl.pallas_call(stage_kernel, out_shape=pltpu.VMEM(shape, weights[0].dtype...  7.43 us
  transfers between devices with their start and end apart: 34, of which 20 were waited for; matrix products, arithmetic and copies ran while one was open for 2% of the time, Pallas kernels for 5%

profile of v4, /device:TPU:8, one launch (start us, length us, event | category | flops | bytes accessed | tf_op | source)
XLA Modules:
  0.0 177.3 jit_solution(14627163607925802011)
XLA Ops:
  1.3 1.7 spread.1
  3.0 8.5 %all-to-all-start = ((bf16[8,2,7296]{2,1,0:T(2,128)(2,1)}), bf16[8,2,7296]{2,1,0:T(2,128)(2,1)S(1)}, u32[]{:S(2)}, u32[]{:S(2)}) async-start(bf16[8,2,7296]{2,1,0:T(2,128)(2,1)} %spread.1), calls=%async_computation | async-start | bytes 466944 | tf_op jit(solution)/shard_map/all_to_all | solution.py:43
  12.6 10.6 %all-to-all-done = bf16[8,2,7296]{2,1,0:T(2,128)(2,1)S(1)} async-done(((bf16[8,2,7296]{2,1,0:T(2,128)(2,1)}), bf16[8,2,7296]{2,1,0:T(2,128)(2,1)S(1)}, u32[]{:S(2)}, u32[]{:S(2)}) %all-to-all-start) | async-done | bytes 233504 | tf_op jit(solution)/shard_map/all_to_all | solution.py:43
  23.3 3.1 %collective-permute-start.4 = (bf16[16,7296]{1,0:T(8,128)(2,1)S(1)}, bf16[16,7296]{1,0:T(8,128)(2,1)S(1)}, u32[]{:S(2)}, u32[]{:S(2)}) collective-permute-start(bf16[16,7296]{1,0:T(8,128)(2,1)S(1)} %reshape.40), channel_id=1, source_target_pairs={{0,128},{1,5},{2,130},{3,7},{4,132},{5,1},{6,134},{7,3},{64,192},{... | collective-permute-start | bytes 700424 | tf_op jit(solution)/shard_map/ppermute | solution.py:23
  28.5 6.4 %collective-permute-done.2 = bf16[16,7296]{1,0:T(8,128)(2,1)S(1)} collective-permute-done((bf16[16,7296]{1,0:T(8,128)(2,1)S(1)}, bf16[16,7296]{1,0:T(8,128)(2,1)S(1)}, u32[]{:S(2)}, u32[]{:S(2)}) %collective-permute-start.2) | collective-permute-done | bytes 233504 | tf_op jit(solution)/shard_map/ppermute | solution.py:23
  37.1 2.3 %stage.3 = bf16[384,7168]{1,0:T(8,128)(2,1)S(1)} custom-call(bf16[192,7168]{1,0:T(8,128)(2,1)S(1)} %bitcast.27, bf16[192,7168]{1,0:T(8,128)(2,1)} %bitcast.4.refs_1_), custom_call_target="tpu_custom_call" | custom-call | bytes 11010048 | tf_op jit(solution)/shard_map/stage/pallas_call | solution.py:141
  39.4 1.7 collective-permute-start.9
  41.5 2.1 %collective-permute-done.7 = bf16[32,7296]{1,0:T(8,128)(2,1)S(1)} collective-permute-done((bf16[32,7296]{1,0:T(8,128)(2,1)S(1)}, bf16[32,7296]{1,0:T(8,128)(2,1)S(1)}, u32[]{:S(2)}, u32[]{:S(2)}) %collective-permute-start.7) | collective-permute-done | bytes 466976 | tf_op jit(solution)/shard_map/ppermute | solution.py:23
  45.7 2.7 %collective-permute-start.12 = (bf16[32,7296]{1,0:T(8,128)(2,1)S(1)}, bf16[32,7296]{1,0:T(8,128)(2,1)S(1)}, u32[]{:S(2)}, u32[]{:S(2)}) collective-permute-start(bf16[32,7296]{1,0:T(8,128)(2,1)S(1)} %collective-permute-done.7), channel_id=1, source_target_pairs={{0,6},{1,193},{2,0},{3,195},{4,2},{5,197},{6,4},{7,199},{64,70},{6... | collective-permute-start | bytes 1400840 | tf_op jit(solution)/shard_map/ppermute | solution.py:23
  48.4 3.1 %stage.4.in_ref = bf16[768,7168]{1,0:T(8,128)(2,1)S(1)} custom-call(bf16[192,7168]{1,0:T(8,128)(2,1)S(1)} %bitcast.28, bf16[192,7168]{1,0:T(8,128)(2,1)} %bitcast.8.refs_1_, bf16[192,7168]{1,0:T(8,128)(2,1)S(1)} %bitcast.29, bf16[192,7168]{1,0:T(8,128)(2,1)} %bitcast.12.refs_3_), custom_call_target="tpu_custom_call" | custom-call | bytes 22020096 | tf_op jit(solution)/shard_map/stage/pallas_call | solution.py:141
  51.6 3.5 %collective-permute-done.11 = bf16[32,7296]{1,0:T(8,128)(2,1)S(1)} collective-permute-done((bf16[32,7296]{1,0:T(8,128)(2,1)S(1)}, bf16[32,7296]{1,0:T(8,128)(2,1)S(1)}, u32[]{:S(2)}, u32[]{:S(2)}) %collective-permute-start.11) | collective-permute-done | bytes 466976 | tf_op jit(solution)/shard_map/ppermute | solution.py:23
  55.2 3.1 %expert.1 = (bf16[256,384]{1,0:T(8,128)(2,1)S(1)}, f32[256,128]{1,0:T(8,128)S(1)}) custom-call(s32[1]{0:T(128)} %bitcast.2.expert_ref, bf16[256,7296]{1,0:T(8,128)(2,1)S(1)} %constant_dynamic-update-slice_fusion.4.row_ref, bf16[768,7168]{1,0:T(8,128)(2,1)S(1)} %stage.4.in_ref), custom_call_target="tpu_custom_call" | custom-call | flops 2818572288 | bytes 14680064 | tf_op jit(solution)/shard_map/expert/pallas_call | solution.py:178
  58.5 2.1 %convolution_convert_fusion = bf16[256,7168]{1,0:T(8,128)(2,1)S(1)} fusion(bf16[256,384]{1,0:T(8,128)(2,1)S(1)} %get-tuple-element.47, bf16[384,7168]{1,0:T(8,128)(2,1)S(1)} %stage.3), kind=kOutput, calls=%fused_computation | convolution fusion | flops 1411121152 | bytes 9371648 | tf_op jit(solution)/shard_map/dot_general | solution.py:272
  60.8 2.4 %collective-permute-start.15 = (bf16[32,7168]{1,0:T(8,128)(2,1)S(1)}, bf16[32,7168]{1,0:T(8,128)(2,1)S(1)}, u32[]{:S(2)}, u32[]{:S(2)}) collective-permute-start(bf16[32,7168]{1,0:T(8,128)(2,1)S(1)} %get-tuple-element.72), channel_id=1, source_target_pairs={{0,2},{1,65},{2,4},{3,67},{4,6},{5,69},{6,0},{7,71},{64,66},{65,12... | collective-permute-start | bytes 1376264 | tf_op jit(solution)/shard_map/ppermute | solution.py:23
  64.2 2.3 %collective-permute-start.17 = (bf16[32,7168]{1,0:T(8,128)(2,1)S(1)}, bf16[32,7168]{1,0:T(8,128)(2,1)S(1)}, u32[]{:S(2)}, u32[]{:S(2)}) collective-permute-start(bf16[32,7168]{1,0:T(8,128)(2,1)S(1)} %get-tuple-element.70), channel_id=1, source_target_pairs={{0,2},{1,65},{2,4},{3,67},{4,6},{5,69},{6,0},{7,71},{64,66},{65,12... | collective-permute-start | bytes 1376264 | tf_op jit(solution)/shard_map/ppermute | solution.py:23
  67.3 3.2 %collective-permute-done.15 = bf16[32,7168]{1,0:T(8,128)(2,1)S(1)} collective-permute-done((bf16[32,7168]{1,0:T(8,128)(2,1)S(1)}, bf16[32,7168]{1,0:T(8,128)(2,1)S(1)}, u32[]{:S(2)}, u32[]{:S(2)}) %collective-permute-start.15) | collective-permute-done | bytes 458784 | tf_op jit(solution)/shard_map/ppermute | solution.py:23
  70.5 2.3 %collective-permute-done.14 = bf16[32,7168]{1,0:T(8,128)(2,1)S(1)} collective-permute-done((bf16[32,7168]{1,0:T(8,128)(2,1)S(1)}, bf16[32,7168]{1,0:T(8,128)(2,1)S(1)}, u32[]{:S(2)}, u32[]{:S(2)}) %collective-permute-start.14) | collective-permute-done | bytes 458784 | tf_op jit(solution)/shard_map/ppermute | solution.py:23
  75.5 2.3 %collective-permute-done.19 = bf16[32,7168]{1,0:T(8,128)(2,1)S(1)} collective-permute-done((bf16[32,7168]{1,0:T(8,128)(2,1)S(1)}, bf16[32,7168]{1,0:T(8,128)(2,1)S(1)}, u32[]{:S(2)}, u32[]{:S(2)}) %collective-permute-start.19) | collective-permute-done | bytes 458784 | tf_op jit(solution)/shard_map/ppermute | solution.py:23
  77.8 4.9 %collective-permute-done.16 = bf16[32,7168]{1,0:T(8,128)(2,1)S(1)} collective-permute-done((bf16[32,7168]{1,0:T(8,128)(2,1)S(1)}, bf16[32,7168]{1,0:T(8,128)(2,1)S(1)}, u32[]{:S(2)}, u32[]{:S(2)}) %collective-permute-start.16) | collective-permute-done | bytes 458784 | tf_op jit(solution)/shard_map/ppermute | solution.py:23
  84.2 1.7 collective-permute-start.22
  88.0 3.8 %collective-permute-done.22 = bf16[16,7168]{1,0:T(8,128)(2,1)S(1)} collective-permute-done((bf16[16,7168]{1,0:T(8,128)(2,1)S(1)}, bf16[16,7168]{1,0:T(8,128)(2,1)S(1)}, u32[]{:S(2)}, u32[]{:S(2)}) %collective-permute-start.22) | collective-permute-done | bytes 229408 | tf_op jit(solution)/shard_map/ppermute | solution.py:23
  94.5 12.8 %all_to_all.26 = bf16[8,2,7168]{2,1,0:T(2,128)(2,1)S(1)} all-to-all(bf16[8,2,7168]{2,1,0:T(2,128)(2,1)S(1)} %reshape.41), channel_id=1, replica_groups=mesh['x'=4,'z'=8,'y'=4,'c'=2] {'z'}, dimensions={0} | all-to-all | bytes 458752 | tf_op jit(solution)/shard_map/all_to_all | solution.py:91
  108.0 12.5 %all_to_all.27 = bf16[8,2,7168]{2,1,0:T(2,128)(2,1)S(1)} all-to-all(bf16[8,2,7168]{2,1,0:T(2,128)(2,1)S(1)} %broadcast_in_dim.52), channel_id=1, replica_groups=mesh['x'=4,'z'=8,'y'=4,'c'=2] {'z'}, dimensions={0} | all-to-all | bytes 458752 | tf_op jit(solution)/shard_map/all_to_all | solution.py:43
  125.5 6.6 %collective-permute-done.24 = bf16[16,7168]{1,0:T(8,128)(2,1)S(1)} collective-permute-done((bf16[16,7168]{1,0:T(8,128)(2,1)S(1)}, bf16[16,7168]{1,0:T(8,128)(2,1)S(1)}, u32[]{:S(2)}, u32[]{:S(2)}) %collective-permute-start.24) | collective-permute-done | bytes 229408 | tf_op jit(solution)/shard_map/ppermute | solution.py:23
  132.3 3.0 %collective-permute-start.28 = (bf16[32,7168]{1,0:T(8,128)(2,1)S(1)}, bf16[32,7168]{1,0:T(8,128)(2,1)S(1)}, u32[]{:S(2)}, u32[]{:S(2)}) collective-permute-start(bf16[32,7168]{1,0:T(8,128)(2,1)S(1)} %get-tuple-element.60), channel_id=1, source_target_pairs={{0,6},{1,193},{2,0},{3,195},{4,2},{5,197},{6,4},{7,199},{64,70},{6... | collective-permute-start | bytes 1376264 | tf_op jit(solution)/shard_map/ppermute | solution.py:23
  135.3 2.0 %stage.5 = bf16[7168,256]{1,0:T(8,128)(2,1)S(1)} custom-call(bf16[7168,256]{1,0:T(8,128)(2,1)} %collective-permute-done.8.refs_0_), custom_call_target="tpu_custom_call" | custom-call | bytes 7340032 | tf_op jit(solution)/shard_map/stage/pallas_call | solution.py:141
  139.6 1.7 collective-permute-done.28
  141.3 2.5 %collective-permute-done.27 = bf16[32,7168]{1,0:T(8,128)(2,1)S(1)} collective-permute-done((bf16[32,7168]{1,0:T(8,128)(2,1)S(1)}, bf16[32,7168]{1,0:T(8,128)(2,1)S(1)}, u32[]{:S(2)}, u32[]{:S(2)}) %collective-permute-start.27) | collective-permute-done | bytes 458784 | tf_op jit(solution)/shard_map/ppermute | solution.py:23
  143.8 2.5 %collective-permute-start.32 = (bf16[32,7168]{1,0:T(8,128)(2,1)S(1)}, bf16[32,7168]{1,0:T(8,128)(2,1)S(1)}, u32[]{:S(2)}, u32[]{:S(2)}) collective-permute-start(bf16[32,7168]{1,0:T(8,128)(2,1)S(1)} %collective-permute-done.28), channel_id=1, source_target_pairs={{0,6},{1,193},{2,0},{3,195},{4,2},{5,197},{6,4},{7,199},{64,70},{6... | collective-permute-start | bytes 1376264 | tf_op jit(solution)/shard_map/ppermute | solution.py:23
  146.3 2.4 %collective-permute-done.29 = bf16[32,7168]{1,0:T(8,128)(2,1)S(1)} collective-permute-done((bf16[32,7168]{1,0:T(8,128)(2,1)S(1)}, bf16[32,7168]{1,0:T(8,128)(2,1)S(1)}, u32[]{:S(2)}, u32[]{:S(2)}) %collective-permute-start.29) | collective-permute-done | bytes 458784 | tf_op jit(solution)/shard_map/ppermute | solution.py:23
  148.9 4.8 %collective-permute-done.31 = bf16[32,7168]{1,0:T(8,128)(2,1)S(1)} collective-permute-done((bf16[32,7168]{1,0:T(8,128)(2,1)S(1)}, bf16[32,7168]{1,0:T(8,128)(2,1)S(1)}, u32[]{:S(2)}, u32[]{:S(2)}) %collective-permute-start.31) | collective-permute-done | bytes 458784 | tf_op jit(solution)/shard_map/ppermute | solution.py:23
  157.0 19.3 %all_to_all.28 = f32[128,1,128]{2,1,0:T(1,128)S(1)} all-to-all(f32[128,1,128]{2,1,0:T(1,128)S(1)} %bitcast.31), channel_id=1, replica_groups=mesh['x'=4,'z'=8,'y'=4,'c'=2] {'x','y','z'}, dimensions={0} | all-to-all | bytes 131072 | tf_op jit(solution)/shard_map/all_to_all | solution.py:317
  (102 shorter events, 32.0 us)
Async XLA Ops:
  0.6 22.7 %collective-permute-start = (bf16[1,7168,192]{1,2,0:T(8,128)(2,1)}, bf16[1,7168,192]{1,2,0:T(8,128)(2,1)}, u32[]{:S(2)}, u32[]{:S(2)}) collective-permute-start(bf16[1,7168,192]{1,2,0:T(8,128)(2,1)} %param.13), channel_id=1, source_target_pairs={{0,1},{1,0},{2,3},{3,2},{4,5},{5,4},{6,7},{7,6},{8,9},{9,8},{10,11... | collective-permute-start | bytes 8257544 | tf_op jit(solution)/shard_map/ppermute | solution.py:27
  0.7 22.6 %collective-permute-start.1 = (bf16[1,7168,192]{1,2,0:T(8,128)(2,1)}, bf16[1,7168,192]{1,2,0:T(8,128)(2,1)}, u32[]{:S(2)}, u32[]{:S(2)}) collective-permute-start(bf16[1,7168,192]{1,2,0:T(8,128)(2,1)} %param.14), channel_id=1, source_target_pairs={{0,1},{1,0},{2,3},{3,2},{4,5},{5,4},{6,7},{7,6},{8,9},{9,8},{10,11... | collective-permute-start | bytes 8257544 | tf_op jit(solution)/shard_map/ppermute | solution.py:27
  1.2 33.7 %collective-permute-start.5 = (bf16[1,192,7168]{2,1,0:T(8,128)(2,1)}, bf16[1,192,7168]{2,1,0:T(8,128)(2,1)}, u32[]{:S(2)}, u32[]{:S(2)}) collective-permute-start(bf16[1,192,7168]{2,1,0:T(8,128)(2,1)} %param.15), channel_id=1, source_target_pairs={{0,1},{1,0},{2,3},{3,2},{4,5},{5,4},{6,7},{7,6},{8,9},{9,8},{10,11... | collective-permute-start | bytes 8257544 | tf_op jit(solution)/shard_map/ppermute | solution.py:27
  3.0 20.2 %all-to-all-start = ((bf16[8,2,7296]{2,1,0:T(2,128)(2,1)}), bf16[8,2,7296]{2,1,0:T(2,128)(2,1)S(1)}, u32[]{:S(2)}, u32[]{:S(2)}) async-start(bf16[8,2,7296]{2,1,0:T(2,128)(2,1)} %spread.1), calls=%async_computation | async-start | bytes 466944 | tf_op jit(solution)/shard_map/all_to_all | solution.py:43
  11.5 33.6 %collective-permute-start.8 = (bf16[7168,256]{1,0:T(8,128)(2,1)}, bf16[7168,256]{1,0:T(8,128)(2,1)}, u32[]{:S(2)}, u32[]{:S(2)}) collective-permute-start(bf16[7168,256]{1,0:T(8,128)(2,1)} %param.17), channel_id=1, source_target_pairs={{0,1},{1,0},{2,3},{3,2},{4,5},{5,4},{6,7},{7,6},{8,9},{9,8},{10,11... | collective-permute-start | bytes 11010056 | tf_op jit(solution)/shard_map/ppermute | solution.py:27
  23.3 11.6 %collective-permute-start.4 = (bf16[16,7296]{1,0:T(8,128)(2,1)S(1)}, bf16[16,7296]{1,0:T(8,128)(2,1)S(1)}, u32[]{:S(2)}, u32[]{:S(2)}) collective-permute-start(bf16[16,7296]{1,0:T(8,128)(2,1)S(1)} %reshape.40), channel_id=1, source_target_pairs={{0,128},{1,5},{2,130},{3,7},{4,132},{5,1},{6,134},{7,3},{64,192},{... | collective-permute-start | bytes 700424 | tf_op jit(solution)/shard_map/ppermute | solution.py:23
  26.4 8.5 %collective-permute-start.3 = (bf16[16,7296]{1,0:T(8,128)(2,1)S(1)}, bf16[16,7296]{1,0:T(8,128)(2,1)S(1)}, u32[]{:S(2)}, u32[]{:S(2)}) collective-permute-start(bf16[16,7296]{1,0:T(8,128)(2,1)S(1)} %reshape.40), channel_id=1, source_target_pairs={{0,192},{1,7},{2,194},{3,1},{4,196},{5,3},{6,198},{7,5},{64,0},{65... | collective-permute-start | bytes 700424 | tf_op jit(solution)/shard_map/ppermute | solution.py:23
  27.6 7.3 %collective-permute-start.2 = (bf16[16,7296]{1,0:T(8,128)(2,1)S(1)}, bf16[16,7296]{1,0:T(8,128)(2,1)S(1)}, u32[]{:S(2)}, u32[]{:S(2)}) collective-permute-start(bf16[16,7296]{1,0:T(8,128)(2,1)S(1)} %reshape.40), channel_id=1, source_target_pairs={{0,64},{1,3},{2,66},{3,5},{4,68},{5,7},{6,70},{7,1},{64,128},{65,6... | collective-permute-start | bytes 700424 | tf_op jit(solution)/shard_map/ppermute | solution.py:23
  35.0 8.6 %collective-permute-start.7 = (bf16[32,7296]{1,0:T(8,128)(2,1)S(1)}, bf16[32,7296]{1,0:T(8,128)(2,1)S(1)}, u32[]{:S(2)}, u32[]{:S(2)}) collective-permute-start(bf16[32,7296]{1,0:T(8,128)(2,1)S(1)} %get-tuple-element.42), channel_id=1, source_target_pairs={{0,6},{1,193},{2,0},{3,195},{4,2},{5,197},{6,4},{7,199},{64,70},{6... | collective-permute-start | bytes 1400840 | tf_op jit(solution)/shard_map/ppermute | solution.py:23
  35.5 9.6 %collective-permute-start.6 = (bf16[32,7296]{1,0:T(8,128)(2,1)S(1)}, bf16[32,7296]{1,0:T(8,128)(2,1)S(1)}, u32[]{:S(2)}, u32[]{:S(2)}) collective-permute-start(bf16[32,7296]{1,0:T(8,128)(2,1)S(1)} %get-tuple-element.43), channel_id=1, source_target_pairs={{0,2},{1,65},{2,4},{3,67},{4,6},{5,69},{6,0},{7,71},{64,66},{65,12... | collective-permute-start | bytes 1400840 | tf_op jit(solution)/shard_map/ppermute | solution.py:23
  39.4 12.0 %collective-permute-start.9 = (bf16[32,7296]{1,0:T(8,128)(2,1)S(1)}, bf16[32,7296]{1,0:T(8,128)(2,1)S(1)}, u32[]{:S(2)}, u32[]{:S(2)}) collective-permute-start(bf16[32,7296]{1,0:T(8,128)(2,1)S(1)} %get-tuple-element.42), channel_id=1, source_target_pairs={{0,2},{1,65},{2,4},{3,67},{4,6},{5,69},{6,0},{7,71},{64,66},{65,12... | collective-permute-start | bytes 1400840 | tf_op jit(solution)/shard_map/ppermute | solution.py:23
  41.1 10.4 %collective-permute-start.10 = (bf16[32,7296]{1,0:T(8,128)(2,1)S(1)}, bf16[32,7296]{1,0:T(8,128)(2,1)S(1)}, u32[]{:S(2)}, u32[]{:S(2)}) collective-permute-start(bf16[32,7296]{1,0:T(8,128)(2,1)S(1)} %get-tuple-element.43), channel_id=1, source_target_pairs={{0,6},{1,193},{2,0},{3,195},{4,2},{5,197},{6,4},{7,199},{64,70},{6... | collective-permute-start | bytes 1400840 | tf_op jit(solution)/shard_map/ppermute | solution.py:23
  45.1 10.0 %collective-permute-start.11 = (bf16[32,7296]{1,0:T(8,128)(2,1)S(1)}, bf16[32,7296]{1,0:T(8,128)(2,1)S(1)}, u32[]{:S(2)}, u32[]{:S(2)}) collective-permute-start(bf16[32,7296]{1,0:T(8,128)(2,1)S(1)} %collective-permute-done.6), channel_id=1, source_target_pairs={{0,2},{1,65},{2,4},{3,67},{4,6},{5,69},{6,0},{7,71},{64,66},{65,12... | collective-permute-start | bytes 1400840 | tf_op jit(solution)/shard_map/ppermute | solution.py:23
  45.7 9.5 %collective-permute-start.12 = (bf16[32,7296]{1,0:T(8,128)(2,1)S(1)}, bf16[32,7296]{1,0:T(8,128)(2,1)S(1)}, u32[]{:S(2)}, u32[]{:S(2)}) collective-permute-start(bf16[32,7296]{1,0:T(8,128)(2,1)S(1)} %collective-permute-done.7), channel_id=1, source_target_pairs={{0,6},{1,193},{2,0},{3,195},{4,2},{5,197},{6,4},{7,199},{64,70},{6... | collective-permute-start | bytes 1400840 | tf_op jit(solution)/shard_map/ppermute | solution.py:23
  60.8 9.8 %collective-permute-start.15 = (bf16[32,7168]{1,0:T(8,128)(2,1)S(1)}, bf16[32,7168]{1,0:T(8,128)(2,1)S(1)}, u32[]{:S(2)}, u32[]{:S(2)}) collective-permute-start(bf16[32,7168]{1,0:T(8,128)(2,1)S(1)} %get-tuple-element.72), channel_id=1, source_target_pairs={{0,2},{1,65},{2,4},{3,67},{4,6},{5,69},{6,0},{7,71},{64,66},{65,12... | collective-permute-start | bytes 1376264 | tf_op jit(solution)/shard_map/ppermute | solution.py:23
  63.2 9.7 %collective-permute-start.14 = (bf16[32,7168]{1,0:T(8,128)(2,1)S(1)}, bf16[32,7168]{1,0:T(8,128)(2,1)S(1)}, u32[]{:S(2)}, u32[]{:S(2)}) collective-permute-start(bf16[32,7168]{1,0:T(8,128)(2,1)S(1)} %get-tuple-element.73), channel_id=1, source_target_pairs={{0,6},{1,193},{2,0},{3,195},{4,2},{5,197},{6,4},{7,199},{64,70},{6... | collective-permute-start | bytes 1376264 | tf_op jit(solution)/shard_map/ppermute | solution.py:23
  64.2 11.3 %collective-permute-start.17 = (bf16[32,7168]{1,0:T(8,128)(2,1)S(1)}, bf16[32,7168]{1,0:T(8,128)(2,1)S(1)}, u32[]{:S(2)}, u32[]{:S(2)}) collective-permute-start(bf16[32,7168]{1,0:T(8,128)(2,1)S(1)} %get-tuple-element.70), channel_id=1, source_target_pairs={{0,2},{1,65},{2,4},{3,67},{4,6},{5,69},{6,0},{7,71},{64,66},{65,12... | collective-permute-start | bytes 1376264 | tf_op jit(solution)/shard_map/ppermute | solution.py:23
  66.4 11.4 %collective-permute-start.19 = (bf16[32,7168]{1,0:T(8,128)(2,1)S(1)}, bf16[32,7168]{1,0:T(8,128)(2,1)S(1)}, u32[]{:S(2)}, u32[]{:S(2)}) collective-permute-start(bf16[32,7168]{1,0:T(8,128)(2,1)S(1)} %get-tuple-element.71), channel_id=1, source_target_pairs={{0,6},{1,193},{2,0},{3,195},{4,2},{5,197},{6,4},{7,199},{64,70},{6... | collective-permute-start | bytes 1376264 | tf_op jit(solution)/shard_map/ppermute | solution.py:23
  73.1 9.6 %collective-permute-start.16 = (bf16[32,7168]{1,0:T(8,128)(2,1)S(1)}, bf16[32,7168]{1,0:T(8,128)(2,1)S(1)}, u32[]{:S(2)}, u32[]{:S(2)}) collective-permute-start(bf16[32,7168]{1,0:T(8,128)(2,1)S(1)} %get-tuple-element.53), channel_id=1, source_target_pairs={{0,6},{1,193},{2,0},{3,195},{4,2},{5,197},{6,4},{7,199},{64,70},{6... | collective-permute-start | bytes 1376264 | tf_op jit(solution)/shard_map/ppermute | solution.py:23
  74.1 9.7 %collective-permute-start.20 = (bf16[32,7168]{1,0:T(8,128)(2,1)S(1)}, bf16[32,7168]{1,0:T(8,128)(2,1)S(1)}, u32[]{:S(2)}, u32[]{:S(2)}) collective-permute-start(bf16[32,7168]{1,0:T(8,128)(2,1)S(1)} %get-tuple-element.54), channel_id=1, source_target_pairs={{0,2},{1,65},{2,4},{3,67},{4,6},{5,69},{6,0},{7,71},{64,66},{65,12... | collective-permute-start | bytes 1376264 | tf_op jit(solution)/shard_map/ppermute | solution.py:23
  84.2 7.6 %collective-permute-start.22 = (bf16[16,7168]{1,0:T(8,128)(2,1)S(1)}, bf16[16,7168]{1,0:T(8,128)(2,1)S(1)}, u32[]{:S(2)}, u32[]{:S(2)}) collective-permute-start(bf16[16,7168]{1,0:T(8,128)(2,1)S(1)} %get-tuple-element.77), channel_id=1, source_target_pairs={{0,128},{1,5},{2,130},{3,7},{4,132},{5,1},{6,134},{7,3},{64,192},{... | collective-permute-start | bytes 688136 | tf_op jit(solution)/shard_map/ppermute | solution.py:23
  85.9 7.0 %collective-permute-start.18 = (bf16[16,7168]{1,0:T(8,128)(2,1)S(1)}, bf16[16,7168]{1,0:T(8,128)(2,1)S(1)}, u32[]{:S(2)}, u32[]{:S(2)}) collective-permute-start(bf16[16,7168]{1,0:T(8,128)(2,1)S(1)} %slice.57), channel_id=1, source_target_pairs={{0,192},{1,7},{2,194},{3,1},{4,196},{5,3},{6,198},{7,5},{64,0},{65... | collective-permute-start | bytes 688136 | tf_op jit(solution)/shard_map/ppermute | solution.py:23
  87.1 7.2 %collective-permute-start.21 = (bf16[16,7168]{1,0:T(8,128)(2,1)S(1)}, bf16[16,7168]{1,0:T(8,128)(2,1)S(1)}, u32[]{:S(2)}, u32[]{:S(2)}) collective-permute-start(bf16[16,7168]{1,0:T(8,128)(2,1)S(1)} %get-tuple-element.76), channel_id=1, source_target_pairs={{0,64},{1,3},{2,66},{3,5},{4,68},{5,7},{6,70},{7,1},{64,128},{65,6... | collective-permute-start | bytes 688136 | tf_op jit(solution)/shard_map/ppermute | solution.py:23
  122.2 10.0 %collective-permute-start.26 = (bf16[16,7168]{1,0:T(8,128)(2,1)S(1)}, bf16[16,7168]{1,0:T(8,128)(2,1)S(1)}, u32[]{:S(2)}, u32[]{:S(2)}) collective-permute-start(bf16[16,7168]{1,0:T(8,128)(2,1)S(1)} %reshape.42), channel_id=1, source_target_pairs={{0,128},{1,5},{2,130},{3,7},{4,132},{5,1},{6,134},{7,3},{64,192},{... | collective-permute-start | bytes 688136 | tf_op jit(solution)/shard_map/ppermute | solution.py:23
  123.5 8.8 %collective-permute-start.25 = (bf16[16,7168]{1,0:T(8,128)(2,1)S(1)}, bf16[16,7168]{1,0:T(8,128)(2,1)S(1)}, u32[]{:S(2)}, u32[]{:S(2)}) collective-permute-start(bf16[16,7168]{1,0:T(8,128)(2,1)S(1)} %reshape.42), channel_id=1, source_target_pairs={{0,192},{1,7},{2,194},{3,1},{4,196},{5,3},{6,198},{7,5},{64,0},{65... | collective-permute-start | bytes 688136 | tf_op jit(solution)/shard_map/ppermute | solution.py:23
  124.7 7.5 %collective-permute-start.24 = (bf16[16,7168]{1,0:T(8,128)(2,1)S(1)}, bf16[16,7168]{1,0:T(8,128)(2,1)S(1)}, u32[]{:S(2)}, u32[]{:S(2)}) collective-permute-start(bf16[16,7168]{1,0:T(8,128)(2,1)S(1)} %reshape.42), channel_id=1, source_target_pairs={{0,64},{1,3},{2,66},{3,5},{4,68},{5,7},{6,70},{7,1},{64,128},{65,6... | collective-permute-start | bytes 688136 | tf_op jit(solution)/shard_map/ppermute | solution.py:23
  132.3 9.0 %collective-permute-start.28 = (bf16[32,7168]{1,0:T(8,128)(2,1)S(1)}, bf16[32,7168]{1,0:T(8,128)(2,1)S(1)}, u32[]{:S(2)}, u32[]{:S(2)}) collective-permute-start(bf16[32,7168]{1,0:T(8,128)(2,1)S(1)} %get-tuple-element.60), channel_id=1, source_target_pairs={{0,6},{1,193},{2,0},{3,195},{4,2},{5,197},{6,4},{7,199},{64,70},{6... | collective-permute-start | bytes 1376264 | tf_op jit(solution)/shard_map/ppermute | solution.py:23
  135.3 8.5 %collective-permute-start.27 = (bf16[32,7168]{1,0:T(8,128)(2,1)S(1)}, bf16[32,7168]{1,0:T(8,128)(2,1)S(1)}, u32[]{:S(2)}, u32[]{:S(2)}) collective-permute-start(bf16[32,7168]{1,0:T(8,128)(2,1)S(1)} %get-tuple-element.61), channel_id=1, source_target_pairs={{0,2},{1,65},{2,4},{3,67},{4,6},{5,69},{6,0},{7,71},{64,66},{65,12... | collective-permute-start | bytes 1376264 | tf_op jit(solution)/shard_map/ppermute | solution.py:23
  137.4 11.3 %collective-permute-start.29 = (bf16[32,7168]{1,0:T(8,128)(2,1)S(1)}, bf16[32,7168]{1,0:T(8,128)(2,1)S(1)}, u32[]{:S(2)}, u32[]{:S(2)}) collective-permute-start(bf16[32,7168]{1,0:T(8,128)(2,1)S(1)} %get-tuple-element.60), channel_id=1, source_target_pairs={{0,2},{1,65},{2,4},{3,67},{4,6},{5,69},{6,0},{7,71},{64,66},{65,12... | collective-permute-start | bytes 1376264 | tf_op jit(solution)/shard_map/ppermute | solution.py:23
  138.2 10.5 %collective-permute-start.30 = (bf16[32,7168]{1,0:T(8,128)(2,1)S(1)}, bf16[32,7168]{1,0:T(8,128)(2,1)S(1)}, u32[]{:S(2)}, u32[]{:S(2)}) collective-permute-start(bf16[32,7168]{1,0:T(8,128)(2,1)S(1)} %get-tuple-element.61), channel_id=1, source_target_pairs={{0,6},{1,193},{2,0},{3,195},{4,2},{5,197},{6,4},{7,199},{64,70},{6... | collective-permute-start | bytes 1376264 | tf_op jit(solution)/shard_map/ppermute | solution.py:23
  143.8 9.8 %collective-permute-start.31 = (bf16[32,7168]{1,0:T(8,128)(2,1)S(1)}, bf16[32,7168]{1,0:T(8,128)(2,1)S(1)}, u32[]{:S(2)}, u32[]{:S(2)}) collective-permute-start(bf16[32,7168]{1,0:T(8,128)(2,1)S(1)} %collective-permute-done.27), channel_id=1, source_target_pairs={{0,2},{1,65},{2,4},{3,67},{4,6},{5,69},{6,0},{7,71},{64,66},{65,12... | collective-permute-start | bytes 1376264 | tf_op jit(solution)/shard_map/ppermute | solution.py:23
  143.8 9.9 %collective-permute-start.32 = (bf16[32,7168]{1,0:T(8,128)(2,1)S(1)}, bf16[32,7168]{1,0:T(8,128)(2,1)S(1)}, u32[]{:S(2)}, u32[]{:S(2)}) collective-permute-start(bf16[32,7168]{1,0:T(8,128)(2,1)S(1)} %collective-permute-done.28), channel_id=1, source_target_pairs={{0,6},{1,193},{2,0},{3,195},{4,2},{5,197},{6,4},{7,199},{64,70},{6... | collective-permute-start | bytes 1376264 | tf_op jit(solution)/shard_map/ppermute | solution.py:23
  (9 other events, 178.0 us)

commit v5 on v4

--- a/solution.py
+++ b/solution.py
@@ -57,8 +57,8 @@
     up_low, down_top = move(low, 1, 1), move(top, -1, 1)
     up_top, down_low, *extra = together(up_top, down_low, *extra)
     far_top, far_low = move(up_top, 1, 1), move(down_low, -1, 1)
-    rows = jnp.concatenate([wide, up_top, up_low, down_top, down_low, far_top, far_low], axis=0)
-    return rows, staged, *extra
+    near = jnp.concatenate([wide, up_top, up_low, down_top, down_low], axis=0)
+    return near, jnp.concatenate([far_top, far_low], axis=0), staged, *extra
 
 
 def narrow(*values):
@@ -194,14 +194,15 @@
     )(expert, rows, in_weight)
 
 
-def stats_kernel(place_ref, own_ref, other_ref, meta_ref, *refs):
+def stats_kernel(place_ref, near_own, near_other, far_own, far_other, meta_ref, *refs):
     out_ref, stats = refs[-2:]
-    rows = own_ref.shape[0]
+    rows = meta_ref.shape[0]
     lane = lax.broadcasted_iota(jnp.int32, (rows, META), 1)
     meta = meta_ref[...]
     goal = jnp.where(lane == 16, meta * 256.0, jnp.where(lane == 17, meta, 0.0))
     goal = jnp.sum(goal, axis=1, keepdims=True).astype(jnp.int32)
-    own, other = own_ref[...], other_ref[...]
+    own = jnp.concatenate([near_own[...], far_own[...]], axis=0)
+    other = jnp.concatenate([near_other[...], far_other[...]], axis=0)
     top = jnp.maximum(jnp.max(own, axis=1, keepdims=True), jnp.max(other, axis=1, keepdims=True))
     total = jnp.zeros_like(top)
     picked = jnp.zeros_like(top)
@@ -242,17 +243,17 @@
     )(stats)
 
 
-def row_stats(own, other, meta, place, *signs):
-    rows = own.shape[0]
+def row_stats(near, far, meta, place, *signs):
+    rows = meta.shape[0]
     return pl.pallas_call(
         stats_kernel,
         out_shape=jax.ShapeDtypeStruct((rows // 2, META), jnp.float32),
-        in_specs=[SMEM, VMEM, VMEM, VMEM] + [ANY] * len(signs),
+        in_specs=[SMEM] + [VMEM] * 5 + [ANY] * len(signs),
         out_specs=VMEM,
         scratch_shapes=[pltpu.VMEM((rows, META), jnp.float32)],
         compiler_params=pltpu.CompilerParams(vmem_limit_bytes=8 * 2**20),
         name="row_stats",
-    )(place, own, other, meta, *signs)
+    )(place, *near, *far, meta, *signs)
 
 
 def shards(
@@ -295,9 +296,10 @@
         expert,
     )
     wide, down = first_axis_rows(column, swap(expert_down))
-    rows, out_weight, gate, up, head = second_axis_rows(
+    near, far, out_weight, gate, up, head = second_axis_rows(
         wide, stage(expert_down[0], down[0]), gate, up, swap(head_weight)
     )
+    rows = jnp.concatenate([near, far], axis=0)
     in_weight = stage(expert_gate[0].T, gate[0].T, expert_up[0].T, up[0].T)
     active, meta = expert_units(rows, in_weight, expert)
     partial, first_sign = together(product(active, out_weight).astype(jnp.bfloat16), swap(meta))
@@ -312,8 +314,9 @@
     column = column_rows(jnp.broadcast_to(normed[None], (depth,) + normed.shape))
     column, second_sign = together(column, swap(column))
     wide, head = first_axis_rows(column, head)
-    every, head = second_axis_rows(wide, stage(head))
-    stats = row_stats(product(every, head_weight), product(every, head), meta, place, first_sign, second_sign)
+    near, far, head = second_axis_rows(wide, stage(head))
+    logits = [[product(part, weight) for weight in (head_weight, head)] for part in (near, far)]
+    stats = row_stats(*logits, meta, place, first_sign, second_sign)
     arrived = lax.all_to_all(stats, ("x", "y", "z"), 0, 0, tiled=True)
     logprob = combine(arrived)
     return (logprob, hidden)

time: 178 us -> 177 us (level)
  waiting for transfers between devices: 64 us -> 62.2 us
    ppermute x27, waiting for transfers between devices: 51.9 us -> 50.1 us  [move(): return lax.ppermute(value, PLANE, pairs)]
    dot_general x3 -> x5, matrix products: 4.29 us -> 5.27 us  [product(): return jnp.dot(left, right, preferred_element_type=jnp.float32)]
  transfers between devices with their start and end apart: 34 -> 34, of which waited for: 20 -> 20; matrix products, arithmetic and copies ran while one was open for 2% -> 3% of each run, Pallas kernels for 5% -> 5%
where the time goes in v5:
time: 177 us
  waiting for transfers between devices  62.2 us (35%)
  starting transfers between devices  45.6 us (26%)
  blocking collectives  44.7 us (25%)
  Pallas kernels  14 us (8%)
  matrix products  5.27 us (3%)
  other arithmetic  2.03 us (1%)
    ppermute x27, waiting for transfers between devices, move(): return lax.ppermute(value, PLANE, pairs)  50.1 us
    ppermute x27, starting transfers between devices, move(): return lax.ppermute(value, PLANE, pairs)  36.1 us
    all_to_all x1, blocking collectives, shards(): arrived = lax.all_to_all(stats, ('x', 'y', 'z'), 0, 0, tiled=True)  19.3 us
    all_to_all x1, blocking collectives, fold_column(): lax.all_to_all(partial.reshape(depth, 2, width), 'z', 0, 0, tiled=True)  12.8 us
    all_to_all x1, blocking collectives, column_rows(): lax.all_to_all(spread, 'z', 0, 0, tiled=True).reshape(depth * rows, width)  12.5 us
    all_to_all x1, waiting for transfers between devices, column_rows(): lax.all_to_all(spread, 'z', 0, 0, tiled=True).reshape(depth * rows, width)  10.6 us
    all_to_all x1, starting transfers between devices, column_rows(): lax.all_to_all(spread, 'z', 0, 0, tiled=True).reshape(depth * rows, width)  8.47 us
    pallas_call x3, Pallas kernels, stage(): pl.pallas_call(stage_kernel, out_shape=pltpu.VMEM(shape, weights[0].dtype...  7.43 us
  transfers between devices with their start and end apart: 34, of which 20 were waited for; matrix products, arithmetic and copies ran while one was open for 3% of the time, Pallas kernels for 5%

profile of v5, /device:TPU:8, one launch (start us, length us, event | category | flops | bytes accessed | tf_op | source)
XLA Modules:
  0.0 176.5 jit_solution(5349833441637406295)
XLA Ops:
  1.3 1.7 spread.1
  3.0 8.5 %all-to-all-start = ((bf16[8,2,7296]{2,1,0:T(2,128)(2,1)}), bf16[8,2,7296]{2,1,0:T(2,128)(2,1)S(1)}, u32[]{:S(2)}, u32[]{:S(2)}) async-start(bf16[8,2,7296]{2,1,0:T(2,128)(2,1)} %spread.1), calls=%async_computation | async-start | bytes 466944 | tf_op jit(solution)/shard_map/all_to_all | solution.py:43
  12.6 10.6 %all-to-all-done = bf16[8,2,7296]{2,1,0:T(2,128)(2,1)S(1)} async-done(((bf16[8,2,7296]{2,1,0:T(2,128)(2,1)}), bf16[8,2,7296]{2,1,0:T(2,128)(2,1)S(1)}, u32[]{:S(2)}, u32[]{:S(2)}) %all-to-all-start) | async-done | bytes 233504 | tf_op jit(solution)/shard_map/all_to_all | solution.py:43
  23.3 3.1 %collective-permute-start.4 = (bf16[16,7296]{1,0:T(8,128)(2,1)S(1)}, bf16[16,7296]{1,0:T(8,128)(2,1)S(1)}, u32[]{:S(2)}, u32[]{:S(2)}) collective-permute-start(bf16[16,7296]{1,0:T(8,128)(2,1)S(1)} %reshape.40), channel_id=1, source_target_pairs={{0,128},{1,5},{2,130},{3,7},{4,132},{5,1},{6,134},{7,3},{64,192},{... | collective-permute-start | bytes 700424 | tf_op jit(solution)/shard_map/ppermute | solution.py:23
  28.5 6.4 %collective-permute-done.2 = bf16[16,7296]{1,0:T(8,128)(2,1)S(1)} collective-permute-done((bf16[16,7296]{1,0:T(8,128)(2,1)S(1)}, bf16[16,7296]{1,0:T(8,128)(2,1)S(1)}, u32[]{:S(2)}, u32[]{:S(2)}) %collective-permute-start.2) | collective-permute-done | bytes 233504 | tf_op jit(solution)/shard_map/ppermute | solution.py:23
  37.1 2.3 %stage.3 = bf16[384,7168]{1,0:T(8,128)(2,1)S(1)} custom-call(bf16[192,7168]{1,0:T(8,128)(2,1)S(1)} %bitcast.31, bf16[192,7168]{1,0:T(8,128)(2,1)} %bitcast.4.refs_1_), custom_call_target="tpu_custom_call" | custom-call | bytes 11010048 | tf_op jit(solution)/shard_map/stage/pallas_call | solution.py:141
  39.4 1.7 collective-permute-start.9
  41.5 2.1 %collective-permute-done.7 = bf16[32,7296]{1,0:T(8,128)(2,1)S(1)} collective-permute-done((bf16[32,7296]{1,0:T(8,128)(2,1)S(1)}, bf16[32,7296]{1,0:T(8,128)(2,1)S(1)}, u32[]{:S(2)}, u32[]{:S(2)}) %collective-permute-start.7) | collective-permute-done | bytes 466976 | tf_op jit(solution)/shard_map/ppermute | solution.py:23
  45.7 2.7 %collective-permute-start.12 = (bf16[32,7296]{1,0:T(8,128)(2,1)S(1)}, bf16[32,7296]{1,0:T(8,128)(2,1)S(1)}, u32[]{:S(2)}, u32[]{:S(2)}) collective-permute-start(bf16[32,7296]{1,0:T(8,128)(2,1)S(1)} %collective-permute-done.7), channel_id=1, source_target_pairs={{0,6},{1,193},{2,0},{3,195},{4,2},{5,197},{6,4},{7,199},{64,70},{6... | collective-permute-start | bytes 1400840 | tf_op jit(solution)/shard_map/ppermute | solution.py:23
  48.4 3.1 %stage.4.in_ref = bf16[768,7168]{1,0:T(8,128)(2,1)S(1)} custom-call(bf16[192,7168]{1,0:T(8,128)(2,1)S(1)} %bitcast.32, bf16[192,7168]{1,0:T(8,128)(2,1)} %bitcast.8.refs_1_, bf16[192,7168]{1,0:T(8,128)(2,1)S(1)} %bitcast.33, bf16[192,7168]{1,0:T(8,128)(2,1)} %bitcast.12.refs_3_), custom_call_target="tpu_custom_call" | custom-call | bytes 22020096 | tf_op jit(solution)/shard_map/stage/pallas_call | solution.py:141
  51.6 3.5 %collective-permute-done.11 = bf16[32,7296]{1,0:T(8,128)(2,1)S(1)} collective-permute-done((bf16[32,7296]{1,0:T(8,128)(2,1)S(1)}, bf16[32,7296]{1,0:T(8,128)(2,1)S(1)}, u32[]{:S(2)}, u32[]{:S(2)}) %collective-permute-start.11) | collective-permute-done | bytes 466976 | tf_op jit(solution)/shard_map/ppermute | solution.py:23
  55.2 3.1 %expert.1 = (bf16[256,384]{1,0:T(8,128)(2,1)S(1)}, f32[256,128]{1,0:T(8,128)S(1)}) custom-call(s32[1]{0:T(128)} %bitcast.2.expert_ref, bf16[256,7296]{1,0:T(8,128)(2,1)S(1)} %constant_dynamic-update-slice_fusion.4.row_ref, bf16[768,7168]{1,0:T(8,128)(2,1)S(1)} %stage.4.in_ref), custom_call_target="tpu_custom_call" | custom-call | flops 2818572288 | bytes 14680064 | tf_op jit(solution)/shard_map/expert/pallas_call | solution.py:178
  58.5 2.1 %convolution_convert_fusion = bf16[256,7168]{1,0:T(8,128)(2,1)S(1)} fusion(bf16[256,384]{1,0:T(8,128)(2,1)S(1)} %get-tuple-element.47, bf16[384,7168]{1,0:T(8,128)(2,1)S(1)} %stage.3), kind=kOutput, calls=%fused_computation | convolution fusion | flops 1411121152 | bytes 9371648 | tf_op jit(solution)/shard_map/dot_general | solution.py:273
  60.8 2.4 %collective-permute-start.15 = (bf16[32,7168]{1,0:T(8,128)(2,1)S(1)}, bf16[32,7168]{1,0:T(8,128)(2,1)S(1)}, u32[]{:S(2)}, u32[]{:S(2)}) collective-permute-start(bf16[32,7168]{1,0:T(8,128)(2,1)S(1)} %get-tuple-element.72), channel_id=1, source_target_pairs={{0,2},{1,65},{2,4},{3,67},{4,6},{5,69},{6,0},{7,71},{64,66},{65,12... | collective-permute-start | bytes 1376264 | tf_op jit(solution)/shard_map/ppermute | solution.py:23
  64.2 2.3 %collective-permute-start.17 = (bf16[32,7168]{1,0:T(8,128)(2,1)S(1)}, bf16[32,7168]{1,0:T(8,128)(2,1)S(1)}, u32[]{:S(2)}, u32[]{:S(2)}) collective-permute-start(bf16[32,7168]{1,0:T(8,128)(2,1)S(1)} %get-tuple-element.70), channel_id=1, source_target_pairs={{0,2},{1,65},{2,4},{3,67},{4,6},{5,69},{6,0},{7,71},{64,66},{65,12... | collective-permute-start | bytes 1376264 | tf_op jit(solution)/shard_map/ppermute | solution.py:23
  67.3 3.2 %collective-permute-done.15 = bf16[32,7168]{1,0:T(8,128)(2,1)S(1)} collective-permute-done((bf16[32,7168]{1,0:T(8,128)(2,1)S(1)}, bf16[32,7168]{1,0:T(8,128)(2,1)S(1)}, u32[]{:S(2)}, u32[]{:S(2)}) %collective-permute-start.15) | collective-permute-done | bytes 458784 | tf_op jit(solution)/shard_map/ppermute | solution.py:23
  70.5 2.3 %collective-permute-done.14 = bf16[32,7168]{1,0:T(8,128)(2,1)S(1)} collective-permute-done((bf16[32,7168]{1,0:T(8,128)(2,1)S(1)}, bf16[32,7168]{1,0:T(8,128)(2,1)S(1)}, u32[]{:S(2)}, u32[]{:S(2)}) %collective-permute-start.14) | collective-permute-done | bytes 458784 | tf_op jit(solution)/shard_map/ppermute | solution.py:23
  75.5 2.3 %collective-permute-done.19 = bf16[32,7168]{1,0:T(8,128)(2,1)S(1)} collective-permute-done((bf16[32,7168]{1,0:T(8,128)(2,1)S(1)}, bf16[32,7168]{1,0:T(8,128)(2,1)S(1)}, u32[]{:S(2)}, u32[]{:S(2)}) %collective-permute-start.19) | collective-permute-done | bytes 458784 | tf_op jit(solution)/shard_map/ppermute | solution.py:23
  77.8 4.9 %collective-permute-done.16 = bf16[32,7168]{1,0:T(8,128)(2,1)S(1)} collective-permute-done((bf16[32,7168]{1,0:T(8,128)(2,1)S(1)}, bf16[32,7168]{1,0:T(8,128)(2,1)S(1)}, u32[]{:S(2)}, u32[]{:S(2)}) %collective-permute-start.16) | collective-permute-done | bytes 458784 | tf_op jit(solution)/shard_map/ppermute | solution.py:23
  84.2 1.7 collective-permute-start.22
  88.0 3.8 %collective-permute-done.22 = bf16[16,7168]{1,0:T(8,128)(2,1)S(1)} collective-permute-done((bf16[16,7168]{1,0:T(8,128)(2,1)S(1)}, bf16[16,7168]{1,0:T(8,128)(2,1)S(1)}, u32[]{:S(2)}, u32[]{:S(2)}) %collective-permute-start.22) | collective-permute-done | bytes 229408 | tf_op jit(solution)/shard_map/ppermute | solution.py:23
  94.5 12.8 %all_to_all.26 = bf16[8,2,7168]{2,1,0:T(2,128)(2,1)S(1)} all-to-all(bf16[8,2,7168]{2,1,0:T(2,128)(2,1)S(1)} %reshape.41), channel_id=1, replica_groups=mesh['x'=4,'z'=8,'y'=4,'c'=2] {'z'}, dimensions={0} | all-to-all | bytes 458752 | tf_op jit(solution)/shard_map/all_to_all | solution.py:91
  108.0 12.5 %all_to_all.27 = bf16[8,2,7168]{2,1,0:T(2,128)(2,1)S(1)} all-to-all(bf16[8,2,7168]{2,1,0:T(2,128)(2,1)S(1)} %broadcast_in_dim.52), channel_id=1, replica_groups=mesh['x'=4,'z'=8,'y'=4,'c'=2] {'z'}, dimensions={0} | all-to-all | bytes 458752 | tf_op jit(solution)/shard_map/all_to_all | solution.py:43
  125.6 6.6 %collective-permute-done.24 = bf16[16,7168]{1,0:T(8,128)(2,1)S(1)} collective-permute-done((bf16[16,7168]{1,0:T(8,128)(2,1)S(1)}, bf16[16,7168]{1,0:T(8,128)(2,1)S(1)}, u32[]{:S(2)}, u32[]{:S(2)}) %collective-permute-start.24) | collective-permute-done | bytes 229408 | tf_op jit(solution)/shard_map/ppermute | solution.py:23
  132.3 3.0 %collective-permute-start.28 = (bf16[32,7168]{1,0:T(8,128)(2,1)S(1)}, bf16[32,7168]{1,0:T(8,128)(2,1)S(1)}, u32[]{:S(2)}, u32[]{:S(2)}) collective-permute-start(bf16[32,7168]{1,0:T(8,128)(2,1)S(1)} %get-tuple-element.60), channel_id=1, source_target_pairs={{0,6},{1,193},{2,0},{3,195},{4,2},{5,197},{6,4},{7,199},{64,70},{6... | collective-permute-start | bytes 1376264 | tf_op jit(solution)/shard_map/ppermute | solution.py:23
  135.3 2.0 %stage.5 = bf16[7168,256]{1,0:T(8,128)(2,1)S(1)} custom-call(bf16[7168,256]{1,0:T(8,128)(2,1)} %collective-permute-done.8.refs_0_), custom_call_target="tpu_custom_call" | custom-call | bytes 7340032 | tf_op jit(solution)/shard_map/stage/pallas_call | solution.py:141
  139.6 1.7 collective-permute-done.28
  141.3 2.5 %collective-permute-done.27 = bf16[32,7168]{1,0:T(8,128)(2,1)S(1)} collective-permute-done((bf16[32,7168]{1,0:T(8,128)(2,1)S(1)}, bf16[32,7168]{1,0:T(8,128)(2,1)S(1)}, u32[]{:S(2)}, u32[]{:S(2)}) %collective-permute-start.27) | collective-permute-done | bytes 458784 | tf_op jit(solution)/shard_map/ppermute | solution.py:23
  143.8 2.5 %collective-permute-start.32 = (bf16[32,7168]{1,0:T(8,128)(2,1)S(1)}, bf16[32,7168]{1,0:T(8,128)(2,1)S(1)}, u32[]{:S(2)}, u32[]{:S(2)}) collective-permute-start(bf16[32,7168]{1,0:T(8,128)(2,1)S(1)} %collective-permute-done.28), channel_id=1, source_target_pairs={{0,6},{1,193},{2,0},{3,195},{4,2},{5,197},{6,4},{7,199},{64,70},{6... | collective-permute-start | bytes 1376264 | tf_op jit(solution)/shard_map/ppermute | solution.py:23
  146.3 2.4 %collective-permute-done.29 = bf16[32,7168]{1,0:T(8,128)(2,1)S(1)} collective-permute-done((bf16[32,7168]{1,0:T(8,128)(2,1)S(1)}, bf16[32,7168]{1,0:T(8,128)(2,1)S(1)}, u32[]{:S(2)}, u32[]{:S(2)}) %collective-permute-start.29) | collective-permute-done | bytes 458784 | tf_op jit(solution)/shard_map/ppermute | solution.py:23
  150.6 3.0 %collective-permute-done.31 = bf16[32,7168]{1,0:T(8,128)(2,1)S(1)} collective-permute-done((bf16[32,7168]{1,0:T(8,128)(2,1)S(1)}, bf16[32,7168]{1,0:T(8,128)(2,1)S(1)}, u32[]{:S(2)}, u32[]{:S(2)}) %collective-permute-start.31) | collective-permute-done | bytes 458784 | tf_op jit(solution)/shard_map/ppermute | solution.py:23
  156.2 19.3 %all_to_all.28 = f32[128,1,128]{2,1,0:T(1,128)S(1)} all-to-all(f32[128,1,128]{2,1,0:T(1,128)S(1)} %bitcast.35), channel_id=1, replica_groups=mesh['x'=4,'z'=8,'y'=4,'c'=2] {'x','y','z'}, dimensions={0} | all-to-all | bytes 131072 | tf_op jit(solution)/shard_map/all_to_all | solution.py:320
  (104 shorter events, 33.0 us)
Async XLA Ops:
  0.6 22.7 %collective-permute-start = (bf16[1,7168,192]{1,2,0:T(8,128)(2,1)}, bf16[1,7168,192]{1,2,0:T(8,128)(2,1)}, u32[]{:S(2)}, u32[]{:S(2)}) collective-permute-start(bf16[1,7168,192]{1,2,0:T(8,128)(2,1)} %param.13), channel_id=1, source_target_pairs={{0,1},{1,0},{2,3},{3,2},{4,5},{5,4},{6,7},{7,6},{8,9},{9,8},{10,11... | collective-permute-start | bytes 8257544 | tf_op jit(solution)/shard_map/ppermute | solution.py:27
  0.7 22.6 %collective-permute-start.1 = (bf16[1,7168,192]{1,2,0:T(8,128)(2,1)}, bf16[1,7168,192]{1,2,0:T(8,128)(2,1)}, u32[]{:S(2)}, u32[]{:S(2)}) collective-permute-start(bf16[1,7168,192]{1,2,0:T(8,128)(2,1)} %param.14), channel_id=1, source_target_pairs={{0,1},{1,0},{2,3},{3,2},{4,5},{5,4},{6,7},{7,6},{8,9},{9,8},{10,11... | collective-permute-start | bytes 8257544 | tf_op jit(solution)/shard_map/ppermute | solution.py:27
  1.2 33.7 %collective-permute-start.5 = (bf16[1,192,7168]{2,1,0:T(8,128)(2,1)}, bf16[1,192,7168]{2,1,0:T(8,128)(2,1)}, u32[]{:S(2)}, u32[]{:S(2)}) collective-permute-start(bf16[1,192,7168]{2,1,0:T(8,128)(2,1)} %param.15), channel_id=1, source_target_pairs={{0,1},{1,0},{2,3},{3,2},{4,5},{5,4},{6,7},{7,6},{8,9},{9,8},{10,11... | collective-permute-start | bytes 8257544 | tf_op jit(solution)/shard_map/ppermute | solution.py:27
  3.0 20.2 %all-to-all-start = ((bf16[8,2,7296]{2,1,0:T(2,128)(2,1)}), bf16[8,2,7296]{2,1,0:T(2,128)(2,1)S(1)}, u32[]{:S(2)}, u32[]{:S(2)}) async-start(bf16[8,2,7296]{2,1,0:T(2,128)(2,1)} %spread.1), calls=%async_computation | async-start | bytes 466944 | tf_op jit(solution)/shard_map/all_to_all | solution.py:43
  11.5 33.6 %collective-permute-start.8 = (bf16[7168,256]{1,0:T(8,128)(2,1)}, bf16[7168,256]{1,0:T(8,128)(2,1)}, u32[]{:S(2)}, u32[]{:S(2)}) collective-permute-start(bf16[7168,256]{1,0:T(8,128)(2,1)} %param.17), channel_id=1, source_target_pairs={{0,1},{1,0},{2,3},{3,2},{4,5},{5,4},{6,7},{7,6},{8,9},{9,8},{10,11... | collective-permute-start | bytes 11010056 | tf_op jit(solution)/shard_map/ppermute | solution.py:27
  23.3 11.6 %collective-permute-start.4 = (bf16[16,7296]{1,0:T(8,128)(2,1)S(1)}, bf16[16,7296]{1,0:T(8,128)(2,1)S(1)}, u32[]{:S(2)}, u32[]{:S(2)}) collective-permute-start(bf16[16,7296]{1,0:T(8,128)(2,1)S(1)} %reshape.40), channel_id=1, source_target_pairs={{0,128},{1,5},{2,130},{3,7},{4,132},{5,1},{6,134},{7,3},{64,192},{... | collective-permute-start | bytes 700424 | tf_op jit(solution)/shard_map/ppermute | solution.py:23
  26.4 8.5 %collective-permute-start.3 = (bf16[16,7296]{1,0:T(8,128)(2,1)S(1)}, bf16[16,7296]{1,0:T(8,128)(2,1)S(1)}, u32[]{:S(2)}, u32[]{:S(2)}) collective-permute-start(bf16[16,7296]{1,0:T(8,128)(2,1)S(1)} %reshape.40), channel_id=1, source_target_pairs={{0,192},{1,7},{2,194},{3,1},{4,196},{5,3},{6,198},{7,5},{64,0},{65... | collective-permute-start | bytes 700424 | tf_op jit(solution)/shard_map/ppermute | solution.py:23
  27.6 7.3 %collective-permute-start.2 = (bf16[16,7296]{1,0:T(8,128)(2,1)S(1)}, bf16[16,7296]{1,0:T(8,128)(2,1)S(1)}, u32[]{:S(2)}, u32[]{:S(2)}) collective-permute-start(bf16[16,7296]{1,0:T(8,128)(2,1)S(1)} %reshape.40), channel_id=1, source_target_pairs={{0,64},{1,3},{2,66},{3,5},{4,68},{5,7},{6,70},{7,1},{64,128},{65,6... | collective-permute-start | bytes 700424 | tf_op jit(solution)/shard_map/ppermute | solution.py:23
  35.0 8.6 %collective-permute-start.7 = (bf16[32,7296]{1,0:T(8,128)(2,1)S(1)}, bf16[32,7296]{1,0:T(8,128)(2,1)S(1)}, u32[]{:S(2)}, u32[]{:S(2)}) collective-permute-start(bf16[32,7296]{1,0:T(8,128)(2,1)S(1)} %get-tuple-element.42), channel_id=1, source_target_pairs={{0,6},{1,193},{2,0},{3,195},{4,2},{5,197},{6,4},{7,199},{64,70},{6... | collective-permute-start | bytes 1400840 | tf_op jit(solution)/shard_map/ppermute | solution.py:23
  35.5 9.6 %collective-permute-start.6 = (bf16[32,7296]{1,0:T(8,128)(2,1)S(1)}, bf16[32,7296]{1,0:T(8,128)(2,1)S(1)}, u32[]{:S(2)}, u32[]{:S(2)}) collective-permute-start(bf16[32,7296]{1,0:T(8,128)(2,1)S(1)} %get-tuple-element.43), channel_id=1, source_target_pairs={{0,2},{1,65},{2,4},{3,67},{4,6},{5,69},{6,0},{7,71},{64,66},{65,12... | collective-permute-start | bytes 1400840 | tf_op jit(solution)/shard_map/ppermute | solution.py:23
  39.4 12.0 %collective-permute-start.9 = (bf16[32,7296]{1,0:T(8,128)(2,1)S(1)}, bf16[32,7296]{1,0:T(8,128)(2,1)S(1)}, u32[]{:S(2)}, u32[]{:S(2)}) collective-permute-start(bf16[32,7296]{1,0:T(8,128)(2,1)S(1)} %get-tuple-element.42), channel_id=1, source_target_pairs={{0,2},{1,65},{2,4},{3,67},{4,6},{5,69},{6,0},{7,71},{64,66},{65,12... | collective-permute-start | bytes 1400840 | tf_op jit(solution)/shard_map/ppermute | solution.py:23
  41.1 10.4 %collective-permute-start.10 = (bf16[32,7296]{1,0:T(8,128)(2,1)S(1)}, bf16[32,7296]{1,0:T(8,128)(2,1)S(1)}, u32[]{:S(2)}, u32[]{:S(2)}) collective-permute-start(bf16[32,7296]{1,0:T(8,128)(2,1)S(1)} %get-tuple-element.43), channel_id=1, source_target_pairs={{0,6},{1,193},{2,0},{3,195},{4,2},{5,197},{6,4},{7,199},{64,70},{6... | collective-permute-start | bytes 1400840 | tf_op jit(solution)/shard_map/ppermute | solution.py:23
  45.1 10.0 %collective-permute-start.11 = (bf16[32,7296]{1,0:T(8,128)(2,1)S(1)}, bf16[32,7296]{1,0:T(8,128)(2,1)S(1)}, u32[]{:S(2)}, u32[]{:S(2)}) collective-permute-start(bf16[32,7296]{1,0:T(8,128)(2,1)S(1)} %collective-permute-done.6), channel_id=1, source_target_pairs={{0,2},{1,65},{2,4},{3,67},{4,6},{5,69},{6,0},{7,71},{64,66},{65,12... | collective-permute-start | bytes 1400840 | tf_op jit(solution)/shard_map/ppermute | solution.py:23
  45.7 9.5 %collective-permute-start.12 = (bf16[32,7296]{1,0:T(8,128)(2,1)S(1)}, bf16[32,7296]{1,0:T(8,128)(2,1)S(1)}, u32[]{:S(2)}, u32[]{:S(2)}) collective-permute-start(bf16[32,7296]{1,0:T(8,128)(2,1)S(1)} %collective-permute-done.7), channel_id=1, source_target_pairs={{0,6},{1,193},{2,0},{3,195},{4,2},{5,197},{6,4},{7,199},{64,70},{6... | collective-permute-start | bytes 1400840 | tf_op jit(solution)/shard_map/ppermute | solution.py:23
  60.8 9.8 %collective-permute-start.15 = (bf16[32,7168]{1,0:T(8,128)(2,1)S(1)}, bf16[32,7168]{1,0:T(8,128)(2,1)S(1)}, u32[]{:S(2)}, u32[]{:S(2)}) collective-permute-start(bf16[32,7168]{1,0:T(8,128)(2,1)S(1)} %get-tuple-element.72), channel_id=1, source_target_pairs={{0,2},{1,65},{2,4},{3,67},{4,6},{5,69},{6,0},{7,71},{64,66},{65,12... | collective-permute-start | bytes 1376264 | tf_op jit(solution)/shard_map/ppermute | solution.py:23
  63.2 9.7 %collective-permute-start.14 = (bf16[32,7168]{1,0:T(8,128)(2,1)S(1)}, bf16[32,7168]{1,0:T(8,128)(2,1)S(1)}, u32[]{:S(2)}, u32[]{:S(2)}) collective-permute-start(bf16[32,7168]{1,0:T(8,128)(2,1)S(1)} %get-tuple-element.73), channel_id=1, source_target_pairs={{0,6},{1,193},{2,0},{3,195},{4,2},{5,197},{6,4},{7,199},{64,70},{6... | collective-permute-start | bytes 1376264 | tf_op jit(solution)/shard_map/ppermute | solution.py:23
  64.2 11.3 %collective-permute-start.17 = (bf16[32,7168]{1,0:T(8,128)(2,1)S(1)}, bf16[32,7168]{1,0:T(8,128)(2,1)S(1)}, u32[]{:S(2)}, u32[]{:S(2)}) collective-permute-start(bf16[32,7168]{1,0:T(8,128)(2,1)S(1)} %get-tuple-element.70), channel_id=1, source_target_pairs={{0,2},{1,65},{2,4},{3,67},{4,6},{5,69},{6,0},{7,71},{64,66},{65,12... | collective-permute-start | bytes 1376264 | tf_op jit(solution)/shard_map/ppermute | solution.py:23
  66.4 11.4 %collective-permute-start.19 = (bf16[32,7168]{1,0:T(8,128)(2,1)S(1)}, bf16[32,7168]{1,0:T(8,128)(2,1)S(1)}, u32[]{:S(2)}, u32[]{:S(2)}) collective-permute-start(bf16[32,7168]{1,0:T(8,128)(2,1)S(1)} %get-tuple-element.71), channel_id=1, source_target_pairs={{0,6},{1,193},{2,0},{3,195},{4,2},{5,197},{6,4},{7,199},{64,70},{6... | collective-permute-start | bytes 1376264 | tf_op jit(solution)/shard_map/ppermute | solution.py:23
  73.1 9.6 %collective-permute-start.16 = (bf16[32,7168]{1,0:T(8,128)(2,1)S(1)}, bf16[32,7168]{1,0:T(8,128)(2,1)S(1)}, u32[]{:S(2)}, u32[]{:S(2)}) collective-permute-start(bf16[32,7168]{1,0:T(8,128)(2,1)S(1)} %get-tuple-element.53), channel_id=1, source_target_pairs={{0,6},{1,193},{2,0},{3,195},{4,2},{5,197},{6,4},{7,199},{64,70},{6... | collective-permute-start | bytes 1376264 | tf_op jit(solution)/shard_map/ppermute | solution.py:23
  74.1 9.7 %collective-permute-start.20 = (bf16[32,7168]{1,0:T(8,128)(2,1)S(1)}, bf16[32,7168]{1,0:T(8,128)(2,1)S(1)}, u32[]{:S(2)}, u32[]{:S(2)}) collective-permute-start(bf16[32,7168]{1,0:T(8,128)(2,1)S(1)} %get-tuple-element.54), channel_id=1, source_target_pairs={{0,2},{1,65},{2,4},{3,67},{4,6},{5,69},{6,0},{7,71},{64,66},{65,12... | collective-permute-start | bytes 1376264 | tf_op jit(solution)/shard_map/ppermute | solution.py:23
  84.2 7.6 %collective-permute-start.22 = (bf16[16,7168]{1,0:T(8,128)(2,1)S(1)}, bf16[16,7168]{1,0:T(8,128)(2,1)S(1)}, u32[]{:S(2)}, u32[]{:S(2)}) collective-permute-start(bf16[16,7168]{1,0:T(8,128)(2,1)S(1)} %get-tuple-element.77), channel_id=1, source_target_pairs={{0,128},{1,5},{2,130},{3,7},{4,132},{5,1},{6,134},{7,3},{64,192},{... | collective-permute-start | bytes 688136 | tf_op jit(solution)/shard_map/ppermute | solution.py:23
  85.9 7.0 %collective-permute-start.18 = (bf16[16,7168]{1,0:T(8,128)(2,1)S(1)}, bf16[16,7168]{1,0:T(8,128)(2,1)S(1)}, u32[]{:S(2)}, u32[]{:S(2)}) collective-permute-start(bf16[16,7168]{1,0:T(8,128)(2,1)S(1)} %slice.57), channel_id=1, source_target_pairs={{0,192},{1,7},{2,194},{3,1},{4,196},{5,3},{6,198},{7,5},{64,0},{65... | collective-permute-start | bytes 688136 | tf_op jit(solution)/shard_map/ppermute | solution.py:23
  87.1 7.2 %collective-permute-start.21 = (bf16[16,7168]{1,0:T(8,128)(2,1)S(1)}, bf16[16,7168]{1,0:T(8,128)(2,1)S(1)}, u32[]{:S(2)}, u32[]{:S(2)}) collective-permute-start(bf16[16,7168]{1,0:T(8,128)(2,1)S(1)} %get-tuple-element.76), channel_id=1, source_target_pairs={{0,64},{1,3},{2,66},{3,5},{4,68},{5,7},{6,70},{7,1},{64,128},{65,6... | collective-permute-start | bytes 688136 | tf_op jit(solution)/shard_map/ppermute | solution.py:23
  122.2 10.0 %collective-permute-start.26 = (bf16[16,7168]{1,0:T(8,128)(2,1)S(1)}, bf16[16,7168]{1,0:T(8,128)(2,1)S(1)}, u32[]{:S(2)}, u32[]{:S(2)}) collective-permute-start(bf16[16,7168]{1,0:T(8,128)(2,1)S(1)} %reshape.42), channel_id=1, source_target_pairs={{0,128},{1,5},{2,130},{3,7},{4,132},{5,1},{6,134},{7,3},{64,192},{... | collective-permute-start | bytes 688136 | tf_op jit(solution)/shard_map/ppermute | solution.py:23
  123.5 8.8 %collective-permute-start.25 = (bf16[16,7168]{1,0:T(8,128)(2,1)S(1)}, bf16[16,7168]{1,0:T(8,128)(2,1)S(1)}, u32[]{:S(2)}, u32[]{:S(2)}) collective-permute-start(bf16[16,7168]{1,0:T(8,128)(2,1)S(1)} %reshape.42), channel_id=1, source_target_pairs={{0,192},{1,7},{2,194},{3,1},{4,196},{5,3},{6,198},{7,5},{64,0},{65... | collective-permute-start | bytes 688136 | tf_op jit(solution)/shard_map/ppermute | solution.py:23
  124.7 7.5 %collective-permute-start.24 = (bf16[16,7168]{1,0:T(8,128)(2,1)S(1)}, bf16[16,7168]{1,0:T(8,128)(2,1)S(1)}, u32[]{:S(2)}, u32[]{:S(2)}) collective-permute-start(bf16[16,7168]{1,0:T(8,128)(2,1)S(1)} %reshape.42), channel_id=1, source_target_pairs={{0,64},{1,3},{2,66},{3,5},{4,68},{5,7},{6,70},{7,1},{64,128},{65,6... | collective-permute-start | bytes 688136 | tf_op jit(solution)/shard_map/ppermute | solution.py:23
  132.3 9.0 %collective-permute-start.28 = (bf16[32,7168]{1,0:T(8,128)(2,1)S(1)}, bf16[32,7168]{1,0:T(8,128)(2,1)S(1)}, u32[]{:S(2)}, u32[]{:S(2)}) collective-permute-start(bf16[32,7168]{1,0:T(8,128)(2,1)S(1)} %get-tuple-element.60), channel_id=1, source_target_pairs={{0,6},{1,193},{2,0},{3,195},{4,2},{5,197},{6,4},{7,199},{64,70},{6... | collective-permute-start | bytes 1376264 | tf_op jit(solution)/shard_map/ppermute | solution.py:23
  135.3 8.5 %collective-permute-start.27 = (bf16[32,7168]{1,0:T(8,128)(2,1)S(1)}, bf16[32,7168]{1,0:T(8,128)(2,1)S(1)}, u32[]{:S(2)}, u32[]{:S(2)}) collective-permute-start(bf16[32,7168]{1,0:T(8,128)(2,1)S(1)} %get-tuple-element.61), channel_id=1, source_target_pairs={{0,2},{1,65},{2,4},{3,67},{4,6},{5,69},{6,0},{7,71},{64,66},{65,12... | collective-permute-start | bytes 1376264 | tf_op jit(solution)/shard_map/ppermute | solution.py:23
  137.4 11.3 %collective-permute-start.29 = (bf16[32,7168]{1,0:T(8,128)(2,1)S(1)}, bf16[32,7168]{1,0:T(8,128)(2,1)S(1)}, u32[]{:S(2)}, u32[]{:S(2)}) collective-permute-start(bf16[32,7168]{1,0:T(8,128)(2,1)S(1)} %get-tuple-element.60), channel_id=1, source_target_pairs={{0,2},{1,65},{2,4},{3,67},{4,6},{5,69},{6,0},{7,71},{64,66},{65,12... | collective-permute-start | bytes 1376264 | tf_op jit(solution)/shard_map/ppermute | solution.py:23
  138.2 10.5 %collective-permute-start.30 = (bf16[32,7168]{1,0:T(8,128)(2,1)S(1)}, bf16[32,7168]{1,0:T(8,128)(2,1)S(1)}, u32[]{:S(2)}, u32[]{:S(2)}) collective-permute-start(bf16[32,7168]{1,0:T(8,128)(2,1)S(1)} %get-tuple-element.61), channel_id=1, source_target_pairs={{0,6},{1,193},{2,0},{3,195},{4,2},{5,197},{6,4},{7,199},{64,70},{6... | collective-permute-start | bytes 1376264 | tf_op jit(solution)/shard_map/ppermute | solution.py:23
  143.8 9.8 %collective-permute-start.31 = (bf16[32,7168]{1,0:T(8,128)(2,1)S(1)}, bf16[32,7168]{1,0:T(8,128)(2,1)S(1)}, u32[]{:S(2)}, u32[]{:S(2)}) collective-permute-start(bf16[32,7168]{1,0:T(8,128)(2,1)S(1)} %collective-permute-done.27), channel_id=1, source_target_pairs={{0,2},{1,65},{2,4},{3,67},{4,6},{5,69},{6,0},{7,71},{64,66},{65,12... | collective-permute-start | bytes 1376264 | tf_op jit(solution)/shard_map/ppermute | solution.py:23
  143.8 9.9 %collective-permute-start.32 = (bf16[32,7168]{1,0:T(8,128)(2,1)S(1)}, bf16[32,7168]{1,0:T(8,128)(2,1)S(1)}, u32[]{:S(2)}, u32[]{:S(2)}) collective-permute-start(bf16[32,7168]{1,0:T(8,128)(2,1)S(1)} %collective-permute-done.28), channel_id=1, source_target_pairs={{0,6},{1,193},{2,0},{3,195},{4,2},{5,197},{6,4},{7,199},{64,70},{6... | collective-permute-start | bytes 1376264 | tf_op jit(solution)/shard_map/ppermute | solution.py:23
  (9 other events, 173.1 us)

commit v6 on v5

--- a/solution.py
+++ b/solution.py
@@ -312,7 +312,7 @@
     normed = (widened * inverse * norm_gain).astype(jnp.bfloat16)
 
     column = column_rows(jnp.broadcast_to(normed[None], (depth,) + normed.shape))
-    column, second_sign = together(column, swap(column))
+    column, second_sign = together(column, swap(column[:, :META]))
     wide, head = first_axis_rows(column, head)
     near, far, head = second_axis_rows(wide, stage(head))
     logits = [[product(part, weight) for weight in (head_weight, head)] for part in (near, far)]

time: 177 us -> 177 us (level)
  no operation moved by 1% of the time
where the time goes in v6:
time: 177 us; the launch traced here: 176 us
  waiting for transfers between devices  61.9 us (35%)
  starting transfers between devices  45.6 us (26%)
  blocking collectives  44.7 us (25%)
  Pallas kernels  14 us (8%)
  matrix products  5.27 us (3%)
  other arithmetic  2.03 us (1%)
    ppermute x27, waiting for transfers between devices, move(): return lax.ppermute(value, PLANE, pairs)  50.1 us
    ppermute x27, starting transfers between devices, move(): return lax.ppermute(value, PLANE, pairs)  36.1 us
    all_to_all x1, blocking collectives, shards(): arrived = lax.all_to_all(stats, ('x', 'y', 'z'), 0, 0, tiled=True)  19.3 us
    all_to_all x1, blocking collectives, fold_column(): lax.all_to_all(partial.reshape(depth, 2, width), 'z', 0, 0, tiled=True)  12.8 us
    all_to_all x1, blocking collectives, column_rows(): lax.all_to_all(spread, 'z', 0, 0, tiled=True).reshape(depth * rows, width)  12.5 us
    all_to_all x1, waiting for transfers between devices, column_rows(): lax.all_to_all(spread, 'z', 0, 0, tiled=True).reshape(depth * rows, width)  10.6 us
    all_to_all x1, starting transfers between devices, column_rows(): lax.all_to_all(spread, 'z', 0, 0, tiled=True).reshape(depth * rows, width)  8.47 us
    pallas_call x3, Pallas kernels, stage(): pl.pallas_call(stage_kernel, out_shape=pltpu.VMEM(shape, weights[0].dtype...  7.43 us
  transfers between devices with their start and end apart: 34, of which 20 were waited for; matrix products, arithmetic and copies ran while one was open for 3% of the time, Pallas kernels for 5%

profile of v6, /device:TPU:8, one launch (start us, length us, event | category | flops | bytes accessed | tf_op | source)
XLA Modules:
  0.0 176.2 jit_solution(13126167736374816980)
XLA Ops:
  1.3 1.7 spread.1
  3.0 8.5 %all-to-all-start = ((bf16[8,2,7296]{2,1,0:T(2,128)(2,1)}), bf16[8,2,7296]{2,1,0:T(2,128)(2,1)S(1)}, u32[]{:S(2)}, u32[]{:S(2)}) async-start(bf16[8,2,7296]{2,1,0:T(2,128)(2,1)} %spread.1), calls=%async_computation | async-start | bytes 466944 | tf_op jit(solution)/shard_map/all_to_all | solution.py:43
  12.6 10.6 %all-to-all-done = bf16[8,2,7296]{2,1,0:T(2,128)(2,1)S(1)} async-done(((bf16[8,2,7296]{2,1,0:T(2,128)(2,1)}), bf16[8,2,7296]{2,1,0:T(2,128)(2,1)S(1)}, u32[]{:S(2)}, u32[]{:S(2)}) %all-to-all-start) | async-done | bytes 233504 | tf_op jit(solution)/shard_map/all_to_all | solution.py:43
  23.3 3.1 %collective-permute-start.4 = (bf16[16,7296]{1,0:T(8,128)(2,1)S(1)}, bf16[16,7296]{1,0:T(8,128)(2,1)S(1)}, u32[]{:S(2)}, u32[]{:S(2)}) collective-permute-start(bf16[16,7296]{1,0:T(8,128)(2,1)S(1)} %reshape.40), channel_id=1, source_target_pairs={{0,128},{1,5},{2,130},{3,7},{4,132},{5,1},{6,134},{7,3},{64,192},{... | collective-permute-start | bytes 700424 | tf_op jit(solution)/shard_map/ppermute | solution.py:23
  28.5 6.4 %collective-permute-done.2 = bf16[16,7296]{1,0:T(8,128)(2,1)S(1)} collective-permute-done((bf16[16,7296]{1,0:T(8,128)(2,1)S(1)}, bf16[16,7296]{1,0:T(8,128)(2,1)S(1)}, u32[]{:S(2)}, u32[]{:S(2)}) %collective-permute-start.2) | collective-permute-done | bytes 233504 | tf_op jit(solution)/shard_map/ppermute | solution.py:23
  37.1 2.3 %stage.3 = bf16[384,7168]{1,0:T(8,128)(2,1)S(1)} custom-call(bf16[192,7168]{1,0:T(8,128)(2,1)S(1)} %bitcast.31, bf16[192,7168]{1,0:T(8,128)(2,1)} %bitcast.4.refs_1_), custom_call_target="tpu_custom_call" | custom-call | bytes 11010048 | tf_op jit(solution)/shard_map/stage/pallas_call | solution.py:141
  39.4 1.7 collective-permute-start.9
  41.5 2.1 %collective-permute-done.7 = bf16[32,7296]{1,0:T(8,128)(2,1)S(1)} collective-permute-done((bf16[32,7296]{1,0:T(8,128)(2,1)S(1)}, bf16[32,7296]{1,0:T(8,128)(2,1)S(1)}, u32[]{:S(2)}, u32[]{:S(2)}) %collective-permute-start.7) | collective-permute-done | bytes 466976 | tf_op jit(solution)/shard_map/ppermute | solution.py:23
  45.7 2.7 %collective-permute-start.12 = (bf16[32,7296]{1,0:T(8,128)(2,1)S(1)}, bf16[32,7296]{1,0:T(8,128)(2,1)S(1)}, u32[]{:S(2)}, u32[]{:S(2)}) collective-permute-start(bf16[32,7296]{1,0:T(8,128)(2,1)S(1)} %collective-permute-done.7), channel_id=1, source_target_pairs={{0,6},{1,193},{2,0},{3,195},{4,2},{5,197},{6,4},{7,199},{64,70},{6... | collective-permute-start | bytes 1400840 | tf_op jit(solution)/shard_map/ppermute | solution.py:23
  48.4 3.1 %stage.4.in_ref = bf16[768,7168]{1,0:T(8,128)(2,1)S(1)} custom-call(bf16[192,7168]{1,0:T(8,128)(2,1)S(1)} %bitcast.32, bf16[192,7168]{1,0:T(8,128)(2,1)} %bitcast.8.refs_1_, bf16[192,7168]{1,0:T(8,128)(2,1)S(1)} %bitcast.33, bf16[192,7168]{1,0:T(8,128)(2,1)} %bitcast.12.refs_3_), custom_call_target="tpu_custom_call" | custom-call | bytes 22020096 | tf_op jit(solution)/shard_map/stage/pallas_call | solution.py:141
  51.6 3.5 %collective-permute-done.11 = bf16[32,7296]{1,0:T(8,128)(2,1)S(1)} collective-permute-done((bf16[32,7296]{1,0:T(8,128)(2,1)S(1)}, bf16[32,7296]{1,0:T(8,128)(2,1)S(1)}, u32[]{:S(2)}, u32[]{:S(2)}) %collective-permute-start.11) | collective-permute-done | bytes 466976 | tf_op jit(solution)/shard_map/ppermute | solution.py:23
  55.2 3.1 %expert.1 = (bf16[256,384]{1,0:T(8,128)(2,1)S(1)}, f32[256,128]{1,0:T(8,128)S(1)}) custom-call(s32[1]{0:T(128)} %bitcast.2.expert_ref, bf16[256,7296]{1,0:T(8,128)(2,1)S(1)} %constant_dynamic-update-slice_fusion.4.row_ref, bf16[768,7168]{1,0:T(8,128)(2,1)S(1)} %stage.4.in_ref), custom_call_target="tpu_custom_call" | custom-call | flops 2818572288 | bytes 14680064 | tf_op jit(solution)/shard_map/expert/pallas_call | solution.py:178
  58.5 2.1 %convolution_convert_fusion = bf16[256,7168]{1,0:T(8,128)(2,1)S(1)} fusion(bf16[256,384]{1,0:T(8,128)(2,1)S(1)} %get-tuple-element.47, bf16[384,7168]{1,0:T(8,128)(2,1)S(1)} %stage.3), kind=kOutput, calls=%fused_computation | convolution fusion | flops 1411121152 | bytes 9371648 | tf_op jit(solution)/shard_map/dot_general | solution.py:273
  60.8 2.4 %collective-permute-start.15 = (bf16[32,7168]{1,0:T(8,128)(2,1)S(1)}, bf16[32,7168]{1,0:T(8,128)(2,1)S(1)}, u32[]{:S(2)}, u32[]{:S(2)}) collective-permute-start(bf16[32,7168]{1,0:T(8,128)(2,1)S(1)} %get-tuple-element.72), channel_id=1, source_target_pairs={{0,2},{1,65},{2,4},{3,67},{4,6},{5,69},{6,0},{7,71},{64,66},{65,12... | collective-permute-start | bytes 1376264 | tf_op jit(solution)/shard_map/ppermute | solution.py:23
  64.2 2.3 %collective-permute-start.17 = (bf16[32,7168]{1,0:T(8,128)(2,1)S(1)}, bf16[32,7168]{1,0:T(8,128)(2,1)S(1)}, u32[]{:S(2)}, u32[]{:S(2)}) collective-permute-start(bf16[32,7168]{1,0:T(8,128)(2,1)S(1)} %get-tuple-element.70), channel_id=1, source_target_pairs={{0,2},{1,65},{2,4},{3,67},{4,6},{5,69},{6,0},{7,71},{64,66},{65,12... | collective-permute-start | bytes 1376264 | tf_op jit(solution)/shard_map/ppermute | solution.py:23
  67.3 3.2 %collective-permute-done.15 = bf16[32,7168]{1,0:T(8,128)(2,1)S(1)} collective-permute-done((bf16[32,7168]{1,0:T(8,128)(2,1)S(1)}, bf16[32,7168]{1,0:T(8,128)(2,1)S(1)}, u32[]{:S(2)}, u32[]{:S(2)}) %collective-permute-start.15) | collective-permute-done | bytes 458784 | tf_op jit(solution)/shard_map/ppermute | solution.py:23
  70.5 2.3 %collective-permute-done.14 = bf16[32,7168]{1,0:T(8,128)(2,1)S(1)} collective-permute-done((bf16[32,7168]{1,0:T(8,128)(2,1)S(1)}, bf16[32,7168]{1,0:T(8,128)(2,1)S(1)}, u32[]{:S(2)}, u32[]{:S(2)}) %collective-permute-start.14) | collective-permute-done | bytes 458784 | tf_op jit(solution)/shard_map/ppermute | solution.py:23
  75.5 2.3 %collective-permute-done.19 = bf16[32,7168]{1,0:T(8,128)(2,1)S(1)} collective-permute-done((bf16[32,7168]{1,0:T(8,128)(2,1)S(1)}, bf16[32,7168]{1,0:T(8,128)(2,1)S(1)}, u32[]{:S(2)}, u32[]{:S(2)}) %collective-permute-start.19) | collective-permute-done | bytes 458784 | tf_op jit(solution)/shard_map/ppermute | solution.py:23
  77.8 4.9 %collective-permute-done.16 = bf16[32,7168]{1,0:T(8,128)(2,1)S(1)} collective-permute-done((bf16[32,7168]{1,0:T(8,128)(2,1)S(1)}, bf16[32,7168]{1,0:T(8,128)(2,1)S(1)}, u32[]{:S(2)}, u32[]{:S(2)}) %collective-permute-start.16) | collective-permute-done | bytes 458784 | tf_op jit(solution)/shard_map/ppermute | solution.py:23
  84.2 1.7 collective-permute-start.22
  88.0 3.8 %collective-permute-done.22 = bf16[16,7168]{1,0:T(8,128)(2,1)S(1)} collective-permute-done((bf16[16,7168]{1,0:T(8,128)(2,1)S(1)}, bf16[16,7168]{1,0:T(8,128)(2,1)S(1)}, u32[]{:S(2)}, u32[]{:S(2)}) %collective-permute-start.22) | collective-permute-done | bytes 229408 | tf_op jit(solution)/shard_map/ppermute | solution.py:23
  94.5 12.8 %all_to_all.26 = bf16[8,2,7168]{2,1,0:T(2,128)(2,1)S(1)} all-to-all(bf16[8,2,7168]{2,1,0:T(2,128)(2,1)S(1)} %reshape.41), channel_id=1, replica_groups=mesh['x'=4,'z'=8,'y'=4,'c'=2] {'z'}, dimensions={0} | all-to-all | bytes 458752 | tf_op jit(solution)/shard_map/all_to_all | solution.py:91
  108.0 12.5 %all_to_all.27 = bf16[8,2,7168]{2,1,0:T(2,128)(2,1)S(1)} all-to-all(bf16[8,2,7168]{2,1,0:T(2,128)(2,1)S(1)} %broadcast_in_dim.52), channel_id=1, replica_groups=mesh['x'=4,'z'=8,'y'=4,'c'=2] {'z'}, dimensions={0} | all-to-all | bytes 458752 | tf_op jit(solution)/shard_map/all_to_all | solution.py:43
  125.2 6.6 %collective-permute-done.24 = bf16[16,7168]{1,0:T(8,128)(2,1)S(1)} collective-permute-done((bf16[16,7168]{1,0:T(8,128)(2,1)S(1)}, bf16[16,7168]{1,0:T(8,128)(2,1)S(1)}, u32[]{:S(2)}, u32[]{:S(2)}) %collective-permute-start.24) | collective-permute-done | bytes 229408 | tf_op jit(solution)/shard_map/ppermute | solution.py:23
  132.0 3.0 %collective-permute-start.28 = (bf16[32,7168]{1,0:T(8,128)(2,1)S(1)}, bf16[32,7168]{1,0:T(8,128)(2,1)S(1)}, u32[]{:S(2)}, u32[]{:S(2)}) collective-permute-start(bf16[32,7168]{1,0:T(8,128)(2,1)S(1)} %get-tuple-element.60), channel_id=1, source_target_pairs={{0,6},{1,193},{2,0},{3,195},{4,2},{5,197},{6,4},{7,199},{64,70},{6... | collective-permute-start | bytes 1376264 | tf_op jit(solution)/shard_map/ppermute | solution.py:23
  135.0 2.0 %stage.5 = bf16[7168,256]{1,0:T(8,128)(2,1)S(1)} custom-call(bf16[7168,256]{1,0:T(8,128)(2,1)} %collective-permute-done.8.refs_0_), custom_call_target="tpu_custom_call" | custom-call | bytes 7340032 | tf_op jit(solution)/shard_map/stage/pallas_call | solution.py:141
  139.3 1.7 collective-permute-done.28
  141.0 2.5 %collective-permute-done.27 = bf16[32,7168]{1,0:T(8,128)(2,1)S(1)} collective-permute-done((bf16[32,7168]{1,0:T(8,128)(2,1)S(1)}, bf16[32,7168]{1,0:T(8,128)(2,1)S(1)}, u32[]{:S(2)}, u32[]{:S(2)}) %collective-permute-start.27) | collective-permute-done | bytes 458784 | tf_op jit(solution)/shard_map/ppermute | solution.py:23
  143.5 2.5 %collective-permute-start.32 = (bf16[32,7168]{1,0:T(8,128)(2,1)S(1)}, bf16[32,7168]{1,0:T(8,128)(2,1)S(1)}, u32[]{:S(2)}, u32[]{:S(2)}) collective-permute-start(bf16[32,7168]{1,0:T(8,128)(2,1)S(1)} %collective-permute-done.28), channel_id=1, source_target_pairs={{0,6},{1,193},{2,0},{3,195},{4,2},{5,197},{6,4},{7,199},{64,70},{6... | collective-permute-start | bytes 1376264 | tf_op jit(solution)/shard_map/ppermute | solution.py:23
  146.0 2.4 %collective-permute-done.29 = bf16[32,7168]{1,0:T(8,128)(2,1)S(1)} collective-permute-done((bf16[32,7168]{1,0:T(8,128)(2,1)S(1)}, bf16[32,7168]{1,0:T(8,128)(2,1)S(1)}, u32[]{:S(2)}, u32[]{:S(2)}) %collective-permute-start.29) | collective-permute-done | bytes 458784 | tf_op jit(solution)/shard_map/ppermute | solution.py:23
  150.3 3.0 %collective-permute-done.31 = bf16[32,7168]{1,0:T(8,128)(2,1)S(1)} collective-permute-done((bf16[32,7168]{1,0:T(8,128)(2,1)S(1)}, bf16[32,7168]{1,0:T(8,128)(2,1)S(1)}, u32[]{:S(2)}, u32[]{:S(2)}) %collective-permute-start.31) | collective-permute-done | bytes 458784 | tf_op jit(solution)/shard_map/ppermute | solution.py:23
  155.9 19.3 %all_to_all.28 = f32[128,1,128]{2,1,0:T(1,128)S(1)} all-to-all(f32[128,1,128]{2,1,0:T(1,128)S(1)} %bitcast.34), channel_id=1, replica_groups=mesh['x'=4,'z'=8,'y'=4,'c'=2] {'x','y','z'}, dimensions={0} | all-to-all | bytes 131072 | tf_op jit(solution)/shard_map/all_to_all | solution.py:320
  (105 shorter events, 32.7 us)
Async XLA Ops:
  0.6 22.7 %collective-permute-start = (bf16[1,7168,192]{1,2,0:T(8,128)(2,1)}, bf16[1,7168,192]{1,2,0:T(8,128)(2,1)}, u32[]{:S(2)}, u32[]{:S(2)}) collective-permute-start(bf16[1,7168,192]{1,2,0:T(8,128)(2,1)} %param.13), channel_id=1, source_target_pairs={{0,1},{1,0},{2,3},{3,2},{4,5},{5,4},{6,7},{7,6},{8,9},{9,8},{10,11... | collective-permute-start | bytes 8257544 | tf_op jit(solution)/shard_map/ppermute | solution.py:27
  0.7 22.6 %collective-permute-start.1 = (bf16[1,7168,192]{1,2,0:T(8,128)(2,1)}, bf16[1,7168,192]{1,2,0:T(8,128)(2,1)}, u32[]{:S(2)}, u32[]{:S(2)}) collective-permute-start(bf16[1,7168,192]{1,2,0:T(8,128)(2,1)} %param.14), channel_id=1, source_target_pairs={{0,1},{1,0},{2,3},{3,2},{4,5},{5,4},{6,7},{7,6},{8,9},{9,8},{10,11... | collective-permute-start | bytes 8257544 | tf_op jit(solution)/shard_map/ppermute | solution.py:27
  1.2 33.7 %collective-permute-start.5 = (bf16[1,192,7168]{2,1,0:T(8,128)(2,1)}, bf16[1,192,7168]{2,1,0:T(8,128)(2,1)}, u32[]{:S(2)}, u32[]{:S(2)}) collective-permute-start(bf16[1,192,7168]{2,1,0:T(8,128)(2,1)} %param.15), channel_id=1, source_target_pairs={{0,1},{1,0},{2,3},{3,2},{4,5},{5,4},{6,7},{7,6},{8,9},{9,8},{10,11... | collective-permute-start | bytes 8257544 | tf_op jit(solution)/shard_map/ppermute | solution.py:27
  3.0 20.2 %all-to-all-start = ((bf16[8,2,7296]{2,1,0:T(2,128)(2,1)}), bf16[8,2,7296]{2,1,0:T(2,128)(2,1)S(1)}, u32[]{:S(2)}, u32[]{:S(2)}) async-start(bf16[8,2,7296]{2,1,0:T(2,128)(2,1)} %spread.1), calls=%async_computation | async-start | bytes 466944 | tf_op jit(solution)/shard_map/all_to_all | solution.py:43
  11.5 33.6 %collective-permute-start.8 = (bf16[7168,256]{1,0:T(8,128)(2,1)}, bf16[7168,256]{1,0:T(8,128)(2,1)}, u32[]{:S(2)}, u32[]{:S(2)}) collective-permute-start(bf16[7168,256]{1,0:T(8,128)(2,1)} %param.17), channel_id=1, source_target_pairs={{0,1},{1,0},{2,3},{3,2},{4,5},{5,4},{6,7},{7,6},{8,9},{9,8},{10,11... | collective-permute-start | bytes 11010056 | tf_op jit(solution)/shard_map/ppermute | solution.py:27
  23.3 11.6 %collective-permute-start.4 = (bf16[16,7296]{1,0:T(8,128)(2,1)S(1)}, bf16[16,7296]{1,0:T(8,128)(2,1)S(1)}, u32[]{:S(2)}, u32[]{:S(2)}) collective-permute-start(bf16[16,7296]{1,0:T(8,128)(2,1)S(1)} %reshape.40), channel_id=1, source_target_pairs={{0,128},{1,5},{2,130},{3,7},{4,132},{5,1},{6,134},{7,3},{64,192},{... | collective-permute-start | bytes 700424 | tf_op jit(solution)/shard_map/ppermute | solution.py:23
  26.4 8.5 %collective-permute-start.3 = (bf16[16,7296]{1,0:T(8,128)(2,1)S(1)}, bf16[16,7296]{1,0:T(8,128)(2,1)S(1)}, u32[]{:S(2)}, u32[]{:S(2)}) collective-permute-start(bf16[16,7296]{1,0:T(8,128)(2,1)S(1)} %reshape.40), channel_id=1, source_target_pairs={{0,192},{1,7},{2,194},{3,1},{4,196},{5,3},{6,198},{7,5},{64,0},{65... | collective-permute-start | bytes 700424 | tf_op jit(solution)/shard_map/ppermute | solution.py:23
  27.6 7.3 %collective-permute-start.2 = (bf16[16,7296]{1,0:T(8,128)(2,1)S(1)}, bf16[16,7296]{1,0:T(8,128)(2,1)S(1)}, u32[]{:S(2)}, u32[]{:S(2)}) collective-permute-start(bf16[16,7296]{1,0:T(8,128)(2,1)S(1)} %reshape.40), channel_id=1, source_target_pairs={{0,64},{1,3},{2,66},{3,5},{4,68},{5,7},{6,70},{7,1},{64,128},{65,6... | collective-permute-start | bytes 700424 | tf_op jit(solution)/shard_map/ppermute | solution.py:23
  35.0 8.6 %collective-permute-start.7 = (bf16[32,7296]{1,0:T(8,128)(2,1)S(1)}, bf16[32,7296]{1,0:T(8,128)(2,1)S(1)}, u32[]{:S(2)}, u32[]{:S(2)}) collective-permute-start(bf16[32,7296]{1,0:T(8,128)(2,1)S(1)} %get-tuple-element.42), channel_id=1, source_target_pairs={{0,6},{1,193},{2,0},{3,195},{4,2},{5,197},{6,4},{7,199},{64,70},{6... | collective-permute-start | bytes 1400840 | tf_op jit(solution)/shard_map/ppermute | solution.py:23
  35.5 9.6 %collective-permute-start.6 = (bf16[32,7296]{1,0:T(8,128)(2,1)S(1)}, bf16[32,7296]{1,0:T(8,128)(2,1)S(1)}, u32[]{:S(2)}, u32[]{:S(2)}) collective-permute-start(bf16[32,7296]{1,0:T(8,128)(2,1)S(1)} %get-tuple-element.43), channel_id=1, source_target_pairs={{0,2},{1,65},{2,4},{3,67},{4,6},{5,69},{6,0},{7,71},{64,66},{65,12... | collective-permute-start | bytes 1400840 | tf_op jit(solution)/shard_map/ppermute | solution.py:23
  39.4 12.0 %collective-permute-start.9 = (bf16[32,7296]{1,0:T(8,128)(2,1)S(1)}, bf16[32,7296]{1,0:T(8,128)(2,1)S(1)}, u32[]{:S(2)}, u32[]{:S(2)}) collective-permute-start(bf16[32,7296]{1,0:T(8,128)(2,1)S(1)} %get-tuple-element.42), channel_id=1, source_target_pairs={{0,2},{1,65},{2,4},{3,67},{4,6},{5,69},{6,0},{7,71},{64,66},{65,12... | collective-permute-start | bytes 1400840 | tf_op jit(solution)/shard_map/ppermute | solution.py:23
  41.1 10.4 %collective-permute-start.10 = (bf16[32,7296]{1,0:T(8,128)(2,1)S(1)}, bf16[32,7296]{1,0:T(8,128)(2,1)S(1)}, u32[]{:S(2)}, u32[]{:S(2)}) collective-permute-start(bf16[32,7296]{1,0:T(8,128)(2,1)S(1)} %get-tuple-element.43), channel_id=1, source_target_pairs={{0,6},{1,193},{2,0},{3,195},{4,2},{5,197},{6,4},{7,199},{64,70},{6... | collective-permute-start | bytes 1400840 | tf_op jit(solution)/shard_map/ppermute | solution.py:23
  45.1 10.0 %collective-permute-start.11 = (bf16[32,7296]{1,0:T(8,128)(2,1)S(1)}, bf16[32,7296]{1,0:T(8,128)(2,1)S(1)}, u32[]{:S(2)}, u32[]{:S(2)}) collective-permute-start(bf16[32,7296]{1,0:T(8,128)(2,1)S(1)} %collective-permute-done.6), channel_id=1, source_target_pairs={{0,2},{1,65},{2,4},{3,67},{4,6},{5,69},{6,0},{7,71},{64,66},{65,12... | collective-permute-start | bytes 1400840 | tf_op jit(solution)/shard_map/ppermute | solution.py:23
  45.7 9.5 %collective-permute-start.12 = (bf16[32,7296]{1,0:T(8,128)(2,1)S(1)}, bf16[32,7296]{1,0:T(8,128)(2,1)S(1)}, u32[]{:S(2)}, u32[]{:S(2)}) collective-permute-start(bf16[32,7296]{1,0:T(8,128)(2,1)S(1)} %collective-permute-done.7), channel_id=1, source_target_pairs={{0,6},{1,193},{2,0},{3,195},{4,2},{5,197},{6,4},{7,199},{64,70},{6... | collective-permute-start | bytes 1400840 | tf_op jit(solution)/shard_map/ppermute | solution.py:23
  60.8 9.8 %collective-permute-start.15 = (bf16[32,7168]{1,0:T(8,128)(2,1)S(1)}, bf16[32,7168]{1,0:T(8,128)(2,1)S(1)}, u32[]{:S(2)}, u32[]{:S(2)}) collective-permute-start(bf16[32,7168]{1,0:T(8,128)(2,1)S(1)} %get-tuple-element.72), channel_id=1, source_target_pairs={{0,2},{1,65},{2,4},{3,67},{4,6},{5,69},{6,0},{7,71},{64,66},{65,12... | collective-permute-start | bytes 1376264 | tf_op jit(solution)/shard_map/ppermute | solution.py:23
  63.2 9.7 %collective-permute-start.14 = (bf16[32,7168]{1,0:T(8,128)(2,1)S(1)}, bf16[32,7168]{1,0:T(8,128)(2,1)S(1)}, u32[]{:S(2)}, u32[]{:S(2)}) collective-permute-start(bf16[32,7168]{1,0:T(8,128)(2,1)S(1)} %get-tuple-element.73), channel_id=1, source_target_pairs={{0,6},{1,193},{2,0},{3,195},{4,2},{5,197},{6,4},{7,199},{64,70},{6... | collective-permute-start | bytes 1376264 | tf_op jit(solution)/shard_map/ppermute | solution.py:23
  64.2 11.3 %collective-permute-start.17 = (bf16[32,7168]{1,0:T(8,128)(2,1)S(1)}, bf16[32,7168]{1,0:T(8,128)(2,1)S(1)}, u32[]{:S(2)}, u32[]{:S(2)}) collective-permute-start(bf16[32,7168]{1,0:T(8,128)(2,1)S(1)} %get-tuple-element.70), channel_id=1, source_target_pairs={{0,2},{1,65},{2,4},{3,67},{4,6},{5,69},{6,0},{7,71},{64,66},{65,12... | collective-permute-start | bytes 1376264 | tf_op jit(solution)/shard_map/ppermute | solution.py:23
  66.4 11.4 %collective-permute-start.19 = (bf16[32,7168]{1,0:T(8,128)(2,1)S(1)}, bf16[32,7168]{1,0:T(8,128)(2,1)S(1)}, u32[]{:S(2)}, u32[]{:S(2)}) collective-permute-start(bf16[32,7168]{1,0:T(8,128)(2,1)S(1)} %get-tuple-element.71), channel_id=1, source_target_pairs={{0,6},{1,193},{2,0},{3,195},{4,2},{5,197},{6,4},{7,199},{64,70},{6... | collective-permute-start | bytes 1376264 | tf_op jit(solution)/shard_map/ppermute | solution.py:23
  73.1 9.6 %collective-permute-start.16 = (bf16[32,7168]{1,0:T(8,128)(2,1)S(1)}, bf16[32,7168]{1,0:T(8,128)(2,1)S(1)}, u32[]{:S(2)}, u32[]{:S(2)}) collective-permute-start(bf16[32,7168]{1,0:T(8,128)(2,1)S(1)} %get-tuple-element.53), channel_id=1, source_target_pairs={{0,6},{1,193},{2,0},{3,195},{4,2},{5,197},{6,4},{7,199},{64,70},{6... | collective-permute-start | bytes 1376264 | tf_op jit(solution)/shard_map/ppermute | solution.py:23
  74.1 9.7 %collective-permute-start.20 = (bf16[32,7168]{1,0:T(8,128)(2,1)S(1)}, bf16[32,7168]{1,0:T(8,128)(2,1)S(1)}, u32[]{:S(2)}, u32[]{:S(2)}) collective-permute-start(bf16[32,7168]{1,0:T(8,128)(2,1)S(1)} %get-tuple-element.54), channel_id=1, source_target_pairs={{0,2},{1,65},{2,4},{3,67},{4,6},{5,69},{6,0},{7,71},{64,66},{65,12... | collective-permute-start | bytes 1376264 | tf_op jit(solution)/shard_map/ppermute | solution.py:23
  84.2 7.6 %collective-permute-start.22 = (bf16[16,7168]{1,0:T(8,128)(2,1)S(1)}, bf16[16,7168]{1,0:T(8,128)(2,1)S(1)}, u32[]{:S(2)}, u32[]{:S(2)}) collective-permute-start(bf16[16,7168]{1,0:T(8,128)(2,1)S(1)} %get-tuple-element.77), channel_id=1, source_target_pairs={{0,128},{1,5},{2,130},{3,7},{4,132},{5,1},{6,134},{7,3},{64,192},{... | collective-permute-start | bytes 688136 | tf_op jit(solution)/shard_map/ppermute | solution.py:23
  85.9 7.0 %collective-permute-start.18 = (bf16[16,7168]{1,0:T(8,128)(2,1)S(1)}, bf16[16,7168]{1,0:T(8,128)(2,1)S(1)}, u32[]{:S(2)}, u32[]{:S(2)}) collective-permute-start(bf16[16,7168]{1,0:T(8,128)(2,1)S(1)} %slice.61), channel_id=1, source_target_pairs={{0,192},{1,7},{2,194},{3,1},{4,196},{5,3},{6,198},{7,5},{64,0},{65... | collective-permute-start | bytes 688136 | tf_op jit(solution)/shard_map/ppermute | solution.py:23
  87.1 7.2 %collective-permute-start.21 = (bf16[16,7168]{1,0:T(8,128)(2,1)S(1)}, bf16[16,7168]{1,0:T(8,128)(2,1)S(1)}, u32[]{:S(2)}, u32[]{:S(2)}) collective-permute-start(bf16[16,7168]{1,0:T(8,128)(2,1)S(1)} %get-tuple-element.76), channel_id=1, source_target_pairs={{0,64},{1,3},{2,66},{3,5},{4,68},{5,7},{6,70},{7,1},{64,128},{65,6... | collective-permute-start | bytes 688136 | tf_op jit(solution)/shard_map/ppermute | solution.py:23
  121.9 10.0 %collective-permute-start.26 = (bf16[16,7168]{1,0:T(8,128)(2,1)S(1)}, bf16[16,7168]{1,0:T(8,128)(2,1)S(1)}, u32[]{:S(2)}, u32[]{:S(2)}) collective-permute-start(bf16[16,7168]{1,0:T(8,128)(2,1)S(1)} %reshape.42), channel_id=1, source_target_pairs={{0,128},{1,5},{2,130},{3,7},{4,132},{5,1},{6,134},{7,3},{64,192},{... | collective-permute-start | bytes 688136 | tf_op jit(solution)/shard_map/ppermute | solution.py:23
  123.2 8.8 %collective-permute-start.25 = (bf16[16,7168]{1,0:T(8,128)(2,1)S(1)}, bf16[16,7168]{1,0:T(8,128)(2,1)S(1)}, u32[]{:S(2)}, u32[]{:S(2)}) collective-permute-start(bf16[16,7168]{1,0:T(8,128)(2,1)S(1)} %reshape.42), channel_id=1, source_target_pairs={{0,192},{1,7},{2,194},{3,1},{4,196},{5,3},{6,198},{7,5},{64,0},{65... | collective-permute-start | bytes 688136 | tf_op jit(solution)/shard_map/ppermute | solution.py:23
  124.4 7.5 %collective-permute-start.24 = (bf16[16,7168]{1,0:T(8,128)(2,1)S(1)}, bf16[16,7168]{1,0:T(8,128)(2,1)S(1)}, u32[]{:S(2)}, u32[]{:S(2)}) collective-permute-start(bf16[16,7168]{1,0:T(8,128)(2,1)S(1)} %reshape.42), channel_id=1, source_target_pairs={{0,64},{1,3},{2,66},{3,5},{4,68},{5,7},{6,70},{7,1},{64,128},{65,6... | collective-permute-start | bytes 688136 | tf_op jit(solution)/shard_map/ppermute | solution.py:23
  132.0 9.0 %collective-permute-start.28 = (bf16[32,7168]{1,0:T(8,128)(2,1)S(1)}, bf16[32,7168]{1,0:T(8,128)(2,1)S(1)}, u32[]{:S(2)}, u32[]{:S(2)}) collective-permute-start(bf16[32,7168]{1,0:T(8,128)(2,1)S(1)} %get-tuple-element.60), channel_id=1, source_target_pairs={{0,6},{1,193},{2,0},{3,195},{4,2},{5,197},{6,4},{7,199},{64,70},{6... | collective-permute-start | bytes 1376264 | tf_op jit(solution)/shard_map/ppermute | solution.py:23
  135.0 8.5 %collective-permute-start.27 = (bf16[32,7168]{1,0:T(8,128)(2,1)S(1)}, bf16[32,7168]{1,0:T(8,128)(2,1)S(1)}, u32[]{:S(2)}, u32[]{:S(2)}) collective-permute-start(bf16[32,7168]{1,0:T(8,128)(2,1)S(1)} %get-tuple-element.61), channel_id=1, source_target_pairs={{0,2},{1,65},{2,4},{3,67},{4,6},{5,69},{6,0},{7,71},{64,66},{65,12... | collective-permute-start | bytes 1376264 | tf_op jit(solution)/shard_map/ppermute | solution.py:23
  137.1 11.3 %collective-permute-start.29 = (bf16[32,7168]{1,0:T(8,128)(2,1)S(1)}, bf16[32,7168]{1,0:T(8,128)(2,1)S(1)}, u32[]{:S(2)}, u32[]{:S(2)}) collective-permute-start(bf16[32,7168]{1,0:T(8,128)(2,1)S(1)} %get-tuple-element.60), channel_id=1, source_target_pairs={{0,2},{1,65},{2,4},{3,67},{4,6},{5,69},{6,0},{7,71},{64,66},{65,12... | collective-permute-start | bytes 1376264 | tf_op jit(solution)/shard_map/ppermute | solution.py:23
  137.9 10.5 %collective-permute-start.30 = (bf16[32,7168]{1,0:T(8,128)(2,1)S(1)}, bf16[32,7168]{1,0:T(8,128)(2,1)S(1)}, u32[]{:S(2)}, u32[]{:S(2)}) collective-permute-start(bf16[32,7168]{1,0:T(8,128)(2,1)S(1)} %get-tuple-element.61), channel_id=1, source_target_pairs={{0,6},{1,193},{2,0},{3,195},{4,2},{5,197},{6,4},{7,199},{64,70},{6... | collective-permute-start | bytes 1376264 | tf_op jit(solution)/shard_map/ppermute | solution.py:23
  143.5 9.8 %collective-permute-start.31 = (bf16[32,7168]{1,0:T(8,128)(2,1)S(1)}, bf16[32,7168]{1,0:T(8,128)(2,1)S(1)}, u32[]{:S(2)}, u32[]{:S(2)}) collective-permute-start(bf16[32,7168]{1,0:T(8,128)(2,1)S(1)} %collective-permute-done.27), channel_id=1, source_target_pairs={{0,2},{1,65},{2,4},{3,67},{4,6},{5,69},{6,0},{7,71},{64,66},{65,12... | collective-permute-start | bytes 1376264 | tf_op jit(solution)/shard_map/ppermute | solution.py:23
  143.5 9.9 %collective-permute-start.32 = (bf16[32,7168]{1,0:T(8,128)(2,1)S(1)}, bf16[32,7168]{1,0:T(8,128)(2,1)S(1)}, u32[]{:S(2)}, u32[]{:S(2)}) collective-permute-start(bf16[32,7168]{1,0:T(8,128)(2,1)S(1)} %collective-permute-done.28), channel_id=1, source_target_pairs={{0,6},{1,193},{2,0},{3,195},{4,2},{5,197},{6,4},{7,199},{64,70},{6... | collective-permute-start | bytes 1376264 | tf_op jit(solution)/shard_map/ppermute | solution.py:23
  (9 other events, 172.5 us)
